TPU v7x, 512 devices: a whole 4x8x8 slice. The times are simulated.
512 devices in a mesh: din: 8 (over y), dout: 32 (over x, z), layer: 2 (over core).
Axes of the slice: x: 4, y: 8, z: 8, core: 2. Of those that a mesh axis runs over, the one named last changes fastest.
Arguments:
- acts: bfloat16 [2048, 8192], P(('layer', 'dout'), 'din'), parts along dimension 0, may hold values from -6 to 6
- grad_y: bfloat16 [2048, 8192], P(('layer', 'din'), 'dout'), parts along dimension 0, may hold values from -6 to 6
- w_base: bfloat16 [16384, 8192], P(('layer', 'din'), 'dout'), parts along dimension 0
- a_left: bfloat16 [16384, 64], P(('layer', 'din')), parts along dimension 0, may hold values from -0.0625 to 0.0625
- b_right: bfloat16 [128, 8192], P('layer', 'dout'), parts along dimension 0, may hold values from -0.75 to 0.75
- magnitude: float32 [16384], P(('layer', 'dout')), parts along dimension 0, may hold values from 0.5 to 2
Outputs:
- grad_acts: bfloat16 [2048, 8192], P(('layer', 'dout'), 'din'), parts along dimension 0
- grad_left: float32 [16384, 64], P(('layer', 'din', 'dout')), parts along dimension 0
- grad_right: float32 [128, 8192], P(('layer', 'din'), 'dout'), parts along dimension 0
- grad_mag: float32 [16384], P(('layer', 'dout')), parts along dimension 0
There are 2 independent parts, one for each index of `layer`. A program takes and returns all parts, laid end to end along the dimension named above; each array names one. Nothing has to cross between parts.
All inputs are finite; a program needn't handle non-finite values.
Results may differ from a plain program's by a relative error of at most 0.023.
Values may be sent and summed in bfloat16 or wider, within the bound.
No kernel may reach another device: no remote copies, remote signals or barrier semaphores. Data moves between devices by JAX's collectives and lax.ppermute only.
A program may use at most 64 MiB of HBM per device.

v0:
```python
import jax
import jax.numpy as jnp
from jax import lax
from jax.sharding import PartitionSpec as P


def local(acts, grad_y, w_base, a_left, b_right, magnitude):
    merged = w_base.astype(jnp.float32) + jnp.dot(
        a_left, b_right, preferred_element_type=jnp.float32
    )
    merged_b = merged.astype(jnp.bfloat16)
    square_part = jnp.sum(merged * merged, axis=0)
    squares = lax.psum(square_part, "din")
    grads = lax.all_gather(grad_y, "din", axis=0, tiled=True)
    grads_wide = grads.astype(jnp.float32)
    whole = lax.all_gather(acts, "dout", axis=0, tiled=True)
    products = lax.dot_general(
        whole, grads, (((0,), (0,)), ((), ())), preferred_element_type=jnp.float32
    )
    outputs = jnp.dot(whole, merged_b, preferred_element_type=jnp.float32)
    stat_part = jnp.sum(grads_wide * outputs, axis=0)
    stat = lax.psum(stat_part, "din")
    norms = jnp.sqrt(squares)
    grad_mag = stat / norms
    scale = magnitude / norms
    scaled = (grads_wide * scale[None, :]).astype(jnp.bfloat16)
    summed = lax.psum_scatter(
        lax.dot_general(
            scaled, merged_b, (((1,), (1,)), ((), ())), preferred_element_type=jnp.float32
        ).astype(jnp.bfloat16),
        "dout",
        scatter_dimension=0,
        tiled=True,
    )
    grad_merged = (products * scale[None, :]).astype(jnp.bfloat16)
    left_part = lax.dot_general(
        grad_merged, b_right, (((1,), (1,)), ((), ())), preferred_element_type=jnp.float32
    )
    grad_left = lax.psum_scatter(
        left_part.astype(jnp.bfloat16), "dout", scatter_dimension=0, tiled=True
    ).astype(jnp.float32)
    right_part = lax.dot_general(
        a_left, grad_merged, (((0,), (0,)), ((), ())), preferred_element_type=jnp.float32
    )
    grad_right = lax.psum_scatter(
        right_part.astype(jnp.bfloat16), "din", scatter_dimension=0, tiled=True
    ).astype(jnp.float32)
    return (summed, grad_left, grad_right, grad_mag)


def solution(mesh):
    return jax.shard_map(
        local,
        mesh=mesh,
        in_specs=(
            P(("layer", "dout"), "din"),
            P(("layer", "din"), "dout"),
            P(("layer", "din"), "dout"),
            P(("layer", "din"), None),
            P("layer", "dout"),
            P(("layer", "dout")),
        ),
        out_specs=(
            P(("layer", "dout"), "din"),
            P(("layer", "din", "dout"), None),
            P(("layer", "din"), "dout"),
            P(("layer", "dout")),
        ),
        check_vma=False,
    )
```

profile of v0, /device:TPU:24, one launch (start us, length us, event | category | flops | bytes accessed | tf_op | source)
XLA Modules:
  0.0 611.9 jit_solution(5595193988097792536)
XLA Ops:
  7.2 0.0 copy-start
  7.2 0.0 all-gather.2.cloned.1.call-start
  7.2 0.7 all-gather.2.cloned.1.call-update
  7.9 0.0 reduce-scatter.8.cloned.1.call-start
  8.0 26.3 %all_gather.6 = bf16[1024,256]{1,0:T(8,128)(2,1)S(1)} all-gather(bf16[128,256]{1,0:T(8,128)(2,1)} %param.7), channel_id=1, replica_groups=mesh['din'=8,'dout'=32,'layer'=2] {'din'}, dimensions={0}, use_global_device_ids=true | all-gather | bytes 589824 | tf_op jit(solution)/shard_map/all_gather | solution.py:14
  34.3 1.5 multiply_reduce_fusion
  35.7 63.9 %all-gather.2.cloned.1.call-done = bf16[1024,1024]{1,0:T(8,128)(2,1)} async-done(((bf16[32,1024]{1,0:T(8,128)(2,1)}), bf16[1024,1024]{1,0:T(8,128)(2,1)}) %all-gather.2.cloned.1.call-update) | async-done | bytes 2097168 | tf_op jit(solution)/shard_map/all_gather | solution.py:16
  99.6 2.3 fusion.2
  101.9 15.6 %all-reduce = (f32[256]{0:T(256)S(1)}, f32[256]{0:T(256)S(1)}) all-reduce(f32[256]{0:T(256)S(1)} %get-tuple-element.8, f32[256]{0:T(256)S(1)} %fusion.2), channel_id=1, replica_groups=mesh['din'=8,'dout'=32,'layer'=2] {'din'}, use_global_device_ids=true, to_apply=%region_1.0 | all-reduce | flops 512 | bytes 4096 | tf_op jit(solution)/shard_map/psum | solution.py:13
  117.5 0.6 sqrt_divide_fusion
  118.1 2.4 fusion.1
  120.5 0.8 fusion.3
  121.3 0.0 reduce-scatter.8.cloned.1.call-update
  121.3 0.0 reduce-scatter.6.cloned.1.call-start
  121.4 1.0 convolution_convert_fusion.1
  122.4 0.0 reduce-scatter.6.cloned.1.call-update
  122.4 0.0 reduce-scatter.4.cloned.1.call-start
  122.5 2.1 convolution_convert_fusion
  124.6 0.0 reduce-scatter.4.cloned.1.call-update
  124.6 31.4 %reduce-scatter.8.cloned.1.call-done = bf16[8,256]{1,0:T(8,128)(2,1)} async-done(((bf16[64,256]{1,0:T(8,128)(2,1)}), bf16[8,256]{1,0:T(8,128)(2,1)}) %reduce-scatter.8.cloned.1.call-update) | async-done | bytes 4112 | tf_op jit(solution)/shard_map/reduce_scatter | solution.py:45
  156.0 1.3 convert_element_type.43
  157.3 223.0 %reduce-scatter.6.cloned.1.call-done = bf16[32,64]{1,0:T(8,128)(2,1)} async-done(((bf16[1024,64]{1,0:T(8,128)(2,1)}), bf16[32,64]{1,0:T(8,128)(2,1)}) %reduce-scatter.6.cloned.1.call-update) | async-done | bytes 4112 | tf_op jit(solution)/shard_map/reduce_scatter | solution.py:39
  380.3 1.3 convert_element_type.40
  381.6 223.8 %reduce-scatter.4.cloned.1.call-done = bf16[32,1024]{1,0:T(8,128)(2,1)} async-done(((bf16[1024,1024]{1,0:T(8,128)(2,1)}), bf16[32,1024]{1,0:T(8,128)(2,1)}) %reduce-scatter.4.cloned.1.call-update) | async-done | bytes 65552 | tf_op jit(solution)/shard_map/reduce_scatter | solution.py:27
  (5 shorter events, 0.0 us)
Async XLA Ops:
  7.2 27.1 %copy-start = (bf16[1024,64]{0,1:T(8,128)(2,1)S(1)}, bf16[1024,64]{0,1:T(8,128)(2,1)}, u32[]{:S(2)}) copy-start(bf16[1024,64]{0,1:T(8,128)(2,1)} %param.9) | copy-start | bytes 393220
  7.2 92.4 %all-gather.2.cloned.1.call-start = ((), (), s32[]{:S(2)}) async-start(), calls=%async_computation.4 | async-start | bytes 2162688 | tf_op jit(solution)/shard_map/all_gather | solution.py:16
  7.9 148.1 %reduce-scatter.8.cloned.1.call-start = ((), (), s32[]{:S(2)}) async-start(), calls=%async_computation.6 | async-start | bytes 36864 | tf_op jit(solution)/shard_map/reduce_scatter | solution.py:45
  99.6 18.0 %copy-start.2 = (f32[256]{0:T(256)S(1)}, f32[256]{0:T(256)}, u32[]{:S(2)}) copy-start(f32[256]{0:T(256)} %param.11) | copy-start | bytes 3076
  118.1 3.3 copy-start.1
  121.3 259.0 %reduce-scatter.6.cloned.1.call-start = ((), (), s32[]{:S(2)}) async-start(), calls=%async_computation.5 | async-start | bytes 270336 | tf_op jit(solution)/shard_map/reduce_scatter | solution.py:39
  122.4 483.0 %reduce-scatter.4.cloned.1.call-start = ((), (), s32[]{:S(2)}) async-start(), calls=%async_computation.3 | async-start | bytes 2162688 | tf_op jit(solution)/shard_map/reduce_scatter | solution.py:27
Sparse Core Ops, SparseCore 0:
  11.2 88.3 all-gather.1
  121.5 34.4 reduce-scatter.7
  161.0 219.2 reduce-scatter.5
  385.1 220.2 reduce-scatter.3
where the time goes:
time: 612 us
  waiting for transfers between devices  543 us (89%)
  blocking collectives  41.9 us (7%)
  between operations  13.8 us (2%)
  matrix products  10.1 us (2%)
    reduce_scatter x1, waiting for transfers between devices, local(): lax.psum_scatter(lax.dot_general(scaled, merged_b, (((1,), (1,)), ((), ()...  224 us
    reduce_scatter x1, waiting for transfers between devices, local(): lax.psum_scatter(left_part.astype(jnp.bfloat16), 'dout', scatter_dimensio...  223 us
    all_gather x1, waiting for transfers between devices, local(): whole = lax.all_gather(acts, 'dout', axis=0, tiled=True)  63.9 us
    reduce_scatter x1, waiting for transfers between devices, local(): lax.psum_scatter(right_part.astype(jnp.bfloat16), 'din', scatter_dimensio...  31.4 us
    all_gather x1, blocking collectives, local(): grads = lax.all_gather(grad_y, 'din', axis=0, tiled=True)  26.3 us
    psum x1, blocking collectives, local(): squares = lax.psum(square_part, 'din')  15.6 us
  transfers between devices with their start and end apart: 4, of which 4 were waited for; matrix products, arithmetic and copies ran while one was open for 1% of the time, Pallas kernels for 0%

commit v1 on v0

v1 whole, which is shorter than its diff:
```python
import jax
import jax.numpy as jnp
from jax import lax
from jax.sharding import Mesh, PartitionSpec as P

F32 = jnp.float32
BF16 = jnp.bfloat16


def spread(block, axis, count):
    return lax.all_to_all(
        jnp.broadcast_to(block[None], (count, *block.shape)), axis, 0, 0, tiled=True
    )


def local(acts, grad_y, w_base, a_left, b_right, magnitude):
    nx, ny, nz = 4, 8, 8
    rows, din = acts.shape
    width = grad_y.shape[1]
    rank = a_left.shape[1]
    tokens = rows * nz
    grads = spread(grad_y, "din", ny).reshape(-1, width)
    merged = w_base.astype(F32) + jnp.dot(a_left, b_right, preferred_element_type=F32)
    merged_b = merged.astype(BF16)
    square_part = jnp.sum(merged * merged, axis=0)
    squares = jnp.sum(spread(square_part[None], "din", ny), axis=(0, 1))
    wide = lax.all_gather(merged_b, "x")
    whole = spread(acts, "z", nz).reshape(tokens, din)
    scale = magnitude / jnp.sqrt(squares)
    scaled = (grads.astype(F32) * scale[None, :]).astype(BF16)
    low = lax.dot_general(
        scaled, b_right, (((1,), (1,)), ((), ())), preferred_element_type=F32
    ).astype(BF16)
    mine = lax.all_to_all(scaled.reshape(nx, tokens, width), "x", 0, 0, tiled=True)
    low_mine = lax.all_to_all(low.reshape(nx, tokens, rank), "x", 0, 0, tiled=True)
    part = sum(
        lax.dot_general(
            mine[k], wide[k], (((1,), (1,)), ((), ())), preferred_element_type=F32
        )
        for k in range(nx)
    ).astype(BF16)
    summed = jnp.sum(
        lax.all_to_all(part.reshape(nz, rows, din), "z", 0, 0, tiled=True).astype(F32),
        axis=0,
    ).astype(BF16)
    low_sum = jnp.sum(low_mine.astype(F32), axis=0).astype(BF16)
    left_part = lax.dot_general(
        whole, low_sum, (((0,), (0,)), ((), ())), preferred_element_type=F32
    ).astype(BF16)
    grad_left = jnp.sum(
        lax.all_to_all(
            left_part.reshape(nx * nz, -1, rank), ("x", "z"), 0, 0, tiled=True
        ).astype(F32),
        axis=0,
    )
    down = jnp.dot(whole, a_left, preferred_element_type=F32).astype(BF16)
    pieces = []
    for k in range(nx):
        outputs = jnp.dot(whole, wide[k], preferred_element_type=F32)
        stat = jnp.sum(mine[k].astype(F32) * outputs, axis=0)
        high = stat.astype(BF16)
        rest = (stat - high.astype(F32)).astype(BF16)
        right = lax.dot_general(
            down, mine[k], (((0,), (0,)), ((), ())), preferred_element_type=F32
        ).astype(BF16)
        tail = jnp.broadcast_to(jnp.stack([high, rest])[None], (ny, 2, width))
        pieces.append(
            jnp.concatenate([right.reshape(ny, rank // ny, width), tail], axis=1)
        )
    packed = jnp.stack(pieces, axis=1).reshape(ny * nx, rank // ny + 2, width)
    got = jnp.sum(
        lax.all_to_all(packed, ("din", "x"), 0, 0, tiled=True).astype(F32), axis=0
    )
    grad_right = got[: rank // ny]
    grad_mag = (got[rank // ny] + got[rank // ny + 1]) / magnitude
    return (summed, grad_left, grad_right, grad_mag)


def solution(mesh):
    fine = Mesh(mesh.devices.reshape(8, 4, 8, 2), ("din", "x", "z", "layer"))
    return jax.shard_map(
        local,
        mesh=fine,
        in_specs=(
            P(("layer", "x", "z"), "din"),
            P(("layer", "din"), ("x", "z")),
            P(("layer", "din"), ("x", "z")),
            P(("layer", "din"), None),
            P("layer", ("x", "z")),
            P(("layer", "x", "z")),
        ),
        out_specs=(
            P(("layer", "x", "z"), "din"),
            P(("layer", "din", "x", "z"), None),
            P(("layer", "din"), ("x", "z")),
            P(("layer", "x", "z")),
        ),
        check_vma=False,
    )
```

time: 612 us -> 148 us (0.24)
  the two profiles are of different devices: /device:TPU:24 before, /device:TPU:8 now
where the time goes in v1:
time: 148 us; the launch traced here: 147 us
  waiting for transfers between devices  47.5 us (32%)
  blocking collectives  32.4 us (22%)
  starting transfers between devices  32.3 us (22%)
  between operations  14.4 us (10%)
  matrix products  11.2 us (8%)
  local copies, waits for them, and re-layouts  5.98 us (4%)
  other arithmetic  3.28 us (2%)
    all_to_all x2, blocking collectives, spread(): lax.all_to_all(jnp.broadcast_to(block[None], (count, *block.shape)), axis...  32.4 us
    all_to_all x1, waiting for transfers between devices, spread(): lax.all_to_all(jnp.broadcast_to(block[None], (count, *block.shape)), axis...  13.2 us
    all_to_all x1, waiting for transfers between devices, local(): lax.all_to_all(part.reshape(nz, rows, din), 'z', 0, 0, tiled=True)  11.1 us
    all_to_all x1, starting transfers between devices, spread(): lax.all_to_all(jnp.broadcast_to(block[None], (count, *block.shape)), axis...  10.3 us
    all_to_all x1, waiting for transfers between devices, local(): lax.all_to_all(packed, ('din', 'x'), 0, 0, tiled=True).astype(F32)  7.22 us
    all_to_all x1, waiting for transfers between devices, local(): lax.all_to_all(scaled.reshape(nx, tokens, width), 'x', 0, 0, tiled=True)  6.49 us
    all_to_all x1, starting transfers between devices, local(): lax.all_to_all(packed, ('din', 'x'), 0, 0, tiled=True).astype(F32)  6.14 us
    all_to_all x1, waiting for transfers between devices, local(): lax.all_to_all(low.reshape(nx, tokens, rank), 'x', 0, 0, tiled=True)  5.08 us
  transfers between devices with their start and end apart: 7, of which 6 were waited for; matrix products, arithmetic and copies ran while one was open for 11% of the time, Pallas kernels for 0%

profile of v1, /device:TPU:8, one launch (start us, length us, event | category | flops | bytes accessed | tf_op | source)
XLA Modules:
  0.0 147.0 jit_solution(7776766148928300996)
XLA Ops:
  7.2 0.8 copy-done
  8.1 2.2 %multiply_reduce_fusion = (f32[256]{0:T(256)S(1)}, bf16[1024,256]{1,0:T(8,128)(2,1)}) fusion(bf16[1024,64]{0,1:T(8,128)(2,1)S(1)} %copy-done, bf16[64,256]{1,0:T(8,128)(2,1)} %param.10, bf16[1024,256]{1,0:T(8,128)(2,1)} %param.8), kind=kOutput, calls=%fused_computation.33 | convolution fusion | flops 34864896 | bytes 1213440 | tf_op jit(solution)/shard_map/dot_general | solution.py:23
  10.3 14.5 %all_to_all.40 = f32[8,1,256]{2,1,0:T(1,128)S(1)} all-to-all(f32[8,1,256]{2,1,0:T(1,128)S(1)} %broadcast_in_dim.15), channel_id=1, replica_groups=mesh['din'=8,'x'=4,'z'=8,'layer'=2] {'din'}, dimensions={0} | all-to-all | bytes 16384 | tf_op jit(solution)/shard_map/all_to_all | solution.py:11
  24.8 0.9 broadcast_in_dim.14
  25.7 17.9 %all_to_all.41 = bf16[8,128,256]{2,1,0:T(8,128)(2,1)S(1)} all-to-all(bf16[8,128,256]{2,1,0:T(8,128)(2,1)S(1)} %broadcast_in_dim.14), channel_id=1, replica_groups=mesh['din'=8,'x'=4,'z'=8,'layer'=2] {'din'}, dimensions={0} | all-to-all | bytes 1048576 | tf_op jit(solution)/shard_map/all_to_all | solution.py:11
  43.6 0.9 broadcast_in_dim.16
  44.5 10.3 %all-to-all-start.5 = ((bf16[8,32,1024]{2,1,0:T(8,128)(2,1)}), bf16[8,32,1024]{2,1,0:T(8,128)(2,1)S(1)}, u32[]{:S(2)}, u32[]{:S(2)}) async-start(bf16[8,32,1024]{2,1,0:T(8,128)(2,1)} %broadcast_in_dim.16), calls=%async_computation.5 | async-start | bytes 1048576 | tf_op jit(solution)/shard_map/all_to_all | solution.py:11
  56.0 13.2 %all-to-all-done.5 = bf16[8,32,1024]{2,1,0:T(8,128)(2,1)S(1)} async-done(((bf16[8,32,1024]{2,1,0:T(8,128)(2,1)}), bf16[8,32,1024]{2,1,0:T(8,128)(2,1)S(1)}, u32[]{:S(2)}, u32[]{:S(2)}) %all-to-all-start.5) | async-done | bytes 524320 | tf_op jit(solution)/shard_map/all_to_all | solution.py:11
  69.1 4.3 %all-to-all-start.4 = ((bf16[4,256,64]{1,2,0:T(8,128)(2,1)}), bf16[4,256,64]{1,2,0:T(8,128)(2,1)S(1)}, u32[]{:S(2)}, u32[]{:S(2)}) async-start(bf16[4,256,64]{1,2,0:T(8,128)(2,1)} %bitcast.102), calls=%async_computation.4 | async-start | bytes 262144 | tf_op jit(solution)/shard_map/all_to_all | solution.py:35
  73.4 0.9 fusion.15
  74.3 5.1 %all-to-all-done.4 = bf16[4,256,64]{1,2,0:T(8,128)(2,1)S(1)} async-done(((bf16[4,256,64]{1,2,0:T(8,128)(2,1)}), bf16[4,256,64]{1,2,0:T(8,128)(2,1)S(1)}, u32[]{:S(2)}, u32[]{:S(2)}) %all-to-all-start.4) | async-done | bytes 131104 | tf_op jit(solution)/shard_map/all_to_all | solution.py:35
  79.4 3.5 %all-to-all-start.2 = ((bf16[4,256,256]{2,1,0:T(8,128)(2,1)}), bf16[4,256,256]{2,1,0:T(8,128)(2,1)S(1)}, u32[]{:S(2)}, u32[]{:S(2)}) async-start(bf16[4,256,256]{2,1,0:T(8,128)(2,1)} %fusion.15), calls=%async_computation.2 | async-start | bytes 1048576 | tf_op jit(solution)/shard_map/all_to_all | solution.py:34
  83.6 0.8 reshape.158
  84.4 6.5 %all-to-all-done.2 = bf16[4,256,256]{2,1,0:T(8,128)(2,1)S(1)} async-done(((bf16[4,256,256]{2,1,0:T(8,128)(2,1)}), bf16[4,256,256]{2,1,0:T(8,128)(2,1)S(1)}, u32[]{:S(2)}, u32[]{:S(2)}) %all-to-all-start.2) | async-done | bytes 524320 | tf_op jit(solution)/shard_map/all_to_all | solution.py:34
  90.9 3.9 %all-to-all-start.6 = ((bf16[32,2,1024]{2,1,0:T(2,128)(2,1)}), bf16[32,2,1024]{2,1,0:T(2,128)(2,1)S(1)}, u32[]{:S(2)}, u32[]{:S(2)}) async-start(bf16[32,2,1024]{2,1,0:T(2,128)(2,1)} %reshape.158), calls=%async_computation.6 | async-start | bytes 262144 | tf_op jit(solution)/shard_map/all_to_all | solution.py:51
  95.5 1.5 %fusion.5 = f32[256]{0:T(256)S(1)} fusion(bf16[256,1024]{1,0:T(8,128)(2,1)S(1)} %bitcast.106, bf16[4096,256]{1,0:T(8,128)(2,1)} %all-gather.3.cloned.1.call-done, bf16[4,256,256]{2,1,0:T(8,128)(2,1)S(1)} %all-to-all-done.2), kind=kOutput, calls=%fused_computation.15 | convolution fusion | flops 134414080 | bytes 1180672 | tf_op jit(solution)/shard_map/dot_general | solution.py:59
  97.0 1.4 fusion.6
  100.7 4.4 %all-to-all-done.6 = bf16[32,2,1024]{2,1,0:T(2,128)(2,1)S(1)} async-done(((bf16[32,2,1024]{2,1,0:T(2,128)(2,1)}), bf16[32,2,1024]{2,1,0:T(2,128)(2,1)S(1)}, u32[]{:S(2)}, u32[]{:S(2)}) %all-to-all-start.6) | async-done | bytes 131104 | tf_op jit(solution)/shard_map/all_to_all | solution.py:51
  105.1 6.1 %all-to-all-start.7 = ((bf16[32,10,256]{2,1,0:T(8,128)(2,1)}), bf16[32,10,256]{2,1,0:T(8,128)(2,1)S(1)}, u32[]{:S(2)}, u32[]{:S(2)}) async-start(bf16[32,10,256]{2,1,0:T(8,128)(2,1)} %bitcast.26), calls=%async_computation.7 | async-start | bytes 524288 | tf_op jit(solution)/shard_map/all_to_all | solution.py:72
  111.2 1.4 convolution_add_fusion.1
  112.6 2.2 %fusion = bf16[256,1024]{1,0:T(8,128)(2,1)} fusion(f32[256,1024]{1,0:T(8,128)S(1)} %convolution_add_fusion.1, bf16[4096,256]{1,0:T(8,128)(2,1)} %all-gather.3.cloned.1.call-done, bf16[4,256,256]{2,1,0:T(8,128)(2,1)S(1)} %all-to-all-done.2), kind=kOutput, calls=%fused_computation.4 | convolution fusion | flops 134742016 | bytes 2228224 | tf_op jit(solution)/shard_map/dot_general | solution.py:37
  114.8 7.2 %all-to-all-done.7 = bf16[32,10,256]{2,1,0:T(8,128)(2,1)S(1)} async-done(((bf16[32,10,256]{2,1,0:T(8,128)(2,1)}), bf16[32,10,256]{2,1,0:T(8,128)(2,1)S(1)}, u32[]{:S(2)}, u32[]{:S(2)}) %all-to-all-start.7) | async-done | bytes 163872 | tf_op jit(solution)/shard_map/all_to_all | solution.py:72
  122.0 4.2 %all-to-all-start.3 = ((bf16[8,32,1024]{2,1,0:T(8,128)(2,1)}), bf16[8,32,1024]{2,1,0:T(8,128)(2,1)S(1)}, u32[]{:S(2)}, u32[]{:S(2)}) async-start(bf16[8,32,1024]{2,1,0:T(8,128)(2,1)} %bitcast.5), calls=%async_computation.3 | async-start | bytes 1048576 | tf_op jit(solution)/shard_map/all_to_all | solution.py:43
  128.3 11.1 %all-to-all-done.3 = bf16[8,32,1024]{2,1,0:T(8,128)(2,1)S(1)} async-done(((bf16[8,32,1024]{2,1,0:T(8,128)(2,1)}), bf16[8,32,1024]{2,1,0:T(8,128)(2,1)S(1)}, u32[]{:S(2)}, u32[]{:S(2)}) %all-to-all-start.3) | async-done | bytes 524320 | tf_op jit(solution)/shard_map/all_to_all | solution.py:43
  (62 shorter events, 7.6 us)
Async XLA Ops:
  7.2 0.9 copy-start
  7.2 36.4 %copy-start.2 = (bf16[32,1024]{1,0:T(8,128)(2,1)S(1)}, bf16[32,1024]{1,0:T(8,128)(2,1)}, u32[]{:S(2)}) copy-start(bf16[32,1024]{1,0:T(8,128)(2,1)} %param.6) | copy-start | bytes 196612
  7.2 88.3 %all-gather.3.cloned.1.call-start = ((), (), s32[]{:S(2)}) async-start(), calls=%async_computation.8 | async-start | bytes 2621440 | tf_op jit(solution)/shard_map/all_gather | solution.py:27
  10.3 44.5 %copy-start.4 = (f32[256]{0:T(256)S(1)}, f32[256]{0:T(256)}, u32[]{:S(2)}) copy-start(f32[256]{0:T(256)} %param.11) | copy-start | bytes 3076
  24.8 30.1 %copy-start.3 = (bf16[64,256]{1,0:T(8,128)(2,1)S(1)}, bf16[64,256]{1,0:T(8,128)(2,1)}, u32[]{:S(2)}) copy-start(bf16[64,256]{1,0:T(8,128)(2,1)} %param.10) | copy-start | bytes 98308
  44.5 24.7 %all-to-all-start.5 = ((bf16[8,32,1024]{2,1,0:T(8,128)(2,1)}), bf16[8,32,1024]{2,1,0:T(8,128)(2,1)S(1)}, u32[]{:S(2)}, u32[]{:S(2)}) async-start(bf16[8,32,1024]{2,1,0:T(8,128)(2,1)} %broadcast_in_dim.16), calls=%async_computation.5 | async-start | bytes 1048576 | tf_op jit(solution)/shard_map/all_to_all | solution.py:11
  69.1 10.3 %all-to-all-start.4 = ((bf16[4,256,64]{1,2,0:T(8,128)(2,1)}), bf16[4,256,64]{1,2,0:T(8,128)(2,1)S(1)}, u32[]{:S(2)}, u32[]{:S(2)}) async-start(bf16[4,256,64]{1,2,0:T(8,128)(2,1)} %bitcast.102), calls=%async_computation.4 | async-start | bytes 262144 | tf_op jit(solution)/shard_map/all_to_all | solution.py:35
  79.4 11.5 %all-to-all-start.2 = ((bf16[4,256,256]{2,1,0:T(8,128)(2,1)}), bf16[4,256,256]{2,1,0:T(8,128)(2,1)S(1)}, u32[]{:S(2)}, u32[]{:S(2)}) async-start(bf16[4,256,256]{2,1,0:T(8,128)(2,1)} %fusion.15), calls=%async_computation.2 | async-start | bytes 1048576 | tf_op jit(solution)/shard_map/all_to_all | solution.py:34
  90.9 14.2 %all-to-all-start.6 = ((bf16[32,2,1024]{2,1,0:T(2,128)(2,1)}), bf16[32,2,1024]{2,1,0:T(2,128)(2,1)S(1)}, u32[]{:S(2)}, u32[]{:S(2)}) async-start(bf16[32,2,1024]{2,1,0:T(2,128)(2,1)} %reshape.158), calls=%async_computation.6 | async-start | bytes 262144 | tf_op jit(solution)/shard_map/all_to_all | solution.py:51
  95.5 2.9 %copy-start.1 = (bf16[4096,256]{1,0:T(8,128)(2,1)S(1)}, bf16[4096,256]{1,0:T(8,128)(2,1)}, u32[]{:S(2)}) copy-start(bf16[4096,256]{1,0:T(8,128)(2,1)} %all-gather.3.cloned.1.call-done) | copy-start | bytes 6291460
  105.1 16.9 %all-to-all-start.7 = ((bf16[32,10,256]{2,1,0:T(8,128)(2,1)}), bf16[32,10,256]{2,1,0:T(8,128)(2,1)S(1)}, u32[]{:S(2)}, u32[]{:S(2)}) async-start(bf16[32,10,256]{2,1,0:T(8,128)(2,1)} %bitcast.26), calls=%async_computation.7 | async-start | bytes 524288 | tf_op jit(solution)/shard_map/all_to_all | solution.py:72
  122.0 17.5 %all-to-all-start.3 = ((bf16[8,32,1024]{2,1,0:T(8,128)(2,1)}), bf16[8,32,1024]{2,1,0:T(8,128)(2,1)S(1)}, u32[]{:S(2)}, u32[]{:S(2)}) async-start(bf16[8,32,1024]{2,1,0:T(8,128)(2,1)} %bitcast.5), calls=%async_computation.3 | async-start | bytes 1048576 | tf_op jit(solution)/shard_map/all_to_all | solution.py:43
Sparse Core Ops, SparseCore 0:
  10.4 40.7 all-gather.2

commit v2 on v1

v2 whole, which is shorter than its diff:
```python
import jax
import jax.numpy as jnp
from jax import lax
from jax.experimental import pallas as pl
from jax.experimental.pallas import tpu as pltpu
from jax.sharding import Mesh, PartitionSpec as P

F32 = jnp.float32
BF16 = jnp.bfloat16
NX, NY, NZ = 4, 8, 8
NT = (((1,), (1,)), ((), ()))
TN = (((0,), (0,)), ((), ()))
VMEM = pl.BlockSpec(memory_space=pltpu.VMEM)
SMEM = pl.BlockSpec(memory_space=pltpu.SMEM)
LIMIT = 48 * 1024 * 1024
HOPS = (0, 1, 3, 2)


def dot(a, b, dims):
    return lax.dot_general(a, b, dims, preferred_element_type=F32)


def call(body, outs, flops, *args):
    moved = sum(a.size * a.dtype.itemsize for a in args)
    moved += sum(o.size * o.dtype.itemsize for o in outs)
    return pl.pallas_call(
        body,
        out_shape=outs,
        in_specs=[SMEM if a.dtype == jnp.int32 else VMEM for a in args],
        out_specs=[VMEM] * len(outs),
        compiler_params=pltpu.CompilerParams(vmem_limit_bytes=LIMIT),
        cost_estimate=pl.CostEstimate(
            flops=flops, bytes_accessed=moved, transcendentals=0
        ),
    )(*args)


def shape(dims, dtype=BF16):
    return jax.ShapeDtypeStruct(dims, dtype)


def two_rows(value, width):
    high = value.astype(BF16).astype(F32)
    row = lax.broadcasted_iota(jnp.int32, (16, width), 0)
    return jnp.where(row == 0, high, jnp.where(row == 1, value - high, 0.0)).astype(BF16)


def merge_body(w_ref, at_ref, b_ref, g_ref, wide_ref, pay_ref):
    din, width = w_ref.shape
    rank = b_ref.shape[0]
    tokens = g_ref.shape[0]
    total = jnp.zeros((1, width), F32)
    step = 256
    for i in range(0, din, step):
        merged = w_ref[pl.ds(i, step), :].astype(F32) + dot(
            at_ref[:, pl.ds(i, step)], b_ref[...], TN
        )
        total += jnp.sum(merged * merged, axis=0, keepdims=True)
        wide_ref[pl.ds(i, step), :] = merged.astype(BF16)
    wide_ref[pl.ds(din, rank), :] = b_ref[...]
    tail = two_rows(total, width)
    for y in range(NY):
        pay_ref[y, pl.ds(0, tokens), :] = g_ref[...]
        pay_ref[y, pl.ds(tokens, 16), :] = tail


def scale_body(x_ref, got_ref, mag_ref, *outs):
    tokens = got_ref.shape[1] - 16
    width = got_ref.shape[2]
    squares = jnp.zeros((16, width), F32)
    for y in range(NY):
        squares += got_ref[y, pl.ds(tokens, 16), :].astype(F32)
    squares = jnp.sum(squares, axis=0, keepdims=True)
    scale = mag_ref[...] / jnp.sqrt(squares)
    half = NY // NX
    for hop, out in zip(HOPS, outs):
        block = lax.rem(x_ref[0] + hop, NX)
        for h in range(half):
            out[pl.ds(h * tokens, tokens), :] = (
                got_ref[block * half + h, pl.ds(0, tokens), :].astype(F32) * scale
            ).astype(BF16)


def source(x_ref, k):
    return lax.rem(x_ref[0] + NX - HOPS[k], NX)


def acts_body(x_ref, s0, s1, s2, s3, wide_ref, whole_ref, out_ref):
    blocks = (s0, s1, s2, s3)
    tokens, din = whole_ref.shape
    rank = wide_ref.shape[1] - din
    step = 256
    for i in range(0, din, step):
        total = sum(
            dot(s[...], wide_ref[source(x_ref, k), pl.ds(i, step), :], NT)
            for k, s in enumerate(blocks)
        )
        out_ref[:, pl.ds(i, step)] = total.astype(BF16)
    low = jnp.zeros((tokens, NX * rank), F32)
    for k, s in enumerate(blocks):
        b = wide_ref[source(x_ref, k), pl.ds(din, rank), :]
        low += dot(s[...], jnp.concatenate([b] * NX, axis=0), NT)
    low = low.astype(BF16)
    lane = lax.broadcasted_iota(jnp.int32, low.shape, 1)
    left = jnp.zeros((din // NX, NX * rank), F32)
    for q in range(NX):
        here = (lane >= q * rank) & (lane < (q + 1) * rank)
        left += dot(
            whole_ref[:, pl.ds(q * (din // NX), din // NX)],
            jnp.where(here, low, jnp.zeros_like(low)),
            TN,
        )
    out_ref[:, pl.ds(din, NX * rank)] = left.astype(BF16)


def stat_body(x_ref, s0, s1, s2, s3, wide_ref, whole_ref, at_ref, *outs):
    din = whole_ref.shape[1]
    rank = at_ref.shape[0]
    down = dot(whole_ref[...], at_ref[...], NT).astype(BF16)
    for k, (s, out) in enumerate(zip((s0, s1, s2, s3), outs)):
        outputs = lax.dot_general(
            whole_ref[...],
            wide_ref[source(x_ref, k), pl.ds(0, din), :],
            (((1,), (0,)), ((), ())),
            preferred_element_type=F32,
        )
        stat = jnp.sum(s[...].astype(F32) * outputs, axis=0, keepdims=True)
        out[pl.ds(0, rank), :] = dot(down, s[...], TN).astype(BF16)
        out[pl.ds(rank, 16), :] = two_rows(stat, stat.shape[1])


def meet_body(r0, r1, r2, r3, pay_ref):
    rows, width = r0.shape
    total = sum(r[...].astype(F32) for r in (r0, r1, r2, r3))
    stat = jnp.sum(total[rows - 16 :], axis=0, keepdims=True)
    tail = two_rows(stat, width)
    each = (rows - 16) // NY
    for y in range(NY):
        pay_ref[y, :, :] = jnp.concatenate(
            [
                total[y * each : (y + 1) * each],
                tail.astype(F32)[:8],
            ],
            axis=0,
        ).astype(BF16)


def sum_body(got_ref, acts_ref, left_ref):
    din = acts_ref.shape[1]
    total = sum(got_ref[z].astype(F32) for z in range(NZ))
    acts_ref[...] = total[:, :din].astype(BF16)
    left_ref[...] = total[:, din:].astype(BF16)


def shift(block, hop):
    return lax.ppermute(block, "x", [(i, (i + hop) % NX) for i in range(NX)])


def local(acts, grad_y, w_base, a_left, b_right, magnitude):
    rows, din = acts.shape
    width = grad_y.shape[1]
    rank = a_left.shape[1]
    tokens = rows * NZ
    spot = lax.axis_index("x").astype(jnp.int32).reshape(1)
    a_turned = a_left.T
    packed, pay = call(
        merge_body,
        [shape((din + rank, width)), shape((NY, grad_y.shape[0] + 16, width))],
        2 * din * width * rank,
        w_base, a_turned, b_right, grad_y,
    )
    wide = lax.all_gather(packed, "x")
    got = lax.all_to_all(pay, "din", 0, 0, tiled=True)
    scaled = call(
        scale_body,
        [shape((tokens, width))] * NX,
        4 * tokens * width * NX,
        spot, got, magnitude.reshape(1, width),
    )
    blocks = [scaled[0]] + [shift(scaled[k], HOPS[k]) for k in range(1, NX)]
    whole = lax.all_to_all(
        jnp.broadcast_to(acts[None], (NZ, rows, din)), "z", 0, 0, tiled=True
    ).reshape(tokens, din)
    (part,) = call(
        acts_body,
        [shape((tokens, din + NX * rank))],
        2 * tokens * din * width * NX,
        spot, *blocks, wide, whole,
    )
    back = lax.all_to_all(
        part.reshape(NZ, rows, din + NX * rank), "z", 0, 0, tiled=True
    )
    sides = call(
        stat_body,
        [shape((rank + 16, width))] * NX,
        2 * tokens * din * width * NX,
        spot, *blocks, wide, whole, a_turned,
    )
    met = [sides[0]] + [shift(sides[k], NX - HOPS[k]) for k in range(1, NX)]
    (pay,) = call(meet_body, [shape((NY, 16, width))], 0, *met)
    summed, left = call(
        sum_body, [shape((rows, din)), shape((rows, NX * rank))], 0, back
    )
    right = jnp.sum(
        lax.all_to_all(pay, "din", 0, 0, tiled=True).astype(F32), axis=0
    )
    lefts = left.astype(F32)
    for hop in (1, 3, 2):
        lefts += shift(left, hop).astype(F32)
    grad_left = lax.dynamic_slice_in_dim(lefts, spot[0] * rank, rank, 1)
    each = rank // NY
    grad_mag = (right[each] + right[each + 1]) / magnitude
    return (summed, grad_left, right[:each], grad_mag)


def solution(mesh):
    fine = Mesh(mesh.devices.reshape(NY, NX, NZ, 2), ("din", "x", "z", "layer"))
    return jax.shard_map(
        local,
        mesh=fine,
        in_specs=(
            P(("layer", "x", "z"), "din"),
            P(("layer", "din"), ("x", "z")),
            P(("layer", "din"), ("x", "z")),
            P(("layer", "din"), None),
            P("layer", ("x", "z")),
            P(("layer", "x", "z")),
        ),
        out_specs=(
            P(("layer", "x", "z"), "din"),
            P(("layer", "din", "x", "z"), None),
            P(("layer", "din"), ("x", "z")),
            P(("layer", "x", "z")),
        ),
        check_vma=False,
    )
```

time: 148 us -> 137 us (0.926)
  starting transfers between devices: 32.3 us -> 53 us
  waiting for transfers between devices: 47.5 us -> 30.5 us
  matrix products: 11.2 us -> 0 us
  blocking collectives: 32.4 us -> 24.8 us
  Pallas kernels: 0 us -> 5.91 us
  other arithmetic: 3.28 us -> 1.27 us
    ppermute x0 -> x9, starting transfers between devices: none -> 30.7 us  [shift(): return lax.ppermute(block, 'x', [(i, (i + hop) % NX) for i in range(NX)])]
    all_to_all x6 -> x3, waiting for transfers between devices: 47.5 us -> 23.4 us  [the longest x1 14.9 us: local(): lax.all_to_all(part.reshape(NZ, rows, din + NX * rank), 'z', 0, 0, tiled=...]
    dot_general x16 -> x0, matrix products: 11.2 us -> none  [the longest x4 4.21 us: local(): lax.dot_general(mine[k], wide[k], (((1,), (1,)), ((), ())), preferred_ele...]
    all_to_all x6 -> x3, starting transfers between devices: 32.3 us -> 22.2 us  [the longest x1 10.3 us: local(): lax.all_to_all(jnp.broadcast_to(acts[None], (NZ, rows, din)), 'z', 0, 0,...]
    all_to_all x2 -> x1, blocking collectives: 32.4 us -> 24.8 us  [local(): got = lax.all_to_all(pay, 'din', 0, 0, tiled=True)]
    ppermute x0 -> x9, waiting for transfers between devices: none -> 7.18 us  [shift(): return lax.ppermute(block, 'x', [(i, (i + hop) % NX) for i in range(NX)])]
    pallas_call x0 -> x6, Pallas kernels: none -> 5.91 us  [call(): pl.pallas_call(body, out_shape=outs, in_specs=[SMEM if a.dtype == jnp.int...]
    unnamed x12 -> x18, local copies, waits for them, and re-layouts: 1.93 us -> 5.18 us
  transfers between devices with their start and end apart: 7 -> 13, of which waited for: 6 -> 7; matrix products, arithmetic and copies ran while one was open for 11% -> 1% of each run, Pallas kernels for 0% -> 2%
where the time goes in v2:
time: 137 us; the launch traced here: 136 us
  starting transfers between devices  53 us (39%)
  waiting for transfers between devices  30.5 us (22%)
  blocking collectives  24.8 us (18%)
  between operations  14.2 us (10%)
  local copies, waits for them, and re-layouts  6.63 us (5%)
  Pallas kernels  5.91 us (4%)
    ppermute x9, starting transfers between devices, shift(): return lax.ppermute(block, 'x', [(i, (i + hop) % NX) for i in range(NX)])  30.7 us
    all_to_all x1, blocking collectives, local(): got = lax.all_to_all(pay, 'din', 0, 0, tiled=True)  24.8 us
    all_to_all x1, waiting for transfers between devices, local(): lax.all_to_all(part.reshape(NZ, rows, din + NX * rank), 'z', 0, 0, tiled=...  14.9 us
    all_to_all x1, starting transfers between devices, local(): lax.all_to_all(jnp.broadcast_to(acts[None], (NZ, rows, din)), 'z', 0, 0,...  10.3 us
    ppermute x9, waiting for transfers between devices, shift(): return lax.ppermute(block, 'x', [(i, (i + hop) % NX) for i in range(NX)])  7.18 us
    all_to_all x1, starting transfers between devices, local(): lax.all_to_all(part.reshape(NZ, rows, din + NX * rank), 'z', 0, 0, tiled=...  6.22 us
    pallas_call x6, Pallas kernels, call(): pl.pallas_call(body, out_shape=outs, in_specs=[SMEM if a.dtype == jnp.int...  5.91 us
    all_to_all x1, starting transfers between devices, local(): lax.all_to_all(pay, 'din', 0, 0, tiled=True).astype(F32)  5.7 us
  transfers between devices with their start and end apart: 13, of which 7 were waited for; matrix products, arithmetic and copies ran while one was open for 1% of the time, Pallas kernels for 2%

profile of v2, /device:TPU:8, one launch (start us, length us, event | category | flops | bytes accessed | tf_op | source)
XLA Modules:
  0.0 136.3 jit_solution(14467681309830392298)
XLA Ops:
  7.2 1.0 copy-done.2
  10.8 1.2 shard_map.93
  12.0 24.8 %all_to_all.20.got_ref = bf16[8,144,256]{2,1,0:T(8,128)(2,1)S(1)} all-to-all(bf16[8,144,256]{2,1,0:T(8,128)(2,1)S(1)} %get-tuple-element.16), channel_id=1, replica_groups=mesh['din'=8,'x'=4,'z'=8,'layer'=2] {'din'}, dimensions={0} | all-to-all | bytes 1179648 | tf_op jit(solution)/shard_map/all_to_all | solution.py:173
  37.6 10.3 %all-to-all-start.1 = ((bf16[8,32,1024]{2,1,0:T(8,128)(2,1)}), bf16[8,32,1024]{2,1,0:T(8,128)(2,1)S(1)}, u32[]{:S(2)}, u32[]{:S(2)}) async-start(bf16[8,32,1024]{2,1,0:T(8,128)(2,1)} %broadcast_in_dim.2), calls=%async_computation.1 | async-start | bytes 1048576 | tf_op jit(solution)/shard_map/all_to_all | solution.py:181
  48.1 3.4 %collective-permute-start = (bf16[256,256]{1,0:T(8,128)(2,1)S(1)}, bf16[256,256]{1,0:T(8,128)(2,1)S(1)}, u32[]{:S(2)}, u32[]{:S(2)}) collective-permute-start(bf16[256,256]{1,0:T(8,128)(2,1)S(1)} %get-tuple-element.18), channel_id=1, source_target_pairs={{0,16},{16,32},{32,48},{48,0},{1,17},{17,33},{33,49},{49,1},{2,18}... | collective-permute-start | bytes 393224 | tf_op jit(solution)/shard_map/ppermute | solution.py:156
  51.5 3.7 %collective-permute-start.1 = (bf16[256,256]{1,0:T(8,128)(2,1)S(1)}, bf16[256,256]{1,0:T(8,128)(2,1)S(1)}, u32[]{:S(2)}, u32[]{:S(2)}) collective-permute-start(bf16[256,256]{1,0:T(8,128)(2,1)S(1)} %get-tuple-element.19), channel_id=1, source_target_pairs={{0,48},{16,0},{32,16},{48,32},{1,49},{17,1},{33,17},{49,33},{2,50}... | collective-permute-start | bytes 393224 | tf_op jit(solution)/shard_map/ppermute | solution.py:156
  55.1 3.7 %collective-permute-start.2 = (bf16[256,256]{1,0:T(8,128)(2,1)S(1)}, bf16[256,256]{1,0:T(8,128)(2,1)S(1)}, u32[]{:S(2)}, u32[]{:S(2)}) collective-permute-start(bf16[256,256]{1,0:T(8,128)(2,1)S(1)} %get-tuple-element.20), channel_id=1, source_target_pairs={{0,32},{16,48},{32,0},{48,16},{1,33},{17,49},{33,1},{49,17},{2,34}... | collective-permute-start | bytes 393224 | tf_op jit(solution)/shard_map/ppermute | solution.py:156
  58.9 3.7 %all-to-all-done.1 = bf16[8,32,1024]{2,1,0:T(8,128)(2,1)S(1)} async-done(((bf16[8,32,1024]{2,1,0:T(8,128)(2,1)}), bf16[8,32,1024]{2,1,0:T(8,128)(2,1)S(1)}, u32[]{:S(2)}, u32[]{:S(2)}) %all-to-all-start.1) | async-done | bytes 524320 | tf_op jit(solution)/shard_map/all_to_all | solution.py:181
  63.5 1.6 %copy-done = bf16[4352,256]{1,0:T(8,128)(2,1)S(1)} copy-done((bf16[4352,256]{1,0:T(8,128)(2,1)S(1)}, bf16[4352,256]{1,0:T(8,128)(2,1)}, u32[]{:S(2)}) %copy-start) | copy-done | bytes 2228248
  65.2 1.0 shard_map.97
  66.2 3.8 %collective-permute-start.6 = (bf16[80,256]{1,0:T(8,128)(2,1)S(1)}, bf16[80,256]{1,0:T(8,128)(2,1)S(1)}, u32[]{:S(2)}, u32[]{:S(2)}) collective-permute-start(bf16[80,256]{1,0:T(8,128)(2,1)S(1)} %get-tuple-element.25), channel_id=1, source_target_pairs={{0,48},{16,0},{32,16},{48,32},{1,49},{17,1},{33,17},{49,33},{2,50}... | collective-permute-start | bytes 122888 | tf_op jit(solution)/shard_map/ppermute | solution.py:156
  70.0 2.1 %collective-permute-start.7 = (bf16[80,256]{1,0:T(8,128)(2,1)S(1)}, bf16[80,256]{1,0:T(8,128)(2,1)S(1)}, u32[]{:S(2)}, u32[]{:S(2)}) collective-permute-start(bf16[80,256]{1,0:T(8,128)(2,1)S(1)} %get-tuple-element.26), channel_id=1, source_target_pairs={{0,16},{16,32},{32,48},{48,0},{1,17},{17,33},{33,49},{49,1},{2,18}... | collective-permute-start | bytes 122888 | tf_op jit(solution)/shard_map/ppermute | solution.py:156
  72.0 4.0 %collective-permute-start.8 = (bf16[80,256]{1,0:T(8,128)(2,1)S(1)}, bf16[80,256]{1,0:T(8,128)(2,1)S(1)}, u32[]{:S(2)}, u32[]{:S(2)}) collective-permute-start(bf16[80,256]{1,0:T(8,128)(2,1)S(1)} %get-tuple-element.27), channel_id=1, source_target_pairs={{0,32},{16,48},{32,0},{48,16},{1,33},{17,49},{33,1},{49,17},{2,34}... | collective-permute-start | bytes 122888 | tf_op jit(solution)/shard_map/ppermute | solution.py:156
  76.1 1.0 collective-permute-done.7.r2
  77.1 2.4 %collective-permute-done.8.r3 = bf16[80,256]{1,0:T(8,128)(2,1)S(1)} collective-permute-done((bf16[80,256]{1,0:T(8,128)(2,1)S(1)}, bf16[80,256]{1,0:T(8,128)(2,1)S(1)}, u32[]{:S(2)}, u32[]{:S(2)}) %collective-permute-start.8) | collective-permute-done | bytes 40992 | tf_op jit(solution)/shard_map/ppermute | solution.py:156
  80.1 5.7 %all-to-all-start.3 = ((bf16[8,16,256]{2,1,0:T(8,128)(2,1)}), bf16[8,16,256]{2,1,0:T(8,128)(2,1)S(1)}, u32[]{:S(2)}, u32[]{:S(2)}) async-start(bf16[8,16,256]{2,1,0:T(8,128)(2,1)} %shard_map.98), calls=%async_computation.3 | async-start | bytes 131072 | tf_op jit(solution)/shard_map/all_to_all | solution.py:205
  85.8 2.2 %shard_map.95 = bf16[256,1280]{1,0:T(8,128)(2,1)} custom-call(s32[1]{0:T(128)} %bitcast.x_ref, bf16[256,256]{1,0:T(8,128)(2,1)S(1)} %get-tuple-element.17.s0, bf16[256,256]{1,0:T(8,128)(2,1)S(1)} %collective-permute-done.s1, bf16[256,256]{1,0:T(8,128)(2,1)S(1)} %collective-permute-done.1.s2, bf16[256,256]{1,0:T(8,128)(2,1)S(1)} %collective-permute-done.2.s3, ...), custom_call_target="tpu_custom_call" | custom-call | flops 536870912 | bytes 3932164 | tf_op jit(solution)/shard_map/pallas_call | solution.py:26
  88.0 4.7 %all-to-all-done.3 = bf16[8,16,256]{2,1,0:T(8,128)(2,1)S(1)} async-done(((bf16[8,16,256]{2,1,0:T(8,128)(2,1)}), bf16[8,16,256]{2,1,0:T(8,128)(2,1)S(1)}, u32[]{:S(2)}, u32[]{:S(2)}) %all-to-all-start.3) | async-done | bytes 65568 | tf_op jit(solution)/shard_map/all_to_all | solution.py:205
  92.7 6.2 %all-to-all-start.2 = ((bf16[8,32,1280]{2,1,0:T(8,128)(2,1)}), bf16[8,32,1280]{2,1,0:T(8,128)(2,1)S(1)}, u32[]{:S(2)}, u32[]{:S(2)}) async-start(bf16[8,32,1280]{2,1,0:T(8,128)(2,1)} %bitcast.5), calls=%async_computation.2 | async-start | bytes 1310720 | tf_op jit(solution)/shard_map/all_to_all | solution.py:190
  99.0 14.9 %all-to-all-done.2.got_ref = bf16[8,32,1280]{2,1,0:T(8,128)(2,1)S(1)} async-done(((bf16[8,32,1280]{2,1,0:T(8,128)(2,1)}), bf16[8,32,1280]{2,1,0:T(8,128)(2,1)S(1)}, u32[]{:S(2)}, u32[]{:S(2)}) %all-to-all-start.2) | async-done | bytes 655392 | tf_op jit(solution)/shard_map/all_to_all | solution.py:190
  114.6 3.1 %collective-permute-start.3 = (bf16[32,256]{1,0:T(8,128)(2,1)S(1)}, bf16[32,256]{1,0:T(8,128)(2,1)S(1)}, u32[]{:S(2)}, u32[]{:S(2)}) collective-permute-start(bf16[32,256]{1,0:T(8,128)(2,1)S(1)} %get-tuple-element.23), channel_id=1, source_target_pairs={{0,16},{16,32},{32,48},{48,0},{1,17},{17,33},{33,49},{49,1},{2,18}... | collective-permute-start | bytes 49160 | tf_op jit(solution)/shard_map/ppermute | solution.py:156
  117.8 3.9 %collective-permute-start.4 = (bf16[32,256]{1,0:T(8,128)(2,1)S(1)}, bf16[32,256]{1,0:T(8,128)(2,1)S(1)}, u32[]{:S(2)}, u32[]{:S(2)}) collective-permute-start(bf16[32,256]{1,0:T(8,128)(2,1)S(1)} %get-tuple-element.23), channel_id=1, source_target_pairs={{0,48},{16,0},{32,16},{48,32},{1,49},{17,1},{33,17},{49,33},{2,50}... | collective-permute-start | bytes 49160 | tf_op jit(solution)/shard_map/ppermute | solution.py:156
  121.7 3.0 %collective-permute-start.5 = (bf16[32,256]{1,0:T(8,128)(2,1)S(1)}, bf16[32,256]{1,0:T(8,128)(2,1)S(1)}, u32[]{:S(2)}, u32[]{:S(2)}) collective-permute-start(bf16[32,256]{1,0:T(8,128)(2,1)S(1)} %get-tuple-element.23), channel_id=1, source_target_pairs={{0,32},{16,48},{32,0},{48,16},{1,33},{17,49},{33,1},{49,17},{2,34}... | collective-permute-start | bytes 49160 | tf_op jit(solution)/shard_map/ppermute | solution.py:156
  125.9 2.9 %collective-permute-done.5 = bf16[32,256]{1,0:T(8,128)(2,1)S(1)} collective-permute-done((bf16[32,256]{1,0:T(8,128)(2,1)S(1)}, bf16[32,256]{1,0:T(8,128)(2,1)S(1)}, u32[]{:S(2)}, u32[]{:S(2)}) %collective-permute-start.5) | collective-permute-done | bytes 16416 | tf_op jit(solution)/shard_map/ppermute | solution.py:156
  (34 shorter events, 7.7 us)
Async XLA Ops:
  7.2 40.8 %copy-start.7 = (f32[256]{0:T(256)S(1)}, f32[256]{0:T(256)}, u32[]{:S(2)}) copy-start(f32[256]{0:T(256)} %param.11) | copy-start | bytes 3076
  7.2 56.3 %all-gather.3.cloned.1.call-start = ((), (), s32[]{:S(2)}) async-start(), calls=%async_computation.4 | async-start | bytes 2785280 | tf_op jit(solution)/shard_map/all_gather | solution.py:172
  7.2 1.0 copy-start.2
  8.3 0.9 copy-start.3
  9.2 0.8 copy-start.5
  10.0 0.8 copy-start.6
  10.8 26.0 %copy-start.8 = (bf16[32,1024]{1,0:T(8,128)(2,1)S(1)}, bf16[32,1024]{1,0:T(8,128)(2,1)}, u32[]{:S(2)}) copy-start(bf16[32,1024]{1,0:T(8,128)(2,1)} %param.6) | copy-start | bytes 196612
  10.8 52.7 %copy-start.4 = (bf16[1024,64]{0,1:T(8,128)(2,1)S(1)}, bf16[1024,64]{0,1:T(8,128)(2,1)}, u32[]{:S(2)}) copy-start(bf16[1024,64]{0,1:T(8,128)(2,1)} %param.9) | copy-start | bytes 393220
  37.6 24.9 %all-to-all-start.1 = ((bf16[8,32,1024]{2,1,0:T(8,128)(2,1)}), bf16[8,32,1024]{2,1,0:T(8,128)(2,1)S(1)}, u32[]{:S(2)}, u32[]{:S(2)}) async-start(bf16[8,32,1024]{2,1,0:T(8,128)(2,1)} %broadcast_in_dim.2), calls=%async_computation.1 | async-start | bytes 1048576 | tf_op jit(solution)/shard_map/all_to_all | solution.py:181
  48.1 14.5 %collective-permute-start = (bf16[256,256]{1,0:T(8,128)(2,1)S(1)}, bf16[256,256]{1,0:T(8,128)(2,1)S(1)}, u32[]{:S(2)}, u32[]{:S(2)}) collective-permute-start(bf16[256,256]{1,0:T(8,128)(2,1)S(1)} %get-tuple-element.18), channel_id=1, source_target_pairs={{0,16},{16,32},{32,48},{48,0},{1,17},{17,33},{33,49},{49,1},{2,18}... | collective-permute-start | bytes 393224 | tf_op jit(solution)/shard_map/ppermute | solution.py:156
  51.5 11.1 %collective-permute-start.1 = (bf16[256,256]{1,0:T(8,128)(2,1)S(1)}, bf16[256,256]{1,0:T(8,128)(2,1)S(1)}, u32[]{:S(2)}, u32[]{:S(2)}) collective-permute-start(bf16[256,256]{1,0:T(8,128)(2,1)S(1)} %get-tuple-element.19), channel_id=1, source_target_pairs={{0,48},{16,0},{32,16},{48,32},{1,49},{17,1},{33,17},{49,33},{2,50}... | collective-permute-start | bytes 393224 | tf_op jit(solution)/shard_map/ppermute | solution.py:156
  55.1 8.4 %collective-permute-start.2 = (bf16[256,256]{1,0:T(8,128)(2,1)S(1)}, bf16[256,256]{1,0:T(8,128)(2,1)S(1)}, u32[]{:S(2)}, u32[]{:S(2)}) collective-permute-start(bf16[256,256]{1,0:T(8,128)(2,1)S(1)} %get-tuple-element.20), channel_id=1, source_target_pairs={{0,32},{16,48},{32,0},{48,16},{1,33},{17,49},{33,1},{49,17},{2,34}... | collective-permute-start | bytes 393224 | tf_op jit(solution)/shard_map/ppermute | solution.py:156
  63.5 1.6 %copy-start = (bf16[4352,256]{1,0:T(8,128)(2,1)S(1)}, bf16[4352,256]{1,0:T(8,128)(2,1)}, u32[]{:S(2)}) copy-start(bf16[4352,256]{1,0:T(8,128)(2,1)} %all-gather.3.cloned.1.call-done) | copy-start | bytes 6684676
  65.1 20.6 %copy-start.1 = (bf16[4352,256]{1,0:T(8,128)(2,1)S(1)}, bf16[4352,256]{1,0:T(8,128)(2,1)}, u32[]{:S(2)}) copy-start(bf16[4352,256]{1,0:T(8,128)(2,1)} %all-gather.3.cloned.1.call-done) | copy-start | bytes 6684676
  66.2 9.9 %collective-permute-start.6 = (bf16[80,256]{1,0:T(8,128)(2,1)S(1)}, bf16[80,256]{1,0:T(8,128)(2,1)S(1)}, u32[]{:S(2)}, u32[]{:S(2)}) collective-permute-start(bf16[80,256]{1,0:T(8,128)(2,1)S(1)} %get-tuple-element.25), channel_id=1, source_target_pairs={{0,48},{16,0},{32,16},{48,32},{1,49},{17,1},{33,17},{49,33},{2,50}... | collective-permute-start | bytes 122888 | tf_op jit(solution)/shard_map/ppermute | solution.py:156
  70.0 7.1 %collective-permute-start.7 = (bf16[80,256]{1,0:T(8,128)(2,1)S(1)}, bf16[80,256]{1,0:T(8,128)(2,1)S(1)}, u32[]{:S(2)}, u32[]{:S(2)}) collective-permute-start(bf16[80,256]{1,0:T(8,128)(2,1)S(1)} %get-tuple-element.26), channel_id=1, source_target_pairs={{0,16},{16,32},{32,48},{48,0},{1,17},{17,33},{33,49},{49,1},{2,18}... | collective-permute-start | bytes 122888 | tf_op jit(solution)/shard_map/ppermute | solution.py:156
  72.0 7.4 %collective-permute-start.8 = (bf16[80,256]{1,0:T(8,128)(2,1)S(1)}, bf16[80,256]{1,0:T(8,128)(2,1)S(1)}, u32[]{:S(2)}, u32[]{:S(2)}) collective-permute-start(bf16[80,256]{1,0:T(8,128)(2,1)S(1)} %get-tuple-element.27), channel_id=1, source_target_pairs={{0,32},{16,48},{32,0},{48,16},{1,33},{17,49},{33,1},{49,17},{2,34}... | collective-permute-start | bytes 122888 | tf_op jit(solution)/shard_map/ppermute | solution.py:156
  80.1 12.6 %all-to-all-start.3 = ((bf16[8,16,256]{2,1,0:T(8,128)(2,1)}), bf16[8,16,256]{2,1,0:T(8,128)(2,1)S(1)}, u32[]{:S(2)}, u32[]{:S(2)}) async-start(bf16[8,16,256]{2,1,0:T(8,128)(2,1)} %shard_map.98), calls=%async_computation.3 | async-start | bytes 131072 | tf_op jit(solution)/shard_map/all_to_all | solution.py:205
  92.7 21.2 %all-to-all-start.2 = ((bf16[8,32,1280]{2,1,0:T(8,128)(2,1)}), bf16[8,32,1280]{2,1,0:T(8,128)(2,1)S(1)}, u32[]{:S(2)}, u32[]{:S(2)}) async-start(bf16[8,32,1280]{2,1,0:T(8,128)(2,1)} %bitcast.5), calls=%async_computation.2 | async-start | bytes 1310720 | tf_op jit(solution)/shard_map/all_to_all | solution.py:190
  114.6 11.3 %collective-permute-start.3 = (bf16[32,256]{1,0:T(8,128)(2,1)S(1)}, bf16[32,256]{1,0:T(8,128)(2,1)S(1)}, u32[]{:S(2)}, u32[]{:S(2)}) collective-permute-start(bf16[32,256]{1,0:T(8,128)(2,1)S(1)} %get-tuple-element.23), channel_id=1, source_target_pairs={{0,16},{16,32},{32,48},{48,0},{1,17},{17,33},{33,49},{49,1},{2,18}... | collective-permute-start | bytes 49160 | tf_op jit(solution)/shard_map/ppermute | solution.py:156
  117.8 8.1 %collective-permute-start.4 = (bf16[32,256]{1,0:T(8,128)(2,1)S(1)}, bf16[32,256]{1,0:T(8,128)(2,1)S(1)}, u32[]{:S(2)}, u32[]{:S(2)}) collective-permute-start(bf16[32,256]{1,0:T(8,128)(2,1)S(1)} %get-tuple-element.23), channel_id=1, source_target_pairs={{0,48},{16,0},{32,16},{48,32},{1,49},{17,1},{33,17},{49,33},{2,50}... | collective-permute-start | bytes 49160 | tf_op jit(solution)/shard_map/ppermute | solution.py:156
  121.7 7.1 %collective-permute-start.5 = (bf16[32,256]{1,0:T(8,128)(2,1)S(1)}, bf16[32,256]{1,0:T(8,128)(2,1)S(1)}, u32[]{:S(2)}, u32[]{:S(2)}) collective-permute-start(bf16[32,256]{1,0:T(8,128)(2,1)S(1)} %get-tuple-element.23), channel_id=1, source_target_pairs={{0,32},{16,48},{32,0},{48,16},{1,33},{17,49},{33,1},{49,17},{2,34}... | collective-permute-start | bytes 49160 | tf_op jit(solution)/shard_map/ppermute | solution.py:156
Sparse Core Ops, SparseCore 0:
  12.1 43.4 all-gather.2

commit v3 on v2

v3 whole, which is shorter than its diff:
```python
import jax
import jax.numpy as jnp
from jax import lax
from jax.experimental import pallas as pl
from jax.experimental.pallas import tpu as pltpu
from jax.sharding import Mesh, PartitionSpec as P

F32 = jnp.float32
BF16 = jnp.bfloat16
NX, NY, NZ = 4, 8, 8
NT = (((1,), (1,)), ((), ()))
TN = (((0,), (0,)), ((), ()))
NN = (((1,), (0,)), ((), ()))
VMEM = pl.BlockSpec(memory_space=pltpu.VMEM)
SMEM = pl.BlockSpec(memory_space=pltpu.SMEM)
HBM = pl.BlockSpec(memory_space=pltpu.HBM)
MIB = 1024 * 1024
STEP = 256
HOPS = (0, 1, 3, 2)


def dot(a, b, dims):
    return lax.dot_general(a, b, dims, preferred_element_type=F32)


def shape(dims, dtype=BF16):
    return jax.ShapeDtypeStruct(dims, dtype)


def call(body, outs, flops, *args, far=(), scratch=(), out_specs=None, limit=16):
    moved = sum(a.size * a.dtype.itemsize for a in args)
    moved += sum(o.size * o.dtype.itemsize for o in outs)
    specs = [
        HBM if i in far else SMEM if a.dtype == jnp.int32 else VMEM
        for i, a in enumerate(args)
    ]
    return pl.pallas_call(
        body,
        out_shape=outs,
        in_specs=specs,
        out_specs=out_specs or [VMEM] * len(outs),
        scratch_shapes=scratch,
        compiler_params=pltpu.CompilerParams(vmem_limit_bytes=limit * MIB),
        cost_estimate=pl.CostEstimate(
            flops=flops, bytes_accessed=moved, transcendentals=0
        ),
    )(*args)


def fetch(pairs, sems):
    copies = [
        pltpu.make_async_copy(src, dst, sems.at[i]) for i, (src, dst) in enumerate(pairs)
    ]
    for copy in copies:
        copy.start()
    return copies


def two_rows(value, width):
    high = value.astype(BF16).astype(F32)
    row = lax.broadcasted_iota(jnp.int32, (16, width), 0)
    return jnp.where(row == 0, high, jnp.where(row == 1, value - high, 0.0)).astype(BF16)


def merge_body(w_hbm, at_hbm, b_hbm, g_hbm, pay_ref, w_ref, at_ref, b_ref, g_ref, sems):
    copies = fetch(
        ((w_hbm, w_ref), (at_hbm, at_ref), (b_hbm, b_ref), (g_hbm, g_ref)), sems
    )
    for copy in copies:
        copy.wait()
    din, width = w_ref.shape
    tokens = g_ref.shape[0]
    total = jnp.zeros((1, width), F32)
    for i in range(0, din, STEP):
        merged = w_ref[pl.ds(i, STEP), :].astype(F32) + dot(
            at_ref[:, pl.ds(i, STEP)], b_ref[...], TN
        )
        total += jnp.sum(merged * merged, axis=0, keepdims=True)
    tail = two_rows(total, width)
    for y in range(NY):
        pay_ref[y, pl.ds(0, tokens), :] = g_ref[...]
        pay_ref[y, pl.ds(tokens, 16), :] = tail


def scale_body(x_ref, got_ref, mag_ref, b_ref, *outs):
    tokens = got_ref.shape[1] - 16
    width = got_ref.shape[2]
    squares = jnp.zeros((16, width), F32)
    for y in range(NY):
        squares += got_ref[y, pl.ds(tokens, 16), :].astype(F32)
    squares = jnp.sum(squares, axis=0, keepdims=True)
    scale = mag_ref[...] / jnp.sqrt(squares)
    half = NY // NX
    for hop, out in zip(HOPS, outs):
        block = lax.rem(x_ref[0] + hop, NX)
        for h in range(half):
            out[pl.ds(h * tokens, tokens), :] = (
                got_ref[block * half + h, pl.ds(0, tokens), :].astype(F32) * scale
            ).astype(BF16)
        out[pl.ds(half * tokens, b_ref.shape[0]), :] = b_ref[...]


def source(x_ref, k):
    return lax.rem(x_ref[0] + NX - HOPS[k], NX)


def acts_body(
    x_ref, s0, s1, s2, s3, wide_hbm, at, whole, out_hbm, wide, out, lefts, sems, out_sems
):
    blocks = (s0, s1, s2, s3)
    tokens, din = whole.shape
    rank = at.shape[0]
    steps = din // STEP
    copies = fetch(
        [
            (
                wide_hbm.at[source(x_ref, k), pl.ds(i * STEP, STEP)],
                wide.at[k, pl.ds(i * STEP, STEP)],
            )
            for i in range(steps)
            for k in range(NX)
        ],
        sems,
    )
    low = jnp.zeros((tokens, NX * rank), F32)
    for s in blocks:
        b = s[pl.ds(tokens, rank), :]
        low += dot(s[pl.ds(0, tokens), :], jnp.concatenate([b] * NX, axis=0), NT)
    low = low.astype(BF16)
    sends = []

    def send(start, count):
        sends.append(
            pltpu.make_async_copy(
                out.at[:, pl.ds(start, count)],
                out_hbm.at[:, pl.ds(start, count)],
                out_sems.at[len(sends)],
            )
        )
        sends[-1].start()

    group = lax.div(lax.broadcasted_iota(jnp.int32, (8, NX * rank), 1), rank)
    each = din // NX
    rows = each // NZ
    for q in range(NX):
        left = dot(whole[:, pl.ds(q * each, each)], low, TN)
        for z in range(NZ):
            piece = jnp.zeros((8, NX * rank), F32)
            for g in range(rows // 8):
                first = z * rows + g * 8
                piece += jnp.where(group == g, left[first : first + 8], 0.0)
            lefts[pl.ds(z * rows + q * 8, 8), :] = piece
    out[:, pl.ds(din, NX * rank)] = lefts[...].astype(BF16)
    send(din, NX * rank)
    for i in range(steps):
        total = dot(low[:, :rank], at[:, pl.ds(i * STEP, STEP)], NN)
        for k, s in enumerate(blocks):
            copies[i * NX + k].wait()
            total += dot(s[pl.ds(0, tokens), :], wide[k, pl.ds(i * STEP, STEP), :], NT)
        out[:, pl.ds(i * STEP, STEP)] = total.astype(BF16)
        send(i * STEP, STEP)
    for copy in sends:
        copy.wait()


def stat_body(x_ref, s0, s1, s2, s3, wide_hbm, at, whole, *rest):
    outs, (wide, sems) = rest[:NX], rest[NX:]
    copies = fetch(
        [(wide_hbm.at[source(x_ref, k)], wide.at[k]) for k in range(NX)], sems
    )
    rank = at.shape[0]
    tokens = whole.shape[0]
    down = dot(whole[...], at[...], NT).astype(BF16)
    for k, (s, out) in enumerate(zip((s0, s1, s2, s3), outs)):
        scaled = s[pl.ds(0, tokens), :]
        out[pl.ds(0, rank), :] = dot(down, scaled, TN).astype(BF16)
        copies[k].wait()
        outputs = dot(whole[...], wide[k], NN) + dot(down, s[pl.ds(tokens, rank), :], NN)
        stat = jnp.sum(scaled.astype(F32) * outputs, axis=0, keepdims=True)
        out[pl.ds(rank, 16), :] = two_rows(stat, stat.shape[1])


def meet_body(r0, r1, r2, r3, pay_ref):
    rows, width = r0.shape
    total = sum(r[...].astype(F32) for r in (r0, r1, r2, r3))
    stat = jnp.sum(total[rows - 16 :], axis=0, keepdims=True)
    tail = two_rows(stat, width).astype(F32)[:8]
    each = (rows - 16) // NY
    for y in range(NY):
        pay_ref[y, :, :] = jnp.concatenate(
            [total[y * each : (y + 1) * each], tail], axis=0
        ).astype(BF16)


def sum_body(x_ref, got_ref, acts_ref, keep_ref, send_ref, lefts):
    din = acts_ref.shape[1]
    total = sum(got_ref[z].astype(F32) for z in range(NZ))
    acts_ref[...] = total[:, :din].astype(BF16)
    lefts[...] = total[:, din:]

    def block(mask):
        x = jnp.bitwise_xor(x_ref[0], mask)
        return lefts[pl.ds(pl.multiple_of(x * 8, 8), 8), :]

    keep_ref[...] = jnp.concatenate([block(0), block(3)], axis=0)
    send_ref[...] = jnp.concatenate([block(1), block(2)], axis=0).astype(BF16)


def pair_body(keep_ref, got_ref, own_ref, send_ref):
    total = keep_ref[...] + got_ref[...].astype(F32)
    own_ref[...] = total[:8]
    send_ref[...] = jnp.concatenate([total[8:], total[8:]], axis=0).astype(BF16)


def last_body(own_ref, more_ref, got_ref, mag_ref, left_ref, right_ref, mag_out):
    total = sum(got_ref[y].astype(F32) for y in range(NY))
    right_ref[...] = total[:8]
    mag_out[...] = (total[8:9] + total[9:10]) / mag_ref[...]
    left = own_ref[...] + more_ref[...].astype(F32)[:8]
    rank = left_ref.shape[1]
    for g in range(left_ref.shape[0] // 8):
        left_ref[pl.ds(g * 8, 8), :] = left[:, g * rank : (g + 1) * rank]


def shift(block, hop):
    return lax.ppermute(block, "x", [(i, (i + hop) % NX) for i in range(NX)])


def swap(block, mask):
    return lax.ppermute(block, "x", [(i, i ^ mask) for i in range(NX)])


def after(value, *others):
    return lax.optimization_barrier((value, *others))[0]


def local(acts, grad_y, w_base, a_left, b_right, magnitude):
    rows, din = acts.shape
    width = grad_y.shape[1]
    rank = a_left.shape[1]
    tokens = rows * NZ
    wider = din + NX * rank
    spot = lax.axis_index("x").astype(jnp.int32).reshape(1)
    mags = magnitude.reshape(1, width)
    a_turned = a_left.T
    wide = lax.all_gather(w_base, "x")
    parts = (w_base, a_turned, b_right, grad_y)
    (pay,) = call(
        merge_body,
        [shape((NY, grad_y.shape[0] + 16, width))],
        2 * din * width * rank,
        *parts,
        far=(0, 1, 2, 3),
        scratch=[pltpu.VMEM(p.shape, p.dtype) for p in parts]
        + [pltpu.SemaphoreType.DMA((4,))],
        limit=60,
    )
    got = lax.all_to_all(pay, "din", 0, 0, tiled=True)
    scaled = call(
        scale_body,
        [shape((tokens + rank, width))] * NX,
        4 * tokens * width * NX,
        spot, got, mags, b_right,
    )
    blocks = [scaled[0]] + [shift(scaled[k], HOPS[k]) for k in range(1, NX)]
    whole = lax.all_to_all(
        after(jnp.broadcast_to(acts[None], (NZ, rows, din)), got), "z", 0, 0, tiled=True
    ).reshape(tokens, din)
    room = pltpu.VMEM((NX, din, width), BF16)
    (part,) = call(
        acts_body,
        [shape((tokens, wider))],
        2 * tokens * din * width * NX,
        spot, *blocks, wide, a_turned, whole,
        far=(5,),
        out_specs=[HBM],
        scratch=[
            room,
            pltpu.VMEM((tokens, wider), BF16),
            pltpu.VMEM((tokens, NX * rank), F32),
            pltpu.SemaphoreType.DMA((NX * (din // STEP),)),
            pltpu.SemaphoreType.DMA((1 + din // STEP,)),
        ],
        limit=58,
    )
    back = lax.all_to_all(part.reshape(NZ, rows, wider), "z", 0, 0, tiled=True)
    sides = call(
        stat_body,
        [shape((rank + 16, width))] * NX,
        2 * tokens * din * width * NX,
        after(spot, part), *blocks, wide, a_turned, whole,
        far=(5,),
        scratch=[room, pltpu.SemaphoreType.DMA((NX,))],
        limit=58,
    )
    met = [sides[0]] + [shift(sides[k], NX - HOPS[k]) for k in range(1, NX)]
    (pay,) = call(meet_body, [shape((NY, 16, width))], 0, *met)
    back, pay = lax.optimization_barrier((back, pay))
    right = lax.all_to_all(pay, "din", 0, 0, tiled=True)
    summed, keep, send = call(
        sum_body,
        [shape((rows, din)), shape((16, width), F32), shape((16, width))],
        0,
        spot, back,
        scratch=[pltpu.VMEM((rows, NX * rank), F32)],
    )
    own, send = call(
        pair_body, [shape((8, width), F32), shape((16, width))], 0, keep, swap(send, 1)
    )
    grad_left, grad_right, grad_mag = call(
        last_body,
        [shape((rows, rank), F32), shape((rank // NY, width), F32), shape((1, width), F32)],
        0,
        own, swap(send, 3), right, mags,
    )
    return (summed, grad_left, grad_right, grad_mag.reshape(width))


def solution(mesh):
    fine = Mesh(mesh.devices.reshape(NY, NX, NZ, 2), ("din", "x", "z", "layer"))
    return jax.shard_map(
        local,
        mesh=fine,
        in_specs=(
            P(("layer", "x", "z"), "din"),
            P(("layer", "din"), ("x", "z")),
            P(("layer", "din"), ("x", "z")),
            P(("layer", "din"), None),
            P("layer", ("x", "z")),
            P(("layer", "x", "z")),
        ),
        out_specs=(
            P(("layer", "x", "z"), "din"),
            P(("layer", "din", "x", "z"), None),
            P(("layer", "din"), ("x", "z")),
            P(("layer", "x", "z")),
        ),
        check_vma=False,
    )
```

time: 137 us -> 123 us (0.90)
  the two profiles are of different devices: /device:TPU:8 before, /device:TPU:14 now
where the time goes in v3:
time: 123 us; the launch traced here: 122 us
  starting transfers between devices  44.9 us (37%)
  blocking collectives  25 us (20%)
  waiting for transfers between devices  19.5 us (16%)
  Pallas kernels  15.6 us (13%)
  between operations  14.2 us (12%)
  local copies, waits for them, and re-layouts  3.13 us (3%)
    all_to_all x1, blocking collectives, local(): got = lax.all_to_all(pay, 'din', 0, 0, tiled=True)  25 us
    ppermute x6, starting transfers between devices, shift(): return lax.ppermute(block, 'x', [(i, (i + hop) % NX) for i in range(NX)])  18.3 us
    pallas_call x8, Pallas kernels, call(): pl.pallas_call(body, out_shape=outs, in_specs=specs, out_specs=out_specs...  15.6 us
    ppermute x6, waiting for transfers between devices, shift(): return lax.ppermute(block, 'x', [(i, (i + hop) % NX) for i in range(NX)])  10.9 us
    all_to_all x1, starting transfers between devices, local(): lax.all_to_all(after(jnp.broadcast_to(acts[None], (NZ, rows, din)), got),...  10.3 us
    ppermute x2, waiting for transfers between devices, swap(): return lax.ppermute(block, 'x', [(i, i ^ mask) for i in range(NX)])  7.98 us
    all_to_all x1, starting transfers between devices, local(): back = lax.all_to_all(part.reshape(NZ, rows, wider), 'z', 0, 0, tiled=True)  7.21 us
    all_to_all x1, starting transfers between devices, local(): right = lax.all_to_all(pay, 'din', 0, 0, tiled=True)  4.71 us
  transfers between devices with their start and end apart: 12, of which 5 were waited for; matrix products, arithmetic and copies ran while one was open for 1% of the time, Pallas kernels for 7%

profile of v3, /device:TPU:14, one launch (start us, length us, event | category | flops | bytes accessed | tf_op | source)
XLA Modules:
  0.0 122.4 jit_solution(5669205489383441294)
XLA Ops:
  7.9 2.3 %shard_map.93 = bf16[8,144,256]{2,1,0:T(8,128)(2,1)} custom-call(bf16[1024,256]{1,0:T(8,128)(2,1)} %w_hbm.1, bf16[64,1024]{1,0:T(8,128)(2,1)} %bitcast.14, bf16[64,256]{1,0:T(8,128)(2,1)} %b_ref.1, bf16[128,256]{1,0:T(8,128)(2,1)} %g_hbm.1), custom_call_target="tpu_custom_call" | custom-call | flops 33554432 | bytes 1343488 | tf_op jit(solution)/shard_map/pallas_call | solution.py:37
  10.2 25.0 %all_to_all.20.got_ref = bf16[8,144,256]{2,1,0:T(8,128)(2,1)S(1)} all-to-all(bf16[8,144,256]{2,1,0:T(8,128)(2,1)} %shard_map.93), channel_id=1, replica_groups=mesh['din'=8,'x'=4,'z'=8,'layer'=2] {'din'}, dimensions={0} | all-to-all | bytes 1179648 | tf_op jit(solution)/shard_map/all_to_all | solution.py:258
  35.2 0.9 broadcast_in_dim.2
  36.1 10.3 %all-to-all-start.1 = ((bf16[8,32,1024]{2,1,0:T(8,128)(2,1)}), bf16[8,32,1024]{2,1,0:T(8,128)(2,1)S(1)}, u32[]{:S(2)}, u32[]{:S(2)}) async-start(bf16[8,32,1024]{2,1,0:T(8,128)(2,1)} %broadcast_in_dim.2), calls=%async_computation.1 | async-start | bytes 1048576 | tf_op jit(solution)/shard_map/all_to_all | solution.py:266
  47.2 2.4 %collective-permute-start = (bf16[320,256]{1,0:T(8,128)(2,1)S(1)}, bf16[320,256]{1,0:T(8,128)(2,1)S(1)}, u32[]{:S(2)}, u32[]{:S(2)}) collective-permute-start(bf16[320,256]{1,0:T(8,128)(2,1)S(1)} %get-tuple-element.25), channel_id=1, source_target_pairs={{0,16},{16,32},{32,48},{48,0},{1,17},{17,33},{33,49},{49,1},{2,18}... | collective-permute-start | bytes 491528 | tf_op jit(solution)/shard_map/ppermute | solution.py:226
  49.6 3.5 %collective-permute-start.1 = (bf16[320,256]{1,0:T(8,128)(2,1)S(1)}, bf16[320,256]{1,0:T(8,128)(2,1)S(1)}, u32[]{:S(2)}, u32[]{:S(2)}) collective-permute-start(bf16[320,256]{1,0:T(8,128)(2,1)S(1)} %get-tuple-element.26), channel_id=1, source_target_pairs={{0,48},{16,0},{32,16},{48,32},{1,49},{17,1},{33,17},{49,33},{2,50}... | collective-permute-start | bytes 491528 | tf_op jit(solution)/shard_map/ppermute | solution.py:226
  53.1 3.3 %collective-permute-start.2 = (bf16[320,256]{1,0:T(8,128)(2,1)S(1)}, bf16[320,256]{1,0:T(8,128)(2,1)S(1)}, u32[]{:S(2)}, u32[]{:S(2)}) collective-permute-start(bf16[320,256]{1,0:T(8,128)(2,1)S(1)} %get-tuple-element.27), channel_id=1, source_target_pairs={{0,32},{16,48},{32,0},{48,16},{1,33},{17,49},{33,1},{49,17},{2,34}... | collective-permute-start | bytes 491528 | tf_op jit(solution)/shard_map/ppermute | solution.py:226
  56.4 2.5 %collective-permute-done.1.s2 = bf16[320,256]{1,0:T(8,128)(2,1)S(1)} collective-permute-done((bf16[320,256]{1,0:T(8,128)(2,1)S(1)}, bf16[320,256]{1,0:T(8,128)(2,1)S(1)}, u32[]{:S(2)}, u32[]{:S(2)}) %collective-permute-start.1) | collective-permute-done | bytes 163872 | tf_op jit(solution)/shard_map/ppermute | solution.py:226
  58.9 2.9 %collective-permute-done.2.s3 = bf16[320,256]{1,0:T(8,128)(2,1)S(1)} collective-permute-done((bf16[320,256]{1,0:T(8,128)(2,1)S(1)}, bf16[320,256]{1,0:T(8,128)(2,1)S(1)}, u32[]{:S(2)}, u32[]{:S(2)}) %collective-permute-start.2) | collective-permute-done | bytes 163872 | tf_op jit(solution)/shard_map/ppermute | solution.py:226
  62.6 6.1 %shard_map.95 = bf16[256,1280]{1,0:T(8,128)(2,1)} custom-call(s32[1]{0:T(128)} %bitcast.x_ref, bf16[320,256]{1,0:T(8,128)(2,1)} %copy-done, bf16[320,256]{1,0:T(8,128)(2,1)} %copy-done.5, bf16[320,256]{1,0:T(8,128)(2,1)} %copy-done.6, bf16[320,256]{1,0:T(8,128)(2,1)} %copy-done.7, bf16[4,1024,256]{2,1,0:T(8,128)(2,1)} %bitcast.9, bf16[64,1024]{1,0:T(8,128)(2,1)} %bitcast.15, ...), custom_call_target="tpu_custom_call" | custom-call | flops 536870912 | bytes 4063236 | tf_op jit(solution)/shard_map/pallas_call | solution.py:37
  68.8 7.2 %all-to-all-start.2 = ((bf16[8,32,1280]{2,1,0:T(8,128)(2,1)}), bf16[8,32,1280]{2,1,0:T(8,128)(2,1)S(1)}, u32[]{:S(2)}, u32[]{:S(2)}) async-start(bf16[8,32,1280]{2,1,0:T(8,128)(2,1)} %bitcast.13), calls=%async_computation.2 | async-start | bytes 1310720 | tf_op jit(solution)/shard_map/all_to_all | solution.py:286
  76.0 5.0 %shard_map.96 = (bf16[80,256]{1,0:T(8,128)(2,1)}, bf16[80,256]{1,0:T(8,128)(2,1)}, bf16[80,256]{1,0:T(8,128)(2,1)}, bf16[80,256]{1,0:T(8,128)(2,1)}) custom-call(s32[1]{0:T(128)} %bitcast.x_ref, bf16[320,256]{1,0:T(8,128)(2,1)} %copy-done, bf16[320,256]{1,0:T(8,128)(2,1)} %copy-done.5, bf16[320,256]{1,0:T(8,128)(2,1)} %copy-done.6, ...), custom_call_target="tpu_custom_call" | custom-call | flops 536870912 | bytes 3571716 | tf_op jit(solution)/shard_map/pallas_call | solution.py:37
  81.0 2.7 %collective-permute-start.3 = (bf16[80,256]{1,0:T(8,128)(2,1)}, bf16[80,256]{1,0:T(8,128)(2,1)S(1)}, u32[]{:S(2)}, u32[]{:S(2)}) collective-permute-start(bf16[80,256]{1,0:T(8,128)(2,1)} %get-tuple-element.31), channel_id=1, source_target_pairs={{0,48},{16,0},{32,16},{48,32},{1,49},{17,1},{33,17},{49,33},{2,50}... | collective-permute-start | bytes 122888 | tf_op jit(solution)/shard_map/ppermute | solution.py:226
  83.7 4.3 %collective-permute-start.4 = (bf16[80,256]{1,0:T(8,128)(2,1)}, bf16[80,256]{1,0:T(8,128)(2,1)S(1)}, u32[]{:S(2)}, u32[]{:S(2)}) collective-permute-start(bf16[80,256]{1,0:T(8,128)(2,1)} %get-tuple-element.32), channel_id=1, source_target_pairs={{0,16},{16,32},{32,48},{48,0},{1,17},{17,33},{33,49},{49,1},{2,18}... | collective-permute-start | bytes 122888 | tf_op jit(solution)/shard_map/ppermute | solution.py:226
  88.1 2.1 %collective-permute-start.5 = (bf16[80,256]{1,0:T(8,128)(2,1)}, bf16[80,256]{1,0:T(8,128)(2,1)S(1)}, u32[]{:S(2)}, u32[]{:S(2)}) collective-permute-start(bf16[80,256]{1,0:T(8,128)(2,1)} %get-tuple-element.33), channel_id=1, source_target_pairs={{0,32},{16,48},{32,0},{48,16},{1,33},{17,49},{33,1},{49,17},{2,34}... | collective-permute-start | bytes 122888 | tf_op jit(solution)/shard_map/ppermute | solution.py:226
  90.2 5.5 %collective-permute-done.5.r3 = bf16[80,256]{1,0:T(8,128)(2,1)S(1)} collective-permute-done((bf16[80,256]{1,0:T(8,128)(2,1)}, bf16[80,256]{1,0:T(8,128)(2,1)S(1)}, u32[]{:S(2)}, u32[]{:S(2)}) %collective-permute-start.5) | collective-permute-done | bytes 40992 | tf_op jit(solution)/shard_map/ppermute | solution.py:226
  95.7 0.8 copy-done.2
  97.1 4.7 %all-to-all-start.3 = ((bf16[8,16,256]{2,1,0:T(8,128)(2,1)}), bf16[8,16,256]{2,1,0:T(8,128)(2,1)S(1)}, u32[]{:S(2)}, u32[]{:S(2)}) async-start(bf16[8,16,256]{2,1,0:T(8,128)(2,1)} %shard_map.97), calls=%async_computation.3 | async-start | bytes 131072 | tf_op jit(solution)/shard_map/all_to_all | solution.py:299
  101.8 0.7 shard_map.98
  102.6 1.9 %collective-permute-start.6 = (bf16[16,256]{1,0:T(8,128)(2,1)S(1)}, bf16[16,256]{1,0:T(8,128)(2,1)S(1)}, u32[]{:S(2)}, u32[]{:S(2)}) collective-permute-start(bf16[16,256]{1,0:T(8,128)(2,1)S(1)} %get-tuple-element.37), channel_id=1, source_target_pairs={{0,16},{16,0},{32,48},{48,32},{1,17},{17,1},{33,49},{49,33},{2,18}... | collective-permute-start | bytes 24584 | tf_op jit(solution)/shard_map/ppermute | solution.py:230
  104.5 3.6 %collective-permute-done.6.got_ref = bf16[16,256]{1,0:T(8,128)(2,1)S(1)} collective-permute-done((bf16[16,256]{1,0:T(8,128)(2,1)S(1)}, bf16[16,256]{1,0:T(8,128)(2,1)S(1)}, u32[]{:S(2)}, u32[]{:S(2)}) %collective-permute-start.6) | collective-permute-done | bytes 8224 | tf_op jit(solution)/shard_map/ppermute | solution.py:230
  108.1 2.4 %collective-permute-start.7 = (bf16[16,256]{1,0:T(8,128)(2,1)S(1)}, bf16[16,256]{1,0:T(8,128)(2,1)S(1)}, u32[]{:S(2)}, u32[]{:S(2)}) collective-permute-start(bf16[16,256]{1,0:T(8,128)(2,1)S(1)} %get-tuple-element.39), channel_id=1, source_target_pairs={{0,48},{16,32},{32,16},{48,0},{1,49},{17,33},{33,17},{49,1},{2,50}... | collective-permute-start | bytes 24584 | tf_op jit(solution)/shard_map/ppermute | solution.py:230
  110.5 4.4 %collective-permute-done.7.more_ref = bf16[16,256]{1,0:T(8,128)(2,1)S(1)} collective-permute-done((bf16[16,256]{1,0:T(8,128)(2,1)S(1)}, bf16[16,256]{1,0:T(8,128)(2,1)S(1)}, u32[]{:S(2)}, u32[]{:S(2)}) %collective-permute-start.7) | collective-permute-done | bytes 8224 | tf_op jit(solution)/shard_map/ppermute | solution.py:230
  114.8 0.7 shard_map.100
  (29 shorter events, 3.0 us)
Async XLA Ops:
  7.2 28.1 %copy-start.8 = (bf16[32,1024]{1,0:T(8,128)(2,1)S(1)}, bf16[32,1024]{1,0:T(8,128)(2,1)}, u32[]{:S(2)}) copy-start(bf16[32,1024]{1,0:T(8,128)(2,1)} %param.6) | copy-start | bytes 196612
  7.2 54.6 %all-gather.3.cloned.1.call-start = ((), (), s32[]{:S(2)}) async-start(), calls=%async_computation.4 | async-start | bytes 2621440 | tf_op jit(solution)/shard_map/all_gather | solution.py:246
  7.9 38.5 %copy-start.1 = (bf16[64,256]{1,0:T(8,128)(2,1)S(1)}, bf16[64,256]{1,0:T(8,128)(2,1)}, u32[]{:S(2)}) copy-start(bf16[64,256]{1,0:T(8,128)(2,1)} %b_ref.1) | copy-start | bytes 98308
  7.9 38.5 %copy-start.3 = (f32[256]{0:T(256)S(1)}, f32[256]{0:T(256)}, u32[]{:S(2)}) copy-start(f32[256]{0:T(256)} %param.11) | copy-start | bytes 3076
  36.1 25.7 %all-to-all-start.1 = ((bf16[8,32,1024]{2,1,0:T(8,128)(2,1)}), bf16[8,32,1024]{2,1,0:T(8,128)(2,1)S(1)}, u32[]{:S(2)}, u32[]{:S(2)}) async-start(bf16[8,32,1024]{2,1,0:T(8,128)(2,1)} %broadcast_in_dim.2), calls=%async_computation.1 | async-start | bytes 1048576 | tf_op jit(solution)/shard_map/all_to_all | solution.py:266
  46.6 0.7 copy-start
  47.2 9.2 %collective-permute-start = (bf16[320,256]{1,0:T(8,128)(2,1)S(1)}, bf16[320,256]{1,0:T(8,128)(2,1)S(1)}, u32[]{:S(2)}, u32[]{:S(2)}) collective-permute-start(bf16[320,256]{1,0:T(8,128)(2,1)S(1)} %get-tuple-element.25), channel_id=1, source_target_pairs={{0,16},{16,32},{32,48},{48,0},{1,17},{17,33},{33,49},{49,1},{2,18}... | collective-permute-start | bytes 491528 | tf_op jit(solution)/shard_map/ppermute | solution.py:226
  49.6 9.3 %collective-permute-start.1 = (bf16[320,256]{1,0:T(8,128)(2,1)S(1)}, bf16[320,256]{1,0:T(8,128)(2,1)S(1)}, u32[]{:S(2)}, u32[]{:S(2)}) collective-permute-start(bf16[320,256]{1,0:T(8,128)(2,1)S(1)} %get-tuple-element.26), channel_id=1, source_target_pairs={{0,48},{16,0},{32,16},{48,32},{1,49},{17,1},{33,17},{49,33},{2,50}... | collective-permute-start | bytes 491528 | tf_op jit(solution)/shard_map/ppermute | solution.py:226
  53.1 8.7 %collective-permute-start.2 = (bf16[320,256]{1,0:T(8,128)(2,1)S(1)}, bf16[320,256]{1,0:T(8,128)(2,1)S(1)}, u32[]{:S(2)}, u32[]{:S(2)}) collective-permute-start(bf16[320,256]{1,0:T(8,128)(2,1)S(1)} %get-tuple-element.27), channel_id=1, source_target_pairs={{0,32},{16,48},{32,0},{48,16},{1,33},{17,49},{33,1},{49,17},{2,34}... | collective-permute-start | bytes 491528 | tf_op jit(solution)/shard_map/ppermute | solution.py:226
  56.4 5.4 %copy-start.5 = (bf16[320,256]{1,0:T(8,128)(2,1)}, bf16[320,256]{1,0:T(8,128)(2,1)S(1)}, u32[]{:S(2)}) copy-start(bf16[320,256]{1,0:T(8,128)(2,1)S(1)} %collective-permute-done.s1) | copy-start | bytes 491524
  58.9 3.0 %copy-start.6 = (bf16[320,256]{1,0:T(8,128)(2,1)}, bf16[320,256]{1,0:T(8,128)(2,1)S(1)}, u32[]{:S(2)}) copy-start(bf16[320,256]{1,0:T(8,128)(2,1)S(1)} %collective-permute-done.1.s2) | copy-start | bytes 491524
  61.8 0.7 copy-start.7
  61.8 0.8 copy-start.4
  68.8 28.3 %all-to-all-start.2 = ((bf16[8,32,1280]{2,1,0:T(8,128)(2,1)}), bf16[8,32,1280]{2,1,0:T(8,128)(2,1)S(1)}, u32[]{:S(2)}, u32[]{:S(2)}) async-start(bf16[8,32,1280]{2,1,0:T(8,128)(2,1)} %bitcast.13), calls=%async_computation.2 | async-start | bytes 1310720 | tf_op jit(solution)/shard_map/all_to_all | solution.py:286
  81.0 9.2 %collective-permute-start.3 = (bf16[80,256]{1,0:T(8,128)(2,1)}, bf16[80,256]{1,0:T(8,128)(2,1)S(1)}, u32[]{:S(2)}, u32[]{:S(2)}) collective-permute-start(bf16[80,256]{1,0:T(8,128)(2,1)} %get-tuple-element.31), channel_id=1, source_target_pairs={{0,48},{16,0},{32,16},{48,32},{1,49},{17,1},{33,17},{49,33},{2,50}... | collective-permute-start | bytes 122888 | tf_op jit(solution)/shard_map/ppermute | solution.py:226
  83.7 6.4 %collective-permute-start.4 = (bf16[80,256]{1,0:T(8,128)(2,1)}, bf16[80,256]{1,0:T(8,128)(2,1)S(1)}, u32[]{:S(2)}, u32[]{:S(2)}) collective-permute-start(bf16[80,256]{1,0:T(8,128)(2,1)} %get-tuple-element.32), channel_id=1, source_target_pairs={{0,16},{16,32},{32,48},{48,0},{1,17},{17,33},{33,49},{49,1},{2,18}... | collective-permute-start | bytes 122888 | tf_op jit(solution)/shard_map/ppermute | solution.py:226
  88.1 7.6 %collective-permute-start.5 = (bf16[80,256]{1,0:T(8,128)(2,1)}, bf16[80,256]{1,0:T(8,128)(2,1)S(1)}, u32[]{:S(2)}, u32[]{:S(2)}) collective-permute-start(bf16[80,256]{1,0:T(8,128)(2,1)} %get-tuple-element.33), channel_id=1, source_target_pairs={{0,32},{16,48},{32,0},{48,16},{1,33},{17,49},{33,1},{49,17},{2,34}... | collective-permute-start | bytes 122888 | tf_op jit(solution)/shard_map/ppermute | solution.py:226
  95.7 0.8 copy-start.2
  97.1 17.7 %all-to-all-start.3 = ((bf16[8,16,256]{2,1,0:T(8,128)(2,1)}), bf16[8,16,256]{2,1,0:T(8,128)(2,1)S(1)}, u32[]{:S(2)}, u32[]{:S(2)}) async-start(bf16[8,16,256]{2,1,0:T(8,128)(2,1)} %shard_map.97), calls=%async_computation.3 | async-start | bytes 131072 | tf_op jit(solution)/shard_map/all_to_all | solution.py:299
  102.6 5.5 %collective-permute-start.6 = (bf16[16,256]{1,0:T(8,128)(2,1)S(1)}, bf16[16,256]{1,0:T(8,128)(2,1)S(1)}, u32[]{:S(2)}, u32[]{:S(2)}) collective-permute-start(bf16[16,256]{1,0:T(8,128)(2,1)S(1)} %get-tuple-element.37), channel_id=1, source_target_pairs={{0,16},{16,0},{32,48},{48,32},{1,17},{17,1},{33,49},{49,33},{2,18}... | collective-permute-start | bytes 24584 | tf_op jit(solution)/shard_map/ppermute | solution.py:230
  108.1 6.7 %collective-permute-start.7 = (bf16[16,256]{1,0:T(8,128)(2,1)S(1)}, bf16[16,256]{1,0:T(8,128)(2,1)S(1)}, u32[]{:S(2)}, u32[]{:S(2)}) collective-permute-start(bf16[16,256]{1,0:T(8,128)(2,1)S(1)} %get-tuple-element.39), channel_id=1, source_target_pairs={{0,48},{16,32},{32,16},{48,0},{1,49},{17,33},{33,17},{49,1},{2,50}... | collective-permute-start | bytes 24584 | tf_op jit(solution)/shard_map/ppermute | solution.py:230
Sparse Core Ops, SparseCore 0:
  10.1 38.9 all-gather.2

commit v4 on v3

--- a/solution.py
+++ b/solution.py
@@ -62,11 +62,22 @@
     return jnp.where(row == 0, high, jnp.where(row == 1, value - high, 0.0)).astype(BF16)
 
 
-def merge_body(w_hbm, at_hbm, b_hbm, g_hbm, pay_ref, w_ref, at_ref, b_ref, g_ref, sems):
+def merge_body(
+    w_hbm, at_hbm, b_hbm, g_hbm, acts_hbm, pay_ref, many_hbm, w_ref, at_ref, b_ref, g_ref, acts_ref, sems, more
+):
     copies = fetch(
-        ((w_hbm, w_ref), (at_hbm, at_ref), (b_hbm, b_ref), (g_hbm, g_ref)), sems
-    )
-    for copy in copies:
+        (
+            (acts_hbm, acts_ref),
+            (w_hbm, w_ref),
+            (at_hbm, at_ref),
+            (b_hbm, b_ref),
+            (g_hbm, g_ref),
+        ),
+        sems,
+    )
+    copies[0].wait()
+    repeats = fetch([(acts_ref, many_hbm.at[z]) for z in range(NZ)], more)
+    for copy in copies[1:]:
         copy.wait()
     din, width = w_ref.shape
     tokens = g_ref.shape[0]
@@ -80,6 +91,8 @@
     for y in range(NY):
         pay_ref[y, pl.ds(0, tokens), :] = g_ref[...]
         pay_ref[y, pl.ds(tokens, 16), :] = tail
+    for copy in repeats:
+        copy.wait()
 
 
 def scale_body(x_ref, got_ref, mag_ref, b_ref, *outs):
@@ -105,23 +118,13 @@
 
 
 def acts_body(
-    x_ref, s0, s1, s2, s3, wide_hbm, at, whole, out_hbm, wide, out, lefts, sems, out_sems
+    x_ref, s0, s1, s2, s3, wide, at, whole, out_hbm, out, lefts, out_sems
 ):
     blocks = (s0, s1, s2, s3)
     tokens, din = whole.shape
     rank = at.shape[0]
     steps = din // STEP
-    copies = fetch(
-        [
-            (
-                wide_hbm.at[source(x_ref, k), pl.ds(i * STEP, STEP)],
-                wide.at[k, pl.ds(i * STEP, STEP)],
-            )
-            for i in range(steps)
-            for k in range(NX)
-        ],
-        sems,
-    )
+    place = [source(x_ref, k) for k in range(NX)]
     low = jnp.zeros((tokens, NX * rank), F32)
     for s in blocks:
         b = s[pl.ds(tokens, rank), :]
@@ -155,27 +158,23 @@
     for i in range(steps):
         total = dot(low[:, :rank], at[:, pl.ds(i * STEP, STEP)], NN)
         for k, s in enumerate(blocks):
-            copies[i * NX + k].wait()
-            total += dot(s[pl.ds(0, tokens), :], wide[k, pl.ds(i * STEP, STEP), :], NT)
+            total += dot(
+                s[pl.ds(0, tokens), :], wide[place[k], pl.ds(i * STEP, STEP), :], NT
+            )
         out[:, pl.ds(i * STEP, STEP)] = total.astype(BF16)
         send(i * STEP, STEP)
     for copy in sends:
         copy.wait()
 
 
-def stat_body(x_ref, s0, s1, s2, s3, wide_hbm, at, whole, *rest):
-    outs, (wide, sems) = rest[:NX], rest[NX:]
-    copies = fetch(
-        [(wide_hbm.at[source(x_ref, k)], wide.at[k]) for k in range(NX)], sems
-    )
+def stat_body(x_ref, s0, s1, s2, s3, wide, at, whole, *outs):
     rank = at.shape[0]
     tokens = whole.shape[0]
     down = dot(whole[...], at[...], NT).astype(BF16)
     for k, (s, out) in enumerate(zip((s0, s1, s2, s3), outs)):
         scaled = s[pl.ds(0, tokens), :]
         out[pl.ds(0, rank), :] = dot(down, scaled, TN).astype(BF16)
-        copies[k].wait()
-        outputs = dot(whole[...], wide[k], NN) + dot(down, s[pl.ds(tokens, rank), :], NN)
+        outputs = dot(whole[...], wide[source(x_ref, k)], NN) + dot(down, s[pl.ds(tokens, rank), :], NN)
         stat = jnp.sum(scaled.astype(F32) * outputs, axis=0, keepdims=True)
         out[pl.ds(rank, 16), :] = two_rows(stat, stat.shape[1])
 
@@ -245,14 +244,15 @@
     a_turned = a_left.T
     wide = lax.all_gather(w_base, "x")
     parts = (w_base, a_turned, b_right, grad_y)
-    (pay,) = call(
+    pay, many = call(
         merge_body,
-        [shape((NY, grad_y.shape[0] + 16, width))],
+        [shape((NY, grad_y.shape[0] + 16, width)), shape((NZ, rows, din))],
         2 * din * width * rank,
-        *parts,
-        far=(0, 1, 2, 3),
-        scratch=[pltpu.VMEM(p.shape, p.dtype) for p in parts]
-        + [pltpu.SemaphoreType.DMA((4,))],
+        *parts, acts,
+        far=(0, 1, 2, 3, 4),
+        out_specs=[VMEM, HBM],
+        scratch=[pltpu.VMEM(p.shape, p.dtype) for p in (*parts, acts)]
+        + [pltpu.SemaphoreType.DMA((5,)), pltpu.SemaphoreType.DMA((NZ,))],
         limit=60,
     )
     got = lax.all_to_all(pay, "din", 0, 0, tiled=True)
@@ -263,25 +263,18 @@
         spot, got, mags, b_right,
     )
     blocks = [scaled[0]] + [shift(scaled[k], HOPS[k]) for k in range(1, NX)]
-    whole = lax.all_to_all(
-        after(jnp.broadcast_to(acts[None], (NZ, rows, din)), got), "z", 0, 0, tiled=True
-    ).reshape(tokens, din)
-    room = pltpu.VMEM((NX, din, width), BF16)
+    whole = lax.all_to_all(after(many, got), "z", 0, 0, tiled=True).reshape(tokens, din)
     (part,) = call(
         acts_body,
         [shape((tokens, wider))],
         2 * tokens * din * width * NX,
         spot, *blocks, wide, a_turned, whole,
-        far=(5,),
         out_specs=[HBM],
         scratch=[
-            room,
             pltpu.VMEM((tokens, wider), BF16),
             pltpu.VMEM((tokens, NX * rank), F32),
-            pltpu.SemaphoreType.DMA((NX * (din // STEP),)),
             pltpu.SemaphoreType.DMA((1 + din // STEP,)),
         ],
-        limit=58,
     )
     back = lax.all_to_all(part.reshape(NZ, rows, wider), "z", 0, 0, tiled=True)
     sides = call(
@@ -289,14 +282,8 @@
         [shape((rank + 16, width))] * NX,
         2 * tokens * din * width * NX,
         after(spot, part), *blocks, wide, a_turned, whole,
-        far=(5,),
-        scratch=[room, pltpu.SemaphoreType.DMA((NX,))],
-        limit=58,
     )
     met = [sides[0]] + [shift(sides[k], NX - HOPS[k]) for k in range(1, NX)]
-    (pay,) = call(meet_body, [shape((NY, 16, width))], 0, *met)
-    back, pay = lax.optimization_barrier((back, pay))
-    right = lax.all_to_all(pay, "din", 0, 0, tiled=True)
     summed, keep, send = call(
         sum_body,
         [shape((rows, din)), shape((16, width), F32), shape((16, width))],
@@ -304,8 +291,11 @@
         spot, back,
         scratch=[pltpu.VMEM((rows, NX * rank), F32)],
     )
+    more = swap(send, 1)
+    (pay,) = call(meet_body, [shape((NY, 16, width))], 0, after(met[0], more), *met[1:])
+    right = lax.all_to_all(pay, "din", 0, 0, tiled=True)
     own, send = call(
-        pair_body, [shape((8, width), F32), shape((16, width))], 0, keep, swap(send, 1)
+        pair_body, [shape((8, width), F32), shape((16, width))], 0, keep, more
     )
     grad_left, grad_right, grad_mag = call(
         last_body,

time: 123 us -> 118 us (0.959)
  the two profiles are of different devices: /device:TPU:14 before, /device:TPU:2 now
where the time goes in v4:
time: 118 us
  starting transfers between devices  46.7 us (40%)
  blocking collectives  26 us (22%)
  waiting for transfers between devices  16.6 us (14%)
  between operations  14.2 us (12%)
  Pallas kernels  8.79 us (7%)
  local copies, waits for them, and re-layouts  5.28 us (4%)
    all_to_all x1, blocking collectives, local(): got = lax.all_to_all(pay, 'din', 0, 0, tiled=True)  26 us
    ppermute x6, starting transfers between devices, shift(): return lax.ppermute(block, 'x', [(i, (i + hop) % NX) for i in range(NX)])  21 us
    all_to_all x1, starting transfers between devices, local(): lax.all_to_all(after(many, got), 'z', 0, 0, tiled=True).reshape(tokens, din)  10.3 us
    pallas_call x8, Pallas kernels, call(): pl.pallas_call(body, out_shape=outs, in_specs=specs, out_specs=out_specs...  8.79 us
    ppermute x2, waiting for transfers between devices, swap(): return lax.ppermute(block, 'x', [(i, i ^ mask) for i in range(NX)])  6.44 us
    all_to_all x1, starting transfers between devices, local(): back = lax.all_to_all(part.reshape(NZ, rows, wider), 'z', 0, 0, tiled=True)  6.26 us
    unnamed x26, local copies, waits for them, and re-layouts  5.28 us
    ppermute x6, waiting for transfers between devices, shift(): return lax.ppermute(block, 'x', [(i, (i + hop) % NX) for i in range(NX)])  4.66 us
  transfers between devices with their start and end apart: 12, of which 7 were waited for; matrix products, arithmetic and copies ran while one was open for 0% of the time, Pallas kernels for 4%

profile of v4, /device:TPU:2, one launch (start us, length us, event | category | flops | bytes accessed | tf_op | source)
XLA Modules:
  0.0 117.6 jit_solution(7678783790265336415)
XLA Ops:
  7.9 2.6 %shard_map.93 = (bf16[8,144,256]{2,1,0:T(8,128)(2,1)}, bf16[8,32,1024]{2,1,0:T(8,128)(2,1)}) custom-call(bf16[1024,256]{1,0:T(8,128)(2,1)} %w_hbm.1, bf16[64,1024]{1,0:T(8,128)(2,1)} %bitcast.11, bf16[64,256]{1,0:T(8,128)(2,1)} %b_ref.1, bf16[128,256]{1,0:T(8,128)(2,1)} %g_hbm.1, bf16[32,1024]{1,0:T(8,128)(2,1)} %acts_hbm.1), custom_call_target="tpu_custom_call" | custom-call | flops 33554432 | bytes 1933312 | tf_op jit(solution)/shard_map/pallas_call | solution.py:37
  10.5 26.0 %all_to_all.20.got_ref = bf16[8,144,256]{2,1,0:T(8,128)(2,1)S(1)} all-to-all(bf16[8,144,256]{2,1,0:T(8,128)(2,1)} %get-tuple-element.25), channel_id=1, replica_groups=mesh['din'=8,'x'=4,'z'=8,'layer'=2] {'din'}, dimensions={0} | all-to-all | bytes 1179648 | tf_op jit(solution)/shard_map/all_to_all | solution.py:258
  36.5 10.3 %all-to-all-start.1 = ((bf16[8,32,1024]{2,1,0:T(8,128)(2,1)}), bf16[8,32,1024]{2,1,0:T(8,128)(2,1)S(1)}, u32[]{:S(2)}, u32[]{:S(2)}) async-start(bf16[8,32,1024]{2,1,0:T(8,128)(2,1)} %get-tuple-element.31), calls=%async_computation.1 | async-start | bytes 1048576 | tf_op jit(solution)/shard_map/all_to_all | solution.py:266
  47.0 3.4 %collective-permute-start = (bf16[320,256]{1,0:T(8,128)(2,1)S(1)}, bf16[320,256]{1,0:T(8,128)(2,1)S(1)}, u32[]{:S(2)}, u32[]{:S(2)}) collective-permute-start(bf16[320,256]{1,0:T(8,128)(2,1)S(1)} %get-tuple-element.27), channel_id=1, source_target_pairs={{0,16},{16,32},{32,48},{48,0},{1,17},{17,33},{33,49},{49,1},{2,18}... | collective-permute-start | bytes 491528 | tf_op jit(solution)/shard_map/ppermute | solution.py:225
  50.4 2.4 %collective-permute-start.1 = (bf16[320,256]{1,0:T(8,128)(2,1)S(1)}, bf16[320,256]{1,0:T(8,128)(2,1)S(1)}, u32[]{:S(2)}, u32[]{:S(2)}) collective-permute-start(bf16[320,256]{1,0:T(8,128)(2,1)S(1)} %get-tuple-element.28), channel_id=1, source_target_pairs={{0,48},{16,0},{32,16},{48,32},{1,49},{17,1},{33,17},{49,33},{2,50}... | collective-permute-start | bytes 491528 | tf_op jit(solution)/shard_map/ppermute | solution.py:225
  52.8 4.0 %collective-permute-start.2 = (bf16[320,256]{1,0:T(8,128)(2,1)S(1)}, bf16[320,256]{1,0:T(8,128)(2,1)S(1)}, u32[]{:S(2)}, u32[]{:S(2)}) collective-permute-start(bf16[320,256]{1,0:T(8,128)(2,1)S(1)} %get-tuple-element.29), channel_id=1, source_target_pairs={{0,32},{16,48},{32,0},{48,16},{1,33},{17,49},{33,1},{49,17},{2,34}... | collective-permute-start | bytes 491528 | tf_op jit(solution)/shard_map/ppermute | solution.py:225
  56.9 2.5 %collective-permute-done.1.s2 = bf16[320,256]{1,0:T(8,128)(2,1)S(1)} collective-permute-done((bf16[320,256]{1,0:T(8,128)(2,1)S(1)}, bf16[320,256]{1,0:T(8,128)(2,1)S(1)}, u32[]{:S(2)}, u32[]{:S(2)}) %collective-permute-start.1) | collective-permute-done | bytes 163872 | tf_op jit(solution)/shard_map/ppermute | solution.py:225
  59.4 2.2 %collective-permute-done.2.s3 = bf16[320,256]{1,0:T(8,128)(2,1)S(1)} collective-permute-done((bf16[320,256]{1,0:T(8,128)(2,1)S(1)}, bf16[320,256]{1,0:T(8,128)(2,1)S(1)}, u32[]{:S(2)}, u32[]{:S(2)}) %collective-permute-start.2) | collective-permute-done | bytes 163872 | tf_op jit(solution)/shard_map/ppermute | solution.py:225
  61.6 1.0 all-to-all-done.1
  62.6 1.6 %copy-done = bf16[4096,256]{1,0:T(8,128)(2,1)S(1)} copy-done((bf16[4096,256]{1,0:T(8,128)(2,1)S(1)}, bf16[4096,256]{1,0:T(8,128)(2,1)}, u32[]{:S(2)}) %copy-start) | copy-done | bytes 2097176
  64.2 2.3 %shard_map.95 = bf16[256,1280]{1,0:T(8,128)(2,1)} custom-call(s32[1]{0:T(128)} %bitcast.x_ref, bf16[320,256]{1,0:T(8,128)(2,1)S(1)} %get-tuple-element.26.s0, bf16[320,256]{1,0:T(8,128)(2,1)S(1)} %collective-permute-done.s1, bf16[320,256]{1,0:T(8,128)(2,1)S(1)} %collective-permute-done.1.s2, bf16[320,256]{1,0:T(8,128)(2,1)S(1)} %collective-permute-done.2.s3, ...), custom_call_target="tpu_custom_call" | custom-call | flops 536870912 | bytes 4063236 | tf_op jit(solution)/shard_map/pallas_call | solution.py:37
  66.5 6.3 %all-to-all-start.2 = ((bf16[8,32,1280]{2,1,0:T(8,128)(2,1)}), bf16[8,32,1280]{2,1,0:T(8,128)(2,1)S(1)}, u32[]{:S(2)}, u32[]{:S(2)}) async-start(bf16[8,32,1280]{2,1,0:T(8,128)(2,1)} %bitcast.5), calls=%async_computation.2 | async-start | bytes 1310720 | tf_op jit(solution)/shard_map/all_to_all | solution.py:279
  75.5 0.9 copy-done.10
  76.5 1.7 %shard_map.98 = (bf16[80,256]{1,0:T(8,128)(2,1)S(1)}, bf16[80,256]{1,0:T(8,128)(2,1)}, bf16[80,256]{1,0:T(8,128)(2,1)S(1)}, bf16[80,256]{1,0:T(8,128)(2,1)S(1)}) custom-call(s32[1]{0:T(128)} %bitcast.x_ref, bf16[320,256]{1,0:T(8,128)(2,1)S(1)} %copy-done.4, bf16[320,256]{1,0:T(8,128)(2,1)S(1)} %copy-done.6, bf16[320,256]{1,0:T(8,128)(2,1)S(1)} %copy-done.8, ...), custom_call_target="tpu_custom_call" | custom-call | flops 536870912 | bytes 3571716 | tf_op jit(solution)/shard_map/pallas_call | solution.py:37
  78.2 3.6 %collective-permute-start.5 = (bf16[80,256]{1,0:T(8,128)(2,1)}, bf16[80,256]{1,0:T(8,128)(2,1)S(1)}, u32[]{:S(2)}, u32[]{:S(2)}) collective-permute-start(bf16[80,256]{1,0:T(8,128)(2,1)} %get-tuple-element.40), channel_id=1, source_target_pairs={{0,48},{16,0},{32,16},{48,32},{1,49},{17,1},{33,17},{49,33},{2,50}... | collective-permute-start | bytes 122888 | tf_op jit(solution)/shard_map/ppermute | solution.py:225
  81.8 2.2 %collective-permute-start.6 = (bf16[80,256]{1,0:T(8,128)(2,1)S(1)}, bf16[80,256]{1,0:T(8,128)(2,1)S(1)}, u32[]{:S(2)}, u32[]{:S(2)}) collective-permute-start(bf16[80,256]{1,0:T(8,128)(2,1)S(1)} %get-tuple-element.41), channel_id=1, source_target_pairs={{0,16},{16,32},{32,48},{48,0},{1,17},{17,33},{33,49},{49,1},{2,18}... | collective-permute-start | bytes 122888 | tf_op jit(solution)/shard_map/ppermute | solution.py:225
  84.0 5.2 %collective-permute-start.7 = (bf16[80,256]{1,0:T(8,128)(2,1)S(1)}, bf16[80,256]{1,0:T(8,128)(2,1)S(1)}, u32[]{:S(2)}, u32[]{:S(2)}) collective-permute-start(bf16[80,256]{1,0:T(8,128)(2,1)S(1)} %get-tuple-element.42), channel_id=1, source_target_pairs={{0,32},{16,48},{32,0},{48,16},{1,33},{17,49},{33,1},{49,17},{2,34}... | collective-permute-start | bytes 122888 | tf_op jit(solution)/shard_map/ppermute | solution.py:225
  89.3 1.0 all-to-all-done.2.got_ref
  91.0 2.5 %collective-permute-start.3 = (bf16[16,256]{1,0:T(8,128)(2,1)S(1)}, bf16[16,256]{1,0:T(8,128)(2,1)S(1)}, u32[]{:S(2)}, u32[]{:S(2)}) collective-permute-start(bf16[16,256]{1,0:T(8,128)(2,1)S(1)} %get-tuple-element.34), channel_id=1, source_target_pairs={{0,16},{16,0},{32,48},{48,32},{1,17},{17,1},{33,49},{49,33},{2,18}... | collective-permute-start | bytes 24584 | tf_op jit(solution)/shard_map/ppermute | solution.py:229
  93.5 3.0 %collective-permute-done.3.got_ref = bf16[16,256]{1,0:T(8,128)(2,1)S(1)} collective-permute-done((bf16[16,256]{1,0:T(8,128)(2,1)S(1)}, bf16[16,256]{1,0:T(8,128)(2,1)S(1)}, u32[]{:S(2)}, u32[]{:S(2)}) %collective-permute-start.3) | collective-permute-done | bytes 8224 | tf_op jit(solution)/shard_map/ppermute | solution.py:229
  97.2 4.5 %all-to-all-start.3 = ((bf16[8,16,256]{2,1,0:T(8,128)(2,1)}), bf16[8,16,256]{2,1,0:T(8,128)(2,1)S(1)}, u32[]{:S(2)}, u32[]{:S(2)}) async-start(bf16[8,16,256]{2,1,0:T(8,128)(2,1)} %shard_map.99), calls=%async_computation.3 | async-start | bytes 131072 | tf_op jit(solution)/shard_map/all_to_all | solution.py:296
  101.7 2.1 %collective-permute-start.4 = (bf16[16,256]{1,0:T(8,128)(2,1)S(1)}, bf16[16,256]{1,0:T(8,128)(2,1)S(1)}, u32[]{:S(2)}, u32[]{:S(2)}) collective-permute-start(bf16[16,256]{1,0:T(8,128)(2,1)S(1)} %get-tuple-element.36), channel_id=1, source_target_pairs={{0,48},{16,32},{32,16},{48,0},{1,49},{17,33},{33,17},{49,1},{2,50}... | collective-permute-start | bytes 24584 | tf_op jit(solution)/shard_map/ppermute | solution.py:229
  103.8 3.4 %collective-permute-done.4.more_ref = bf16[16,256]{1,0:T(8,128)(2,1)S(1)} collective-permute-done((bf16[16,256]{1,0:T(8,128)(2,1)S(1)}, bf16[16,256]{1,0:T(8,128)(2,1)S(1)}, u32[]{:S(2)}, u32[]{:S(2)}) %collective-permute-start.4) | collective-permute-done | bytes 8224 | tf_op jit(solution)/shard_map/ppermute | solution.py:229
  107.3 2.8 %all-to-all-done.3.got_ref = bf16[8,16,256]{2,1,0:T(8,128)(2,1)S(1)} async-done(((bf16[8,16,256]{2,1,0:T(8,128)(2,1)}), bf16[8,16,256]{2,1,0:T(8,128)(2,1)S(1)}, u32[]{:S(2)}, u32[]{:S(2)}) %all-to-all-start.3) | async-done | bytes 65568 | tf_op jit(solution)/shard_map/all_to_all | solution.py:296
  (36 shorter events, 5.7 us)
Async XLA Ops:
  7.2 39.7 %copy-start.11 = (bf16[64,256]{1,0:T(8,128)(2,1)S(1)}, bf16[64,256]{1,0:T(8,128)(2,1)}, u32[]{:S(2)}) copy-start(bf16[64,256]{1,0:T(8,128)(2,1)} %b_ref.1) | copy-start | bytes 98308
  7.2 55.4 %copy-start.2 = (bf16[1024,64]{0,1:T(8,128)(2,1)S(1)}, bf16[1024,64]{0,1:T(8,128)(2,1)}, u32[]{:S(2)}) copy-start(bf16[1024,64]{0,1:T(8,128)(2,1)} %param.9) | copy-start | bytes 393220
  7.2 39.7 %copy-start.12 = (f32[256]{0:T(256)S(1)}, f32[256]{0:T(256)}, u32[]{:S(2)}) copy-start(f32[256]{0:T(256)} %param.11) | copy-start | bytes 3076
  7.2 55.4 %all-gather.3.cloned.1.call-start = ((), (), s32[]{:S(2)}) async-start(), calls=%async_computation.4 | async-start | bytes 2621440 | tf_op jit(solution)/shard_map/all_gather | solution.py:245
  36.5 26.1 %all-to-all-start.1 = ((bf16[8,32,1024]{2,1,0:T(8,128)(2,1)}), bf16[8,32,1024]{2,1,0:T(8,128)(2,1)S(1)}, u32[]{:S(2)}, u32[]{:S(2)}) async-start(bf16[8,32,1024]{2,1,0:T(8,128)(2,1)} %get-tuple-element.31), calls=%async_computation.1 | async-start | bytes 1048576 | tf_op jit(solution)/shard_map/all_to_all | solution.py:266
  47.0 19.5 %copy-start.3 = (bf16[320,256]{1,0:T(8,128)(2,1)}, bf16[320,256]{1,0:T(8,128)(2,1)S(1)}, u32[]{:S(2)}) copy-start(bf16[320,256]{1,0:T(8,128)(2,1)S(1)} %get-tuple-element.26.s0) | copy-start | bytes 491524
  47.0 9.9 %collective-permute-start = (bf16[320,256]{1,0:T(8,128)(2,1)S(1)}, bf16[320,256]{1,0:T(8,128)(2,1)S(1)}, u32[]{:S(2)}, u32[]{:S(2)}) collective-permute-start(bf16[320,256]{1,0:T(8,128)(2,1)S(1)} %get-tuple-element.27), channel_id=1, source_target_pairs={{0,16},{16,32},{32,48},{48,0},{1,17},{17,33},{33,49},{49,1},{2,18}... | collective-permute-start | bytes 491528 | tf_op jit(solution)/shard_map/ppermute | solution.py:225
  50.4 9.0 %collective-permute-start.1 = (bf16[320,256]{1,0:T(8,128)(2,1)S(1)}, bf16[320,256]{1,0:T(8,128)(2,1)S(1)}, u32[]{:S(2)}, u32[]{:S(2)}) collective-permute-start(bf16[320,256]{1,0:T(8,128)(2,1)S(1)} %get-tuple-element.28), channel_id=1, source_target_pairs={{0,48},{16,0},{32,16},{48,32},{1,49},{17,1},{33,17},{49,33},{2,50}... | collective-permute-start | bytes 491528 | tf_op jit(solution)/shard_map/ppermute | solution.py:225
  52.8 8.7 %collective-permute-start.2 = (bf16[320,256]{1,0:T(8,128)(2,1)S(1)}, bf16[320,256]{1,0:T(8,128)(2,1)S(1)}, u32[]{:S(2)}, u32[]{:S(2)}) collective-permute-start(bf16[320,256]{1,0:T(8,128)(2,1)S(1)} %get-tuple-element.29), channel_id=1, source_target_pairs={{0,32},{16,48},{32,0},{48,16},{1,33},{17,49},{33,1},{49,17},{2,34}... | collective-permute-start | bytes 491528 | tf_op jit(solution)/shard_map/ppermute | solution.py:225
  56.9 9.6 %copy-start.5 = (bf16[320,256]{1,0:T(8,128)(2,1)}, bf16[320,256]{1,0:T(8,128)(2,1)S(1)}, u32[]{:S(2)}) copy-start(bf16[320,256]{1,0:T(8,128)(2,1)S(1)} %collective-permute-done.s1) | copy-start | bytes 491524
  59.4 7.1 %copy-start.7 = (bf16[320,256]{1,0:T(8,128)(2,1)}, bf16[320,256]{1,0:T(8,128)(2,1)S(1)}, u32[]{:S(2)}) copy-start(bf16[320,256]{1,0:T(8,128)(2,1)S(1)} %collective-permute-done.1.s2) | copy-start | bytes 491524
  61.6 5.0 %copy-start.9 = (bf16[320,256]{1,0:T(8,128)(2,1)}, bf16[320,256]{1,0:T(8,128)(2,1)S(1)}, u32[]{:S(2)}) copy-start(bf16[320,256]{1,0:T(8,128)(2,1)S(1)} %collective-permute-done.2.s3) | copy-start | bytes 491524
  62.6 1.6 %copy-start = (bf16[4096,256]{1,0:T(8,128)(2,1)S(1)}, bf16[4096,256]{1,0:T(8,128)(2,1)}, u32[]{:S(2)}) copy-start(bf16[4096,256]{1,0:T(8,128)(2,1)} %all-gather.3.cloned.1.call-done) | copy-start | bytes 6291460
  64.2 8.6 %copy-start.1 = (bf16[4096,256]{1,0:T(8,128)(2,1)S(1)}, bf16[4096,256]{1,0:T(8,128)(2,1)}, u32[]{:S(2)}) copy-start(bf16[4096,256]{1,0:T(8,128)(2,1)} %all-gather.3.cloned.1.call-done) | copy-start | bytes 6291460
  66.5 23.7 %all-to-all-start.2 = ((bf16[8,32,1280]{2,1,0:T(8,128)(2,1)}), bf16[8,32,1280]{2,1,0:T(8,128)(2,1)S(1)}, u32[]{:S(2)}, u32[]{:S(2)}) async-start(bf16[8,32,1280]{2,1,0:T(8,128)(2,1)} %bitcast.5), calls=%async_computation.2 | async-start | bytes 1310720 | tf_op jit(solution)/shard_map/all_to_all | solution.py:279
  72.8 0.9 copy-start.4
  74.6 0.9 copy-start.8
  75.5 0.9 copy-start.10
  78.2 18.3 %collective-permute-start.5 = (bf16[80,256]{1,0:T(8,128)(2,1)}, bf16[80,256]{1,0:T(8,128)(2,1)S(1)}, u32[]{:S(2)}, u32[]{:S(2)}) collective-permute-start(bf16[80,256]{1,0:T(8,128)(2,1)} %get-tuple-element.40), channel_id=1, source_target_pairs={{0,48},{16,0},{32,16},{48,32},{1,49},{17,1},{33,17},{49,33},{2,50}... | collective-permute-start | bytes 122888 | tf_op jit(solution)/shard_map/ppermute | solution.py:225
  81.8 14.7 %collective-permute-start.6 = (bf16[80,256]{1,0:T(8,128)(2,1)S(1)}, bf16[80,256]{1,0:T(8,128)(2,1)S(1)}, u32[]{:S(2)}, u32[]{:S(2)}) collective-permute-start(bf16[80,256]{1,0:T(8,128)(2,1)S(1)} %get-tuple-element.41), channel_id=1, source_target_pairs={{0,16},{16,32},{32,48},{48,0},{1,17},{17,33},{33,49},{49,1},{2,18}... | collective-permute-start | bytes 122888 | tf_op jit(solution)/shard_map/ppermute | solution.py:225
  84.0 12.5 %collective-permute-start.7 = (bf16[80,256]{1,0:T(8,128)(2,1)S(1)}, bf16[80,256]{1,0:T(8,128)(2,1)S(1)}, u32[]{:S(2)}, u32[]{:S(2)}) collective-permute-start(bf16[80,256]{1,0:T(8,128)(2,1)S(1)} %get-tuple-element.42), channel_id=1, source_target_pairs={{0,32},{16,48},{32,0},{48,16},{1,33},{17,49},{33,1},{49,17},{2,34}... | collective-permute-start | bytes 122888 | tf_op jit(solution)/shard_map/ppermute | solution.py:225
  91.0 5.5 %collective-permute-start.3 = (bf16[16,256]{1,0:T(8,128)(2,1)S(1)}, bf16[16,256]{1,0:T(8,128)(2,1)S(1)}, u32[]{:S(2)}, u32[]{:S(2)}) collective-permute-start(bf16[16,256]{1,0:T(8,128)(2,1)S(1)} %get-tuple-element.34), channel_id=1, source_target_pairs={{0,16},{16,0},{32,48},{48,32},{1,17},{17,1},{33,49},{49,33},{2,18}... | collective-permute-start | bytes 24584 | tf_op jit(solution)/shard_map/ppermute | solution.py:229
  97.2 12.9 %all-to-all-start.3 = ((bf16[8,16,256]{2,1,0:T(8,128)(2,1)}), bf16[8,16,256]{2,1,0:T(8,128)(2,1)S(1)}, u32[]{:S(2)}, u32[]{:S(2)}) async-start(bf16[8,16,256]{2,1,0:T(8,128)(2,1)} %shard_map.99), calls=%async_computation.3 | async-start | bytes 131072 | tf_op jit(solution)/shard_map/all_to_all | solution.py:296
  101.7 5.5 %collective-permute-start.4 = (bf16[16,256]{1,0:T(8,128)(2,1)S(1)}, bf16[16,256]{1,0:T(8,128)(2,1)S(1)}, u32[]{:S(2)}, u32[]{:S(2)}) collective-permute-start(bf16[16,256]{1,0:T(8,128)(2,1)S(1)} %get-tuple-element.36), channel_id=1, source_target_pairs={{0,48},{16,32},{32,16},{48,0},{1,49},{17,33},{33,17},{49,1},{2,50}... | collective-permute-start | bytes 24584 | tf_op jit(solution)/shard_map/ppermute | solution.py:229
  (1 other events, 0.9 us)
Sparse Core Ops, SparseCore 0:
  10.1 39.8 all-gather.2

commit v5 on v4

--- a/solution.py
+++ b/solution.py
@@ -118,8 +118,9 @@
 
 
 def acts_body(
-    x_ref, s0, s1, s2, s3, wide, at, whole, out_hbm, out, lefts, out_sems
+    x_ref, s0, s1, s2, s3, wide, at, whole, out_hbm, *rest
 ):
+    side_hbm, (out, lefts, sides, out_sems, side_sems) = rest[:NX], rest[NX:]
     blocks = (s0, s1, s2, s3)
     tokens, din = whole.shape
     rank = at.shape[0]
@@ -163,20 +164,19 @@
             )
         out[:, pl.ds(i * STEP, STEP)] = total.astype(BF16)
         send(i * STEP, STEP)
+    down = dot(whole[...], at[...], NT).astype(BF16)
+    for k, s in enumerate(blocks):
+        scaled = s[pl.ds(0, tokens), :]
+        outputs = dot(whole[...], wide[place[k]], NN) + dot(
+            down, s[pl.ds(tokens, rank), :], NN
+        )
+        stat = jnp.sum(scaled.astype(F32) * outputs, axis=0, keepdims=True)
+        sides[k, pl.ds(0, rank), :] = dot(down, scaled, TN).astype(BF16)
+        sides[k, pl.ds(rank, 16), :] = two_rows(stat, stat.shape[1])
+        sends.append(pltpu.make_async_copy(sides.at[k], side_hbm[k], side_sems.at[k]))
+        sends[-1].start()
     for copy in sends:
         copy.wait()
-
-
-def stat_body(x_ref, s0, s1, s2, s3, wide, at, whole, *outs):
-    rank = at.shape[0]
-    tokens = whole.shape[0]
-    down = dot(whole[...], at[...], NT).astype(BF16)
-    for k, (s, out) in enumerate(zip((s0, s1, s2, s3), outs)):
-        scaled = s[pl.ds(0, tokens), :]
-        out[pl.ds(0, rank), :] = dot(down, scaled, TN).astype(BF16)
-        outputs = dot(whole[...], wide[source(x_ref, k)], NN) + dot(down, s[pl.ds(tokens, rank), :], NN)
-        stat = jnp.sum(scaled.astype(F32) * outputs, axis=0, keepdims=True)
-        out[pl.ds(rank, 16), :] = two_rows(stat, stat.shape[1])
 
 
 def meet_body(r0, r1, r2, r3, pay_ref):
@@ -264,25 +264,22 @@
     )
     blocks = [scaled[0]] + [shift(scaled[k], HOPS[k]) for k in range(1, NX)]
     whole = lax.all_to_all(after(many, got), "z", 0, 0, tiled=True).reshape(tokens, din)
-    (part,) = call(
+    part, *sides = call(
         acts_body,
-        [shape((tokens, wider))],
-        2 * tokens * din * width * NX,
+        [shape((tokens, wider))] + [shape((rank + 16, width))] * NX,
+        4 * tokens * din * width * NX,
         spot, *blocks, wide, a_turned, whole,
-        out_specs=[HBM],
+        out_specs=[HBM] * (1 + NX),
         scratch=[
             pltpu.VMEM((tokens, wider), BF16),
             pltpu.VMEM((tokens, NX * rank), F32),
+            pltpu.VMEM((NX, rank + 16, width), BF16),
             pltpu.SemaphoreType.DMA((1 + din // STEP,)),
+            pltpu.SemaphoreType.DMA((NX,)),
         ],
+        limit=16,
     )
     back = lax.all_to_all(part.reshape(NZ, rows, wider), "z", 0, 0, tiled=True)
-    sides = call(
-        stat_body,
-        [shape((rank + 16, width))] * NX,
-        2 * tokens * din * width * NX,
-        after(spot, part), *blocks, wide, a_turned, whole,
-    )
     met = [sides[0]] + [shift(sides[k], NX - HOPS[k]) for k in range(1, NX)]
     summed, keep, send = call(
         sum_body,
@@ -292,8 +289,8 @@
         scratch=[pltpu.VMEM((rows, NX * rank), F32)],
     )
     more = swap(send, 1)
-    (pay,) = call(meet_body, [shape((NY, 16, width))], 0, after(met[0], more), *met[1:])
-    right = lax.all_to_all(pay, "din", 0, 0, tiled=True)
+    (pay,) = call(meet_body, [shape((NY, 16, width))], 0, *met)
+    right = lax.all_to_all(after(pay, send), "din", 0, 0, tiled=True)
     own, send = call(
         pair_body, [shape((8, width), F32), shape((16, width))], 0, keep, more
     )

time: 118 us -> 118 us (level)
  the two profiles are of different devices: /device:TPU:2 before, /device:TPU:8 now
where the time goes in v5:
time: 118 us; the launch traced here: 117 us
  starting transfers between devices  51.6 us (44%)
  blocking collectives  25 us (21%)
  waiting for transfers between devices  16.4 us (14%)
  between operations  14.2 us (12%)
  Pallas kernels  8.62 us (7%)
  local copies, waits for them, and re-layouts  1.6 us (1%)
    all_to_all x1, blocking collectives, local(): got = lax.all_to_all(pay, 'din', 0, 0, tiled=True)  25 us
    ppermute x6, starting transfers between devices, shift(): return lax.ppermute(block, 'x', [(i, (i + hop) % NX) for i in range(NX)])  20.3 us
    all_to_all x1, starting transfers between devices, local(): lax.all_to_all(after(many, got), 'z', 0, 0, tiled=True).reshape(tokens, din)  10.3 us
    ppermute x6, waiting for transfers between devices, shift(): return lax.ppermute(block, 'x', [(i, (i + hop) % NX) for i in range(NX)])  8.64 us
    pallas_call x7, Pallas kernels, call(): pl.pallas_call(body, out_shape=outs, in_specs=specs, out_specs=out_specs...  8.62 us
    all_to_all x1, starting transfers between devices, local(): back = lax.all_to_all(part.reshape(NZ, rows, wider), 'z', 0, 0, tiled=True)  7.21 us
    ppermute x2, starting transfers between devices, swap(): return lax.ppermute(block, 'x', [(i, i ^ mask) for i in range(NX)])  6.96 us
    all_to_all x1, starting transfers between devices, local(): right = lax.all_to_all(after(pay, send), 'din', 0, 0, tiled=True)  6.77 us
  transfers between devices with their start and end apart: 12, of which 7 were waited for; matrix products, arithmetic and copies ran while one was open for 0% of the time, Pallas kernels for 3%

profile of v5, /device:TPU:8, one launch (start us, length us, event | category | flops | bytes accessed | tf_op | source)
XLA Modules:
  0.0 117.5 jit_solution(18226988149757857507)
XLA Ops:
  7.9 2.6 %shard_map.93 = (bf16[8,144,256]{2,1,0:T(8,128)(2,1)}, bf16[8,32,1024]{2,1,0:T(8,128)(2,1)}) custom-call(bf16[1024,256]{1,0:T(8,128)(2,1)} %w_hbm.1, bf16[64,1024]{1,0:T(8,128)(2,1)} %bitcast.8, bf16[64,256]{1,0:T(8,128)(2,1)} %b_ref.1, bf16[128,256]{1,0:T(8,128)(2,1)} %g_hbm.1, bf16[32,1024]{1,0:T(8,128)(2,1)} %acts_hbm.1), custom_call_target="tpu_custom_call" | custom-call | flops 33554432 | bytes 1933312 | tf_op jit(solution)/shard_map/pallas_call | solution.py:37
  10.5 25.0 %all_to_all.20.got_ref = bf16[8,144,256]{2,1,0:T(8,128)(2,1)S(1)} all-to-all(bf16[8,144,256]{2,1,0:T(8,128)(2,1)} %get-tuple-element.25), channel_id=1, replica_groups=mesh['din'=8,'x'=4,'z'=8,'layer'=2] {'din'}, dimensions={0} | all-to-all | bytes 1179648 | tf_op jit(solution)/shard_map/all_to_all | solution.py:258
  35.5 10.3 %all-to-all-start.1 = ((bf16[8,32,1024]{2,1,0:T(8,128)(2,1)}), bf16[8,32,1024]{2,1,0:T(8,128)(2,1)S(1)}, u32[]{:S(2)}, u32[]{:S(2)}) async-start(bf16[8,32,1024]{2,1,0:T(8,128)(2,1)} %get-tuple-element.31), calls=%async_computation.1 | async-start | bytes 1048576 | tf_op jit(solution)/shard_map/all_to_all | solution.py:266
  46.0 3.4 %collective-permute-start = (bf16[320,256]{1,0:T(8,128)(2,1)S(1)}, bf16[320,256]{1,0:T(8,128)(2,1)S(1)}, u32[]{:S(2)}, u32[]{:S(2)}) collective-permute-start(bf16[320,256]{1,0:T(8,128)(2,1)S(1)} %get-tuple-element.27), channel_id=1, source_target_pairs={{0,16},{16,32},{32,48},{48,0},{1,17},{17,33},{33,49},{49,1},{2,18}... | collective-permute-start | bytes 491528 | tf_op jit(solution)/shard_map/ppermute | solution.py:225
  49.4 3.7 %collective-permute-start.1 = (bf16[320,256]{1,0:T(8,128)(2,1)S(1)}, bf16[320,256]{1,0:T(8,128)(2,1)S(1)}, u32[]{:S(2)}, u32[]{:S(2)}) collective-permute-start(bf16[320,256]{1,0:T(8,128)(2,1)S(1)} %get-tuple-element.28), channel_id=1, source_target_pairs={{0,48},{16,0},{32,16},{48,32},{1,49},{17,1},{33,17},{49,33},{2,50}... | collective-permute-start | bytes 491528 | tf_op jit(solution)/shard_map/ppermute | solution.py:225
  53.1 3.7 %collective-permute-start.2 = (bf16[320,256]{1,0:T(8,128)(2,1)S(1)}, bf16[320,256]{1,0:T(8,128)(2,1)S(1)}, u32[]{:S(2)}, u32[]{:S(2)}) collective-permute-start(bf16[320,256]{1,0:T(8,128)(2,1)S(1)} %get-tuple-element.29), channel_id=1, source_target_pairs={{0,32},{16,48},{32,0},{48,16},{1,33},{17,49},{33,1},{49,17},{2,34}... | collective-permute-start | bytes 491528 | tf_op jit(solution)/shard_map/ppermute | solution.py:225
  56.8 0.8 collective-permute-done.1.s2
  57.6 4.2 %collective-permute-done.2.s3 = bf16[320,256]{1,0:T(8,128)(2,1)S(1)} collective-permute-done((bf16[320,256]{1,0:T(8,128)(2,1)S(1)}, bf16[320,256]{1,0:T(8,128)(2,1)S(1)}, u32[]{:S(2)}, u32[]{:S(2)}) %collective-permute-start.2) | collective-permute-done | bytes 163872 | tf_op jit(solution)/shard_map/ppermute | solution.py:225
  61.8 1.6 %copy-done.3 = bf16[4096,256]{1,0:T(8,128)(2,1)S(1)} copy-done((bf16[4096,256]{1,0:T(8,128)(2,1)S(1)}, bf16[4096,256]{1,0:T(8,128)(2,1)}, u32[]{:S(2)}) %copy-start.3) | copy-done | bytes 2097176
  63.4 3.8 %shard_map.95 = (bf16[256,1280]{1,0:T(8,128)(2,1)}, bf16[80,256]{1,0:T(8,128)(2,1)S(1)}, bf16[80,256]{1,0:T(8,128)(2,1)S(1)}, bf16[80,256]{1,0:T(8,128)(2,1)S(1)}, bf16[80,256]{1,0:T(8,128)(2,1)S(1)}) custom-call(s32[1]{0:T(128)} %bitcast.x_ref, bf16[320,256]{1,0:T(8,128)(2,1)S(1)} %get-tuple-element.26.s0, bf16[320,256]{1,0:T(8,128)(2,1)S(1)} %collective-permute-done.s1, ...), custom_call_target="tpu_custom_call" | custom-call | flops 1073741824 | bytes 4227076 | tf_op jit(solution)/shard_map/pallas_call | solution.py:37
  67.2 7.2 %all-to-all-start.2 = ((bf16[8,32,1280]{2,1,0:T(8,128)(2,1)}), bf16[8,32,1280]{2,1,0:T(8,128)(2,1)S(1)}, u32[]{:S(2)}, u32[]{:S(2)}) async-start(bf16[8,32,1280]{2,1,0:T(8,128)(2,1)} %bitcast.5), calls=%async_computation.2 | async-start | bytes 1310720 | tf_op jit(solution)/shard_map/all_to_all | solution.py:282
  74.4 3.4 %collective-permute-start.5 = (bf16[80,256]{1,0:T(8,128)(2,1)S(1)}, bf16[80,256]{1,0:T(8,128)(2,1)S(1)}, u32[]{:S(2)}, u32[]{:S(2)}) collective-permute-start(bf16[80,256]{1,0:T(8,128)(2,1)S(1)} %get-tuple-element.39), channel_id=1, source_target_pairs={{0,48},{16,0},{32,16},{48,32},{1,49},{17,1},{33,17},{49,33},{2,50}... | collective-permute-start | bytes 122888 | tf_op jit(solution)/shard_map/ppermute | solution.py:225
  77.9 2.4 %collective-permute-start.6 = (bf16[80,256]{1,0:T(8,128)(2,1)S(1)}, bf16[80,256]{1,0:T(8,128)(2,1)S(1)}, u32[]{:S(2)}, u32[]{:S(2)}) collective-permute-start(bf16[80,256]{1,0:T(8,128)(2,1)S(1)} %get-tuple-element.40), channel_id=1, source_target_pairs={{0,16},{16,32},{32,48},{48,0},{1,17},{17,33},{33,49},{49,1},{2,18}... | collective-permute-start | bytes 122888 | tf_op jit(solution)/shard_map/ppermute | solution.py:225
  80.3 3.7 %collective-permute-start.7 = (bf16[80,256]{1,0:T(8,128)(2,1)S(1)}, bf16[80,256]{1,0:T(8,128)(2,1)S(1)}, u32[]{:S(2)}, u32[]{:S(2)}) collective-permute-start(bf16[80,256]{1,0:T(8,128)(2,1)S(1)} %get-tuple-element.41), channel_id=1, source_target_pairs={{0,32},{16,48},{32,0},{48,16},{1,33},{17,49},{33,1},{49,17},{2,34}... | collective-permute-start | bytes 122888 | tf_op jit(solution)/shard_map/ppermute | solution.py:225
  84.0 1.0 collective-permute-done.6.r2
  85.0 2.7 %collective-permute-done.7.r3 = bf16[80,256]{1,0:T(8,128)(2,1)S(1)} collective-permute-done((bf16[80,256]{1,0:T(8,128)(2,1)S(1)}, bf16[80,256]{1,0:T(8,128)(2,1)S(1)}, u32[]{:S(2)}, u32[]{:S(2)}) %collective-permute-start.7) | collective-permute-done | bytes 40992 | tf_op jit(solution)/shard_map/ppermute | solution.py:225
  88.3 1.8 %all-to-all-done.2.got_ref = bf16[8,32,1280]{2,1,0:T(8,128)(2,1)S(1)} async-done(((bf16[8,32,1280]{2,1,0:T(8,128)(2,1)}), bf16[8,32,1280]{2,1,0:T(8,128)(2,1)S(1)}, u32[]{:S(2)}, u32[]{:S(2)}) %all-to-all-start.2) | async-done | bytes 655392 | tf_op jit(solution)/shard_map/all_to_all | solution.py:282
  90.1 0.7 shard_map.96
  90.9 6.8 %all-to-all-start.3 = ((bf16[8,16,256]{2,1,0:T(8,128)(2,1)}), bf16[8,16,256]{2,1,0:T(8,128)(2,1)S(1)}, u32[]{:S(2)}, u32[]{:S(2)}) async-start(bf16[8,16,256]{2,1,0:T(8,128)(2,1)} %shard_map.98), calls=%async_computation.3 | async-start | bytes 131072 | tf_op jit(solution)/shard_map/all_to_all | solution.py:293
  97.6 3.1 %collective-permute-start.3 = (bf16[16,256]{1,0:T(8,128)(2,1)S(1)}, bf16[16,256]{1,0:T(8,128)(2,1)S(1)}, u32[]{:S(2)}, u32[]{:S(2)}) collective-permute-start(bf16[16,256]{1,0:T(8,128)(2,1)S(1)} %get-tuple-element.35), channel_id=1, source_target_pairs={{0,16},{16,0},{32,48},{48,32},{1,17},{17,1},{33,49},{49,33},{2,18}... | collective-permute-start | bytes 24584 | tf_op jit(solution)/shard_map/ppermute | solution.py:229
  100.8 2.4 %collective-permute-done.3.got_ref = bf16[16,256]{1,0:T(8,128)(2,1)S(1)} collective-permute-done((bf16[16,256]{1,0:T(8,128)(2,1)S(1)}, bf16[16,256]{1,0:T(8,128)(2,1)S(1)}, u32[]{:S(2)}, u32[]{:S(2)}) %collective-permute-start.3) | collective-permute-done | bytes 8224 | tf_op jit(solution)/shard_map/ppermute | solution.py:229
  103.2 3.8 %collective-permute-start.4 = (bf16[16,256]{1,0:T(8,128)(2,1)S(1)}, bf16[16,256]{1,0:T(8,128)(2,1)S(1)}, u32[]{:S(2)}, u32[]{:S(2)}) collective-permute-start(bf16[16,256]{1,0:T(8,128)(2,1)S(1)} %get-tuple-element.37), channel_id=1, source_target_pairs={{0,48},{16,32},{32,16},{48,0},{1,49},{17,33},{33,17},{49,1},{2,50}... | collective-permute-start | bytes 24584 | tf_op jit(solution)/shard_map/ppermute | solution.py:229
  107.0 2.9 %collective-permute-done.4.more_ref = bf16[16,256]{1,0:T(8,128)(2,1)S(1)} collective-permute-done((bf16[16,256]{1,0:T(8,128)(2,1)S(1)}, bf16[16,256]{1,0:T(8,128)(2,1)S(1)}, u32[]{:S(2)}, u32[]{:S(2)}) %collective-permute-start.4) | collective-permute-done | bytes 8224 | tf_op jit(solution)/shard_map/ppermute | solution.py:229
  109.9 0.7 shard_map.99
  (17 shorter events, 1.5 us)
Async XLA Ops:
  7.2 38.7 %copy-start.1 = (bf16[64,256]{1,0:T(8,128)(2,1)S(1)}, bf16[64,256]{1,0:T(8,128)(2,1)}, u32[]{:S(2)}) copy-start(bf16[64,256]{1,0:T(8,128)(2,1)} %b_ref.1) | copy-start | bytes 98308
  7.2 54.6 %copy-start = (bf16[1024,64]{0,1:T(8,128)(2,1)S(1)}, bf16[1024,64]{0,1:T(8,128)(2,1)}, u32[]{:S(2)}) copy-start(bf16[1024,64]{0,1:T(8,128)(2,1)} %param.9) | copy-start | bytes 393220
  7.2 38.7 %copy-start.2 = (f32[256]{0:T(256)S(1)}, f32[256]{0:T(256)}, u32[]{:S(2)}) copy-start(f32[256]{0:T(256)} %param.11) | copy-start | bytes 3076
  7.2 54.6 %all-gather.3.cloned.1.call-start = ((), (), s32[]{:S(2)}) async-start(), calls=%async_computation.4 | async-start | bytes 2621440 | tf_op jit(solution)/shard_map/all_gather | solution.py:245
  35.5 26.3 %all-to-all-start.1 = ((bf16[8,32,1024]{2,1,0:T(8,128)(2,1)}), bf16[8,32,1024]{2,1,0:T(8,128)(2,1)S(1)}, u32[]{:S(2)}, u32[]{:S(2)}) async-start(bf16[8,32,1024]{2,1,0:T(8,128)(2,1)} %get-tuple-element.31), calls=%async_computation.1 | async-start | bytes 1048576 | tf_op jit(solution)/shard_map/all_to_all | solution.py:266
  46.0 10.8 %collective-permute-start = (bf16[320,256]{1,0:T(8,128)(2,1)S(1)}, bf16[320,256]{1,0:T(8,128)(2,1)S(1)}, u32[]{:S(2)}, u32[]{:S(2)}) collective-permute-start(bf16[320,256]{1,0:T(8,128)(2,1)S(1)} %get-tuple-element.27), channel_id=1, source_target_pairs={{0,16},{16,32},{32,48},{48,0},{1,17},{17,33},{33,49},{49,1},{2,18}... | collective-permute-start | bytes 491528 | tf_op jit(solution)/shard_map/ppermute | solution.py:225
  49.4 8.2 %collective-permute-start.1 = (bf16[320,256]{1,0:T(8,128)(2,1)S(1)}, bf16[320,256]{1,0:T(8,128)(2,1)S(1)}, u32[]{:S(2)}, u32[]{:S(2)}) collective-permute-start(bf16[320,256]{1,0:T(8,128)(2,1)S(1)} %get-tuple-element.28), channel_id=1, source_target_pairs={{0,48},{16,0},{32,16},{48,32},{1,49},{17,1},{33,17},{49,33},{2,50}... | collective-permute-start | bytes 491528 | tf_op jit(solution)/shard_map/ppermute | solution.py:225
  53.1 8.7 %collective-permute-start.2 = (bf16[320,256]{1,0:T(8,128)(2,1)S(1)}, bf16[320,256]{1,0:T(8,128)(2,1)S(1)}, u32[]{:S(2)}, u32[]{:S(2)}) collective-permute-start(bf16[320,256]{1,0:T(8,128)(2,1)S(1)} %get-tuple-element.29), channel_id=1, source_target_pairs={{0,32},{16,48},{32,0},{48,16},{1,33},{17,49},{33,1},{49,17},{2,34}... | collective-permute-start | bytes 491528 | tf_op jit(solution)/shard_map/ppermute | solution.py:225
  61.8 1.6 %copy-start.3 = (bf16[4096,256]{1,0:T(8,128)(2,1)S(1)}, bf16[4096,256]{1,0:T(8,128)(2,1)}, u32[]{:S(2)}) copy-start(bf16[4096,256]{1,0:T(8,128)(2,1)} %all-gather.3.cloned.1.call-done) | copy-start | bytes 6291460
  67.2 22.9 %all-to-all-start.2 = ((bf16[8,32,1280]{2,1,0:T(8,128)(2,1)}), bf16[8,32,1280]{2,1,0:T(8,128)(2,1)S(1)}, u32[]{:S(2)}, u32[]{:S(2)}) async-start(bf16[8,32,1280]{2,1,0:T(8,128)(2,1)} %bitcast.5), calls=%async_computation.2 | async-start | bytes 1310720 | tf_op jit(solution)/shard_map/all_to_all | solution.py:282
  74.4 9.6 %collective-permute-start.5 = (bf16[80,256]{1,0:T(8,128)(2,1)S(1)}, bf16[80,256]{1,0:T(8,128)(2,1)S(1)}, u32[]{:S(2)}, u32[]{:S(2)}) collective-permute-start(bf16[80,256]{1,0:T(8,128)(2,1)S(1)} %get-tuple-element.39), channel_id=1, source_target_pairs={{0,48},{16,0},{32,16},{48,32},{1,49},{17,1},{33,17},{49,33},{2,50}... | collective-permute-start | bytes 122888 | tf_op jit(solution)/shard_map/ppermute | solution.py:225
  77.9 7.1 %collective-permute-start.6 = (bf16[80,256]{1,0:T(8,128)(2,1)S(1)}, bf16[80,256]{1,0:T(8,128)(2,1)S(1)}, u32[]{:S(2)}, u32[]{:S(2)}) collective-permute-start(bf16[80,256]{1,0:T(8,128)(2,1)S(1)} %get-tuple-element.40), channel_id=1, source_target_pairs={{0,16},{16,32},{32,48},{48,0},{1,17},{17,33},{33,49},{49,1},{2,18}... | collective-permute-start | bytes 122888 | tf_op jit(solution)/shard_map/ppermute | solution.py:225
  80.3 7.4 %collective-permute-start.7 = (bf16[80,256]{1,0:T(8,128)(2,1)S(1)}, bf16[80,256]{1,0:T(8,128)(2,1)S(1)}, u32[]{:S(2)}, u32[]{:S(2)}) collective-permute-start(bf16[80,256]{1,0:T(8,128)(2,1)S(1)} %get-tuple-element.41), channel_id=1, source_target_pairs={{0,32},{16,48},{32,0},{48,16},{1,33},{17,49},{33,1},{49,17},{2,34}... | collective-permute-start | bytes 122888 | tf_op jit(solution)/shard_map/ppermute | solution.py:225
  90.9 19.1 %all-to-all-start.3 = ((bf16[8,16,256]{2,1,0:T(8,128)(2,1)}), bf16[8,16,256]{2,1,0:T(8,128)(2,1)S(1)}, u32[]{:S(2)}, u32[]{:S(2)}) async-start(bf16[8,16,256]{2,1,0:T(8,128)(2,1)} %shard_map.98), calls=%async_computation.3 | async-start | bytes 131072 | tf_op jit(solution)/shard_map/all_to_all | solution.py:293
  97.6 5.5 %collective-permute-start.3 = (bf16[16,256]{1,0:T(8,128)(2,1)S(1)}, bf16[16,256]{1,0:T(8,128)(2,1)S(1)}, u32[]{:S(2)}, u32[]{:S(2)}) collective-permute-start(bf16[16,256]{1,0:T(8,128)(2,1)S(1)} %get-tuple-element.35), channel_id=1, source_target_pairs={{0,16},{16,0},{32,48},{48,32},{1,17},{17,1},{33,49},{49,33},{2,18}... | collective-permute-start | bytes 24584 | tf_op jit(solution)/shard_map/ppermute | solution.py:229
  103.2 6.7 %collective-permute-start.4 = (bf16[16,256]{1,0:T(8,128)(2,1)S(1)}, bf16[16,256]{1,0:T(8,128)(2,1)S(1)}, u32[]{:S(2)}, u32[]{:S(2)}) collective-permute-start(bf16[16,256]{1,0:T(8,128)(2,1)S(1)} %get-tuple-element.37), channel_id=1, source_target_pairs={{0,48},{16,32},{32,16},{48,0},{1,49},{17,33},{33,17},{49,1},{2,50}... | collective-permute-start | bytes 24584 | tf_op jit(solution)/shard_map/ppermute | solution.py:229
Sparse Core Ops, SparseCore 0:
  10.1 41.8 all-gather.2

commit v6 on v5

--- a/solution.py
+++ b/solution.py
@@ -111,6 +111,11 @@
                 got_ref[block * half + h, pl.ds(0, tokens), :].astype(F32) * scale
             ).astype(BF16)
         out[pl.ds(half * tokens, b_ref.shape[0]), :] = b_ref[...]
+
+
+def bring_body(wide_hbm, out_ref, sems):
+    for copy in fetch([(wide_hbm.at[k], out_ref.at[k]) for k in range(NX)], sems):
+        copy.wait()
 
 
 def source(x_ref, k):
@@ -264,6 +269,15 @@
     )
     blocks = [scaled[0]] + [shift(scaled[k], HOPS[k]) for k in range(1, NX)]
     whole = lax.all_to_all(after(many, got), "z", 0, 0, tiled=True).reshape(tokens, din)
+    (wide,) = call(
+        bring_body,
+        [shape(wide.shape)],
+        0,
+        wide,
+        far=(0,),
+        scratch=[pltpu.SemaphoreType.DMA((NX,))],
+        limit=4,
+    )
     part, *sides = call(
         acts_body,
         [shape((tokens, wider))] + [shape((rank + 16, width))] * NX,

time: 118 us -> 117 us (level)
  the two profiles are of different devices: /device:TPU:8 before, /device:TPU:14 now
where the time goes in v6:
time: 117 us
  starting transfers between devices  46.6 us (40%)
  blocking collectives  25 us (21%)
  waiting for transfers between devices  19 us (16%)
  between operations  14.2 us (12%)
  Pallas kernels  9.51 us (8%)
  local copies, waits for them, and re-layouts  2.21 us (2%)
    all_to_all x1, blocking collectives, local(): got = lax.all_to_all(pay, 'din', 0, 0, tiled=True)  25 us
    ppermute x6, starting transfers between devices, shift(): return lax.ppermute(block, 'x', [(i, (i + hop) % NX) for i in range(NX)])  18.3 us
    all_to_all x1, starting transfers between devices, local(): lax.all_to_all(after(many, got), 'z', 0, 0, tiled=True).reshape(tokens, din)  10.3 us
    pallas_call x8, Pallas kernels, call(): pl.pallas_call(body, out_shape=outs, in_specs=specs, out_specs=out_specs...  9.51 us
    ppermute x6, waiting for transfers between devices, shift(): return lax.ppermute(block, 'x', [(i, (i + hop) % NX) for i in range(NX)])  9.05 us
    ppermute x2, waiting for transfers between devices, swap(): return lax.ppermute(block, 'x', [(i, i ^ mask) for i in range(NX)])  8.44 us
    all_to_all x1, starting transfers between devices, local(): back = lax.all_to_all(part.reshape(NZ, rows, wider), 'z', 0, 0, tiled=True)  7.2 us
    all_to_all x1, starting transfers between devices, local(): right = lax.all_to_all(after(pay, send), 'din', 0, 0, tiled=True)  6.97 us
  transfers between devices with their start and end apart: 12, of which 6 were waited for; matrix products, arithmetic and copies ran while one was open for 0% of the time, Pallas kernels for 4%

profile of v6, /device:TPU:14, one launch (start us, length us, event | category | flops | bytes accessed | tf_op | source)
XLA Modules:
  0.0 116.5 jit_solution(8020618226357859376)
XLA Ops:
  7.9 2.6 %shard_map.93 = (bf16[8,144,256]{2,1,0:T(8,128)(2,1)}, bf16[8,32,1024]{2,1,0:T(8,128)(2,1)}) custom-call(bf16[1024,256]{1,0:T(8,128)(2,1)} %w_hbm.1, bf16[64,1024]{1,0:T(8,128)(2,1)} %bitcast.9, bf16[64,256]{1,0:T(8,128)(2,1)} %b_ref.1, bf16[128,256]{1,0:T(8,128)(2,1)} %g_hbm.1, bf16[32,1024]{1,0:T(8,128)(2,1)} %acts_hbm.1), custom_call_target="tpu_custom_call" | custom-call | flops 33554432 | bytes 1933312 | tf_op jit(solution)/shard_map/pallas_call | solution.py:37
  10.5 25.0 %all_to_all.20.got_ref = bf16[8,144,256]{2,1,0:T(8,128)(2,1)S(1)} all-to-all(bf16[8,144,256]{2,1,0:T(8,128)(2,1)} %get-tuple-element.25), channel_id=1, replica_groups=mesh['din'=8,'x'=4,'z'=8,'layer'=2] {'din'}, dimensions={0} | all-to-all | bytes 1179648 | tf_op jit(solution)/shard_map/all_to_all | solution.py:263
  35.5 10.3 %all-to-all-start.1 = ((bf16[8,32,1024]{2,1,0:T(8,128)(2,1)}), bf16[8,32,1024]{2,1,0:T(8,128)(2,1)S(1)}, u32[]{:S(2)}, u32[]{:S(2)}) async-start(bf16[8,32,1024]{2,1,0:T(8,128)(2,1)} %get-tuple-element.31), calls=%async_computation.1 | async-start | bytes 1048576 | tf_op jit(solution)/shard_map/all_to_all | solution.py:271
  45.8 0.9 shard_map.94
  46.7 2.4 %collective-permute-start = (bf16[320,256]{1,0:T(8,128)(2,1)}, bf16[320,256]{1,0:T(8,128)(2,1)S(1)}, u32[]{:S(2)}, u32[]{:S(2)}) collective-permute-start(bf16[320,256]{1,0:T(8,128)(2,1)} %get-tuple-element.27), channel_id=1, source_target_pairs={{0,16},{16,32},{32,48},{48,0},{1,17},{17,33},{33,49},{49,1},{2,18}... | collective-permute-start | bytes 491528 | tf_op jit(solution)/shard_map/ppermute | solution.py:230
  49.1 3.5 %collective-permute-start.1 = (bf16[320,256]{1,0:T(8,128)(2,1)}, bf16[320,256]{1,0:T(8,128)(2,1)S(1)}, u32[]{:S(2)}, u32[]{:S(2)}) collective-permute-start(bf16[320,256]{1,0:T(8,128)(2,1)} %get-tuple-element.28), channel_id=1, source_target_pairs={{0,48},{16,0},{32,16},{48,32},{1,49},{17,1},{33,17},{49,33},{2,50}... | collective-permute-start | bytes 491528 | tf_op jit(solution)/shard_map/ppermute | solution.py:230
  52.5 3.3 %collective-permute-start.2 = (bf16[320,256]{1,0:T(8,128)(2,1)}, bf16[320,256]{1,0:T(8,128)(2,1)S(1)}, u32[]{:S(2)}, u32[]{:S(2)}) collective-permute-start(bf16[320,256]{1,0:T(8,128)(2,1)} %get-tuple-element.29), channel_id=1, source_target_pairs={{0,32},{16,48},{32,0},{48,16},{1,33},{17,49},{33,1},{49,17},{2,34}... | collective-permute-start | bytes 491528 | tf_op jit(solution)/shard_map/ppermute | solution.py:230
  55.9 1.6 %copy-done = bf16[4096,256]{1,0:T(8,128)(2,1)S(1)} copy-done((bf16[4096,256]{1,0:T(8,128)(2,1)S(1)}, bf16[4096,256]{1,0:T(8,128)(2,1)}, u32[]{:S(2)}) %copy-start) | copy-done | bytes 2097176
  57.7 0.9 collective-permute-done.1.s2
  58.5 2.9 %collective-permute-done.2.s3 = bf16[320,256]{1,0:T(8,128)(2,1)S(1)} collective-permute-done((bf16[320,256]{1,0:T(8,128)(2,1)}, bf16[320,256]{1,0:T(8,128)(2,1)S(1)}, u32[]{:S(2)}, u32[]{:S(2)}) %collective-permute-start.2) | collective-permute-done | bytes 163872 | tf_op jit(solution)/shard_map/ppermute | solution.py:230
  61.5 3.8 %shard_map.96 = (bf16[256,1280]{1,0:T(8,128)(2,1)}, bf16[80,256]{1,0:T(8,128)(2,1)S(1)}, bf16[80,256]{1,0:T(8,128)(2,1)S(1)}, bf16[80,256]{1,0:T(8,128)(2,1)S(1)}, bf16[80,256]{1,0:T(8,128)(2,1)S(1)}) custom-call(s32[1]{0:T(128)} %bitcast.x_ref, bf16[320,256]{1,0:T(8,128)(2,1)S(1)} %get-tuple-element.26.s0, bf16[320,256]{1,0:T(8,128)(2,1)S(1)} %collective-permute-done.s1, ...), custom_call_target="tpu_custom_call" | custom-call | flops 1073741824 | bytes 4227076 | tf_op jit(solution)/shard_map/pallas_call | solution.py:37
  65.9 7.2 %all-to-all-start.2 = ((bf16[8,32,1280]{2,1,0:T(8,128)(2,1)}), bf16[8,32,1280]{2,1,0:T(8,128)(2,1)S(1)}, u32[]{:S(2)}, u32[]{:S(2)}) async-start(bf16[8,32,1280]{2,1,0:T(8,128)(2,1)} %bitcast.5), calls=%async_computation.2 | async-start | bytes 1310720 | tf_op jit(solution)/shard_map/all_to_all | solution.py:296
  73.1 2.7 %collective-permute-start.5 = (bf16[80,256]{1,0:T(8,128)(2,1)}, bf16[80,256]{1,0:T(8,128)(2,1)S(1)}, u32[]{:S(2)}, u32[]{:S(2)}) collective-permute-start(bf16[80,256]{1,0:T(8,128)(2,1)} %copy-done.4), channel_id=1, source_target_pairs={{0,48},{16,0},{32,16},{48,32},{1,49},{17,1},{33,17},{49,33},{2,50}... | collective-permute-start | bytes 122888 | tf_op jit(solution)/shard_map/ppermute | solution.py:230
  75.9 4.3 %collective-permute-start.6 = (bf16[80,256]{1,0:T(8,128)(2,1)S(1)}, bf16[80,256]{1,0:T(8,128)(2,1)S(1)}, u32[]{:S(2)}, u32[]{:S(2)}) collective-permute-start(bf16[80,256]{1,0:T(8,128)(2,1)S(1)} %get-tuple-element.40), channel_id=1, source_target_pairs={{0,16},{16,32},{32,48},{48,0},{1,17},{17,33},{33,49},{49,1},{2,18}... | collective-permute-start | bytes 122888 | tf_op jit(solution)/shard_map/ppermute | solution.py:230
  80.2 2.1 %collective-permute-start.7 = (bf16[80,256]{1,0:T(8,128)(2,1)S(1)}, bf16[80,256]{1,0:T(8,128)(2,1)S(1)}, u32[]{:S(2)}, u32[]{:S(2)}) collective-permute-start(bf16[80,256]{1,0:T(8,128)(2,1)S(1)} %get-tuple-element.41), channel_id=1, source_target_pairs={{0,32},{16,48},{32,0},{48,16},{1,33},{17,49},{33,1},{49,17},{2,34}... | collective-permute-start | bytes 122888 | tf_op jit(solution)/shard_map/ppermute | solution.py:230
  82.3 5.3 %collective-permute-done.7.r3 = bf16[80,256]{1,0:T(8,128)(2,1)S(1)} collective-permute-done((bf16[80,256]{1,0:T(8,128)(2,1)S(1)}, bf16[80,256]{1,0:T(8,128)(2,1)S(1)}, u32[]{:S(2)}, u32[]{:S(2)}) %collective-permute-start.7) | collective-permute-done | bytes 40992 | tf_op jit(solution)/shard_map/ppermute | solution.py:230
  88.2 0.8 all-to-all-done.2.got_ref
  89.0 0.7 shard_map.97
  89.8 7.0 %all-to-all-start.3 = ((bf16[8,16,256]{2,1,0:T(8,128)(2,1)}), bf16[8,16,256]{2,1,0:T(8,128)(2,1)S(1)}, u32[]{:S(2)}, u32[]{:S(2)}) async-start(bf16[8,16,256]{2,1,0:T(8,128)(2,1)} %shard_map.99), calls=%async_computation.3 | async-start | bytes 131072 | tf_op jit(solution)/shard_map/all_to_all | solution.py:307
  96.7 1.9 %collective-permute-start.3 = (bf16[16,256]{1,0:T(8,128)(2,1)S(1)}, bf16[16,256]{1,0:T(8,128)(2,1)S(1)}, u32[]{:S(2)}, u32[]{:S(2)}) collective-permute-start(bf16[16,256]{1,0:T(8,128)(2,1)S(1)} %get-tuple-element.35), channel_id=1, source_target_pairs={{0,16},{16,0},{32,48},{48,32},{1,17},{17,1},{33,49},{49,33},{2,18}... | collective-permute-start | bytes 24584 | tf_op jit(solution)/shard_map/ppermute | solution.py:234
  98.7 3.6 %collective-permute-done.3.got_ref = bf16[16,256]{1,0:T(8,128)(2,1)S(1)} collective-permute-done((bf16[16,256]{1,0:T(8,128)(2,1)S(1)}, bf16[16,256]{1,0:T(8,128)(2,1)S(1)}, u32[]{:S(2)}, u32[]{:S(2)}) %collective-permute-start.3) | collective-permute-done | bytes 8224 | tf_op jit(solution)/shard_map/ppermute | solution.py:234
  102.3 1.9 %collective-permute-start.4 = (bf16[16,256]{1,0:T(8,128)(2,1)S(1)}, bf16[16,256]{1,0:T(8,128)(2,1)S(1)}, u32[]{:S(2)}, u32[]{:S(2)}) collective-permute-start(bf16[16,256]{1,0:T(8,128)(2,1)S(1)} %get-tuple-element.37), channel_id=1, source_target_pairs={{0,48},{16,32},{32,16},{48,0},{1,49},{17,33},{33,17},{49,1},{2,50}... | collective-permute-start | bytes 24584 | tf_op jit(solution)/shard_map/ppermute | solution.py:234
  104.2 4.8 %collective-permute-done.4.more_ref = bf16[16,256]{1,0:T(8,128)(2,1)S(1)} collective-permute-done((bf16[16,256]{1,0:T(8,128)(2,1)S(1)}, bf16[16,256]{1,0:T(8,128)(2,1)S(1)}, u32[]{:S(2)}, u32[]{:S(2)}) %collective-permute-start.4) | collective-permute-done | bytes 8224 | tf_op jit(solution)/shard_map/ppermute | solution.py:234
  109.0 0.7 shard_map.100
  (20 shorter events, 2.2 us)
Async XLA Ops:
  7.2 38.7 %copy-start.2 = (bf16[64,256]{1,0:T(8,128)(2,1)S(1)}, bf16[64,256]{1,0:T(8,128)(2,1)}, u32[]{:S(2)}) copy-start(bf16[64,256]{1,0:T(8,128)(2,1)} %b_ref.1) | copy-start | bytes 98308
  7.2 38.7 %copy-start.3 = (f32[256]{0:T(256)S(1)}, f32[256]{0:T(256)}, u32[]{:S(2)}) copy-start(f32[256]{0:T(256)} %param.11) | copy-start | bytes 3076
  7.2 48.7 %all-gather.3.cloned.1.call-start = ((), (), s32[]{:S(2)}) async-start(), calls=%async_computation.4 | async-start | bytes 2621440 | tf_op jit(solution)/shard_map/all_gather | solution.py:250
  35.5 26.0 %all-to-all-start.1 = ((bf16[8,32,1024]{2,1,0:T(8,128)(2,1)}), bf16[8,32,1024]{2,1,0:T(8,128)(2,1)S(1)}, u32[]{:S(2)}, u32[]{:S(2)}) async-start(bf16[8,32,1024]{2,1,0:T(8,128)(2,1)} %get-tuple-element.31), calls=%async_computation.1 | async-start | bytes 1048576 | tf_op jit(solution)/shard_map/all_to_all | solution.py:271
  46.7 11.0 %collective-permute-start = (bf16[320,256]{1,0:T(8,128)(2,1)}, bf16[320,256]{1,0:T(8,128)(2,1)S(1)}, u32[]{:S(2)}, u32[]{:S(2)}) collective-permute-start(bf16[320,256]{1,0:T(8,128)(2,1)} %get-tuple-element.27), channel_id=1, source_target_pairs={{0,16},{16,32},{32,48},{48,0},{1,17},{17,33},{33,49},{49,1},{2,18}... | collective-permute-start | bytes 491528 | tf_op jit(solution)/shard_map/ppermute | solution.py:230
  49.1 9.5 %collective-permute-start.1 = (bf16[320,256]{1,0:T(8,128)(2,1)}, bf16[320,256]{1,0:T(8,128)(2,1)S(1)}, u32[]{:S(2)}, u32[]{:S(2)}) collective-permute-start(bf16[320,256]{1,0:T(8,128)(2,1)} %get-tuple-element.28), channel_id=1, source_target_pairs={{0,48},{16,0},{32,16},{48,32},{1,49},{17,1},{33,17},{49,33},{2,50}... | collective-permute-start | bytes 491528 | tf_op jit(solution)/shard_map/ppermute | solution.py:230
  52.5 8.9 %collective-permute-start.2 = (bf16[320,256]{1,0:T(8,128)(2,1)}, bf16[320,256]{1,0:T(8,128)(2,1)S(1)}, u32[]{:S(2)}, u32[]{:S(2)}) collective-permute-start(bf16[320,256]{1,0:T(8,128)(2,1)} %get-tuple-element.29), channel_id=1, source_target_pairs={{0,32},{16,48},{32,0},{48,16},{1,33},{17,49},{33,1},{49,17},{2,34}... | collective-permute-start | bytes 491528 | tf_op jit(solution)/shard_map/ppermute | solution.py:230
  55.9 1.6 %copy-start = (bf16[4096,256]{1,0:T(8,128)(2,1)S(1)}, bf16[4096,256]{1,0:T(8,128)(2,1)}, u32[]{:S(2)}) copy-start(bf16[4096,256]{1,0:T(8,128)(2,1)} %all-gather.3.cloned.1.call-done) | copy-start | bytes 6291460
  57.5 4.0 %copy-start.1 = (bf16[1024,64]{0,1:T(8,128)(2,1)S(1)}, bf16[1024,64]{0,1:T(8,128)(2,1)}, u32[]{:S(2)}) copy-start(bf16[1024,64]{0,1:T(8,128)(2,1)} %param.9) | copy-start | bytes 393220
  65.3 0.6 copy-start.4
  65.9 23.1 %all-to-all-start.2 = ((bf16[8,32,1280]{2,1,0:T(8,128)(2,1)}), bf16[8,32,1280]{2,1,0:T(8,128)(2,1)S(1)}, u32[]{:S(2)}, u32[]{:S(2)}) async-start(bf16[8,32,1280]{2,1,0:T(8,128)(2,1)} %bitcast.5), calls=%async_computation.2 | async-start | bytes 1310720 | tf_op jit(solution)/shard_map/all_to_all | solution.py:296
  73.1 9.2 %collective-permute-start.5 = (bf16[80,256]{1,0:T(8,128)(2,1)}, bf16[80,256]{1,0:T(8,128)(2,1)S(1)}, u32[]{:S(2)}, u32[]{:S(2)}) collective-permute-start(bf16[80,256]{1,0:T(8,128)(2,1)} %copy-done.4), channel_id=1, source_target_pairs={{0,48},{16,0},{32,16},{48,32},{1,49},{17,1},{33,17},{49,33},{2,50}... | collective-permute-start | bytes 122888 | tf_op jit(solution)/shard_map/ppermute | solution.py:230
  75.9 6.5 %collective-permute-start.6 = (bf16[80,256]{1,0:T(8,128)(2,1)S(1)}, bf16[80,256]{1,0:T(8,128)(2,1)S(1)}, u32[]{:S(2)}, u32[]{:S(2)}) collective-permute-start(bf16[80,256]{1,0:T(8,128)(2,1)S(1)} %get-tuple-element.40), channel_id=1, source_target_pairs={{0,16},{16,32},{32,48},{48,0},{1,17},{17,33},{33,49},{49,1},{2,18}... | collective-permute-start | bytes 122888 | tf_op jit(solution)/shard_map/ppermute | solution.py:230
  80.2 7.4 %collective-permute-start.7 = (bf16[80,256]{1,0:T(8,128)(2,1)S(1)}, bf16[80,256]{1,0:T(8,128)(2,1)S(1)}, u32[]{:S(2)}, u32[]{:S(2)}) collective-permute-start(bf16[80,256]{1,0:T(8,128)(2,1)S(1)} %get-tuple-element.41), channel_id=1, source_target_pairs={{0,32},{16,48},{32,0},{48,16},{1,33},{17,49},{33,1},{49,17},{2,34}... | collective-permute-start | bytes 122888 | tf_op jit(solution)/shard_map/ppermute | solution.py:230
  89.8 19.3 %all-to-all-start.3 = ((bf16[8,16,256]{2,1,0:T(8,128)(2,1)}), bf16[8,16,256]{2,1,0:T(8,128)(2,1)S(1)}, u32[]{:S(2)}, u32[]{:S(2)}) async-start(bf16[8,16,256]{2,1,0:T(8,128)(2,1)} %shard_map.99), calls=%async_computation.3 | async-start | bytes 131072 | tf_op jit(solution)/shard_map/all_to_all | solution.py:307
  96.7 5.5 %collective-permute-start.3 = (bf16[16,256]{1,0:T(8,128)(2,1)S(1)}, bf16[16,256]{1,0:T(8,128)(2,1)S(1)}, u32[]{:S(2)}, u32[]{:S(2)}) collective-permute-start(bf16[16,256]{1,0:T(8,128)(2,1)S(1)} %get-tuple-element.35), channel_id=1, source_target_pairs={{0,16},{16,0},{32,48},{48,32},{1,17},{17,1},{33,49},{49,33},{2,18}... | collective-permute-start | bytes 24584 | tf_op jit(solution)/shard_map/ppermute | solution.py:234
  102.3 6.7 %collective-permute-start.4 = (bf16[16,256]{1,0:T(8,128)(2,1)S(1)}, bf16[16,256]{1,0:T(8,128)(2,1)S(1)}, u32[]{:S(2)}, u32[]{:S(2)}) collective-permute-start(bf16[16,256]{1,0:T(8,128)(2,1)S(1)} %get-tuple-element.37), channel_id=1, source_target_pairs={{0,48},{16,32},{32,16},{48,0},{1,49},{17,33},{33,17},{49,1},{2,50}... | collective-permute-start | bytes 24584 | tf_op jit(solution)/shard_map/ppermute | solution.py:234
Sparse Core Ops, SparseCore 0:
  10.1 39.1 all-gather.2

commit v7 on v6

--- a/solution.py
+++ b/solution.py
@@ -273,7 +273,7 @@
         bring_body,
         [shape(wide.shape)],
         0,
-        wide,
+        after(wide, blocks[1]),
         far=(0,),
         scratch=[pltpu.SemaphoreType.DMA((NX,))],
         limit=4,

time: 117 us -> 117 us (level)
  no operation moved by 1% of the time
where the time goes in v7:
time: 117 us; the launch traced here: 116 us
  starting transfers between devices  46.7 us (40%)
  blocking collectives  25 us (21%)
  waiting for transfers between devices  19 us (16%)
  between operations  14.2 us (12%)
  Pallas kernels  9.45 us (8%)
  local copies, waits for them, and re-layouts  2.21 us (2%)
    all_to_all x1, blocking collectives, local(): got = lax.all_to_all(pay, 'din', 0, 0, tiled=True)  25 us
    ppermute x6, starting transfers between devices, shift(): return lax.ppermute(block, 'x', [(i, (i + hop) % NX) for i in range(NX)])  18.3 us
    all_to_all x1, starting transfers between devices, local(): lax.all_to_all(after(many, got), 'z', 0, 0, tiled=True).reshape(tokens, din)  10.3 us
    pallas_call x8, Pallas kernels, call(): pl.pallas_call(body, out_shape=outs, in_specs=specs, out_specs=out_specs...  9.45 us
    ppermute x6, waiting for transfers between devices, shift(): return lax.ppermute(block, 'x', [(i, (i + hop) % NX) for i in range(NX)])  9.05 us
    ppermute x2, waiting for transfers between devices, swap(): return lax.ppermute(block, 'x', [(i, i ^ mask) for i in range(NX)])  8.4 us
    all_to_all x1, starting transfers between devices, local(): back = lax.all_to_all(part.reshape(NZ, rows, wider), 'z', 0, 0, tiled=True)  7.2 us
    all_to_all x1, starting transfers between devices, local(): right = lax.all_to_all(after(pay, send), 'din', 0, 0, tiled=True)  6.97 us
  transfers between devices with their start and end apart: 12, of which 6 were waited for; matrix products, arithmetic and copies ran while one was open for 0% of the time, Pallas kernels for 4%

profile of v7, /device:TPU:14, one launch (start us, length us, event | category | flops | bytes accessed | tf_op | source)
XLA Modules:
  0.0 116.5 jit_solution(17001783495736516847)
XLA Ops:
  7.9 2.6 %shard_map.93 = (bf16[8,144,256]{2,1,0:T(8,128)(2,1)}, bf16[8,32,1024]{2,1,0:T(8,128)(2,1)}) custom-call(bf16[1024,256]{1,0:T(8,128)(2,1)} %w_hbm.1, bf16[64,1024]{1,0:T(8,128)(2,1)} %bitcast.9, bf16[64,256]{1,0:T(8,128)(2,1)} %b_ref.1, bf16[128,256]{1,0:T(8,128)(2,1)} %g_hbm.1, bf16[32,1024]{1,0:T(8,128)(2,1)} %acts_hbm.1), custom_call_target="tpu_custom_call" | custom-call | flops 33554432 | bytes 1933312 | tf_op jit(solution)/shard_map/pallas_call | solution.py:37
  10.5 25.0 %all_to_all.20.got_ref = bf16[8,144,256]{2,1,0:T(8,128)(2,1)S(1)} all-to-all(bf16[8,144,256]{2,1,0:T(8,128)(2,1)} %get-tuple-element.26), channel_id=1, replica_groups=mesh['din'=8,'x'=4,'z'=8,'layer'=2] {'din'}, dimensions={0} | all-to-all | bytes 1179648 | tf_op jit(solution)/shard_map/all_to_all | solution.py:263
  35.5 10.3 %all-to-all-start.1 = ((bf16[8,32,1024]{2,1,0:T(8,128)(2,1)}), bf16[8,32,1024]{2,1,0:T(8,128)(2,1)S(1)}, u32[]{:S(2)}, u32[]{:S(2)}) async-start(bf16[8,32,1024]{2,1,0:T(8,128)(2,1)} %get-tuple-element.33), calls=%async_computation.1 | async-start | bytes 1048576 | tf_op jit(solution)/shard_map/all_to_all | solution.py:271
  45.8 0.8 shard_map.94
  46.6 2.4 %collective-permute-start = (bf16[320,256]{1,0:T(8,128)(2,1)S(1)}, bf16[320,256]{1,0:T(8,128)(2,1)S(1)}, u32[]{:S(2)}, u32[]{:S(2)}) collective-permute-start(bf16[320,256]{1,0:T(8,128)(2,1)S(1)} %get-tuple-element.28), channel_id=1, source_target_pairs={{0,16},{16,32},{32,48},{48,0},{1,17},{17,33},{33,49},{49,1},{2,18}... | collective-permute-start | bytes 491528 | tf_op jit(solution)/shard_map/ppermute | solution.py:230
  49.0 3.5 %collective-permute-start.1 = (bf16[320,256]{1,0:T(8,128)(2,1)}, bf16[320,256]{1,0:T(8,128)(2,1)S(1)}, u32[]{:S(2)}, u32[]{:S(2)}) collective-permute-start(bf16[320,256]{1,0:T(8,128)(2,1)} %get-tuple-element.29), channel_id=1, source_target_pairs={{0,48},{16,0},{32,16},{48,32},{1,49},{17,1},{33,17},{49,33},{2,50}... | collective-permute-start | bytes 491528 | tf_op jit(solution)/shard_map/ppermute | solution.py:230
  52.5 3.3 %collective-permute-start.2 = (bf16[320,256]{1,0:T(8,128)(2,1)}, bf16[320,256]{1,0:T(8,128)(2,1)S(1)}, u32[]{:S(2)}, u32[]{:S(2)}) collective-permute-start(bf16[320,256]{1,0:T(8,128)(2,1)} %get-tuple-element.30), channel_id=1, source_target_pairs={{0,32},{16,48},{32,0},{48,16},{1,33},{17,49},{33,1},{49,17},{2,34}... | collective-permute-start | bytes 491528 | tf_op jit(solution)/shard_map/ppermute | solution.py:230
  55.8 1.6 %copy-done = bf16[4096,256]{1,0:T(8,128)(2,1)S(1)} copy-done((bf16[4096,256]{1,0:T(8,128)(2,1)S(1)}, bf16[4096,256]{1,0:T(8,128)(2,1)}, u32[]{:S(2)}) %copy-start) | copy-done | bytes 2097176
  57.6 0.9 collective-permute-done.1.s2
  58.5 2.9 %collective-permute-done.2.s3 = bf16[320,256]{1,0:T(8,128)(2,1)S(1)} collective-permute-done((bf16[320,256]{1,0:T(8,128)(2,1)}, bf16[320,256]{1,0:T(8,128)(2,1)S(1)}, u32[]{:S(2)}, u32[]{:S(2)}) %collective-permute-start.2) | collective-permute-done | bytes 163872 | tf_op jit(solution)/shard_map/ppermute | solution.py:230
  61.4 3.8 %shard_map.96 = (bf16[256,1280]{1,0:T(8,128)(2,1)}, bf16[80,256]{1,0:T(8,128)(2,1)S(1)}, bf16[80,256]{1,0:T(8,128)(2,1)S(1)}, bf16[80,256]{1,0:T(8,128)(2,1)S(1)}, bf16[80,256]{1,0:T(8,128)(2,1)S(1)}) custom-call(s32[1]{0:T(128)} %bitcast.x_ref, bf16[320,256]{1,0:T(8,128)(2,1)S(1)} %get-tuple-element.27.s0, bf16[320,256]{1,0:T(8,128)(2,1)S(1)} %collective-permute-done.s1, ...), custom_call_target="tpu_custom_call" | custom-call | flops 1073741824 | bytes 4227076 | tf_op jit(solution)/shard_map/pallas_call | solution.py:37
  65.9 7.2 %all-to-all-start.2 = ((bf16[8,32,1280]{2,1,0:T(8,128)(2,1)}), bf16[8,32,1280]{2,1,0:T(8,128)(2,1)S(1)}, u32[]{:S(2)}, u32[]{:S(2)}) async-start(bf16[8,32,1280]{2,1,0:T(8,128)(2,1)} %bitcast.5), calls=%async_computation.2 | async-start | bytes 1310720 | tf_op jit(solution)/shard_map/all_to_all | solution.py:296
  73.1 2.7 %collective-permute-start.5 = (bf16[80,256]{1,0:T(8,128)(2,1)}, bf16[80,256]{1,0:T(8,128)(2,1)S(1)}, u32[]{:S(2)}, u32[]{:S(2)}) collective-permute-start(bf16[80,256]{1,0:T(8,128)(2,1)} %copy-done.4), channel_id=1, source_target_pairs={{0,48},{16,0},{32,16},{48,32},{1,49},{17,1},{33,17},{49,33},{2,50}... | collective-permute-start | bytes 122888 | tf_op jit(solution)/shard_map/ppermute | solution.py:230
  75.8 4.3 %collective-permute-start.6 = (bf16[80,256]{1,0:T(8,128)(2,1)S(1)}, bf16[80,256]{1,0:T(8,128)(2,1)S(1)}, u32[]{:S(2)}, u32[]{:S(2)}) collective-permute-start(bf16[80,256]{1,0:T(8,128)(2,1)S(1)} %get-tuple-element.42), channel_id=1, source_target_pairs={{0,16},{16,32},{32,48},{48,0},{1,17},{17,33},{33,49},{49,1},{2,18}... | collective-permute-start | bytes 122888 | tf_op jit(solution)/shard_map/ppermute | solution.py:230
  80.1 2.1 %collective-permute-start.7 = (bf16[80,256]{1,0:T(8,128)(2,1)S(1)}, bf16[80,256]{1,0:T(8,128)(2,1)S(1)}, u32[]{:S(2)}, u32[]{:S(2)}) collective-permute-start(bf16[80,256]{1,0:T(8,128)(2,1)S(1)} %get-tuple-element.43), channel_id=1, source_target_pairs={{0,32},{16,48},{32,0},{48,16},{1,33},{17,49},{33,1},{49,17},{2,34}... | collective-permute-start | bytes 122888 | tf_op jit(solution)/shard_map/ppermute | solution.py:230
  82.3 5.3 %collective-permute-done.7.r3 = bf16[80,256]{1,0:T(8,128)(2,1)S(1)} collective-permute-done((bf16[80,256]{1,0:T(8,128)(2,1)S(1)}, bf16[80,256]{1,0:T(8,128)(2,1)S(1)}, u32[]{:S(2)}, u32[]{:S(2)}) %collective-permute-start.7) | collective-permute-done | bytes 40992 | tf_op jit(solution)/shard_map/ppermute | solution.py:230
  88.2 0.8 all-to-all-done.2.got_ref
  89.0 0.7 shard_map.97
  89.7 7.0 %all-to-all-start.3 = ((bf16[8,16,256]{2,1,0:T(8,128)(2,1)}), bf16[8,16,256]{2,1,0:T(8,128)(2,1)S(1)}, u32[]{:S(2)}, u32[]{:S(2)}) async-start(bf16[8,16,256]{2,1,0:T(8,128)(2,1)} %shard_map.99), calls=%async_computation.3 | async-start | bytes 131072 | tf_op jit(solution)/shard_map/all_to_all | solution.py:307
  96.7 1.9 %collective-permute-start.3 = (bf16[16,256]{1,0:T(8,128)(2,1)S(1)}, bf16[16,256]{1,0:T(8,128)(2,1)S(1)}, u32[]{:S(2)}, u32[]{:S(2)}) collective-permute-start(bf16[16,256]{1,0:T(8,128)(2,1)S(1)} %get-tuple-element.37), channel_id=1, source_target_pairs={{0,16},{16,0},{32,48},{48,32},{1,17},{17,1},{33,49},{49,33},{2,18}... | collective-permute-start | bytes 24584 | tf_op jit(solution)/shard_map/ppermute | solution.py:234
  98.6 3.6 %collective-permute-done.3.got_ref = bf16[16,256]{1,0:T(8,128)(2,1)S(1)} collective-permute-done((bf16[16,256]{1,0:T(8,128)(2,1)S(1)}, bf16[16,256]{1,0:T(8,128)(2,1)S(1)}, u32[]{:S(2)}, u32[]{:S(2)}) %collective-permute-start.3) | collective-permute-done | bytes 8224 | tf_op jit(solution)/shard_map/ppermute | solution.py:234
  102.2 2.0 %collective-permute-start.4 = (bf16[16,256]{1,0:T(8,128)(2,1)S(1)}, bf16[16,256]{1,0:T(8,128)(2,1)S(1)}, u32[]{:S(2)}, u32[]{:S(2)}) collective-permute-start(bf16[16,256]{1,0:T(8,128)(2,1)S(1)} %get-tuple-element.39), channel_id=1, source_target_pairs={{0,48},{16,32},{32,16},{48,0},{1,49},{17,33},{33,17},{49,1},{2,50}... | collective-permute-start | bytes 24584 | tf_op jit(solution)/shard_map/ppermute | solution.py:234
  104.2 4.8 %collective-permute-done.4.more_ref = bf16[16,256]{1,0:T(8,128)(2,1)S(1)} collective-permute-done((bf16[16,256]{1,0:T(8,128)(2,1)S(1)}, bf16[16,256]{1,0:T(8,128)(2,1)S(1)}, u32[]{:S(2)}, u32[]{:S(2)}) %collective-permute-start.4) | collective-permute-done | bytes 8224 | tf_op jit(solution)/shard_map/ppermute | solution.py:234
  109.0 0.7 shard_map.100
  (20 shorter events, 2.2 us)
Async XLA Ops:
  7.2 38.7 %copy-start.2 = (bf16[64,256]{1,0:T(8,128)(2,1)S(1)}, bf16[64,256]{1,0:T(8,128)(2,1)}, u32[]{:S(2)}) copy-start(bf16[64,256]{1,0:T(8,128)(2,1)} %b_ref.1) | copy-start | bytes 98308
  7.2 38.7 %copy-start.3 = (f32[256]{0:T(256)S(1)}, f32[256]{0:T(256)}, u32[]{:S(2)}) copy-start(f32[256]{0:T(256)} %param.11) | copy-start | bytes 3076
  7.2 48.6 %all-gather.3.cloned.1.call-start = ((), (), s32[]{:S(2)}) async-start(), calls=%async_computation.4 | async-start | bytes 2621440 | tf_op jit(solution)/shard_map/all_gather | solution.py:250
  35.5 25.9 %all-to-all-start.1 = ((bf16[8,32,1024]{2,1,0:T(8,128)(2,1)}), bf16[8,32,1024]{2,1,0:T(8,128)(2,1)S(1)}, u32[]{:S(2)}, u32[]{:S(2)}) async-start(bf16[8,32,1024]{2,1,0:T(8,128)(2,1)} %get-tuple-element.33), calls=%async_computation.1 | async-start | bytes 1048576 | tf_op jit(solution)/shard_map/all_to_all | solution.py:271
  46.6 9.2 %collective-permute-start = (bf16[320,256]{1,0:T(8,128)(2,1)S(1)}, bf16[320,256]{1,0:T(8,128)(2,1)S(1)}, u32[]{:S(2)}, u32[]{:S(2)}) collective-permute-start(bf16[320,256]{1,0:T(8,128)(2,1)S(1)} %get-tuple-element.28), channel_id=1, source_target_pairs={{0,16},{16,32},{32,48},{48,0},{1,17},{17,33},{33,49},{49,1},{2,18}... | collective-permute-start | bytes 491528 | tf_op jit(solution)/shard_map/ppermute | solution.py:230
  49.0 9.5 %collective-permute-start.1 = (bf16[320,256]{1,0:T(8,128)(2,1)}, bf16[320,256]{1,0:T(8,128)(2,1)S(1)}, u32[]{:S(2)}, u32[]{:S(2)}) collective-permute-start(bf16[320,256]{1,0:T(8,128)(2,1)} %get-tuple-element.29), channel_id=1, source_target_pairs={{0,48},{16,0},{32,16},{48,32},{1,49},{17,1},{33,17},{49,33},{2,50}... | collective-permute-start | bytes 491528 | tf_op jit(solution)/shard_map/ppermute | solution.py:230
  52.5 8.9 %collective-permute-start.2 = (bf16[320,256]{1,0:T(8,128)(2,1)}, bf16[320,256]{1,0:T(8,128)(2,1)S(1)}, u32[]{:S(2)}, u32[]{:S(2)}) collective-permute-start(bf16[320,256]{1,0:T(8,128)(2,1)} %get-tuple-element.30), channel_id=1, source_target_pairs={{0,32},{16,48},{32,0},{48,16},{1,33},{17,49},{33,1},{49,17},{2,34}... | collective-permute-start | bytes 491528 | tf_op jit(solution)/shard_map/ppermute | solution.py:230
  55.8 1.6 %copy-start = (bf16[4096,256]{1,0:T(8,128)(2,1)S(1)}, bf16[4096,256]{1,0:T(8,128)(2,1)}, u32[]{:S(2)}) copy-start(bf16[4096,256]{1,0:T(8,128)(2,1)} %all-gather.3.cloned.1.call-done) | copy-start | bytes 6291460
  57.4 4.0 %copy-start.1 = (bf16[1024,64]{0,1:T(8,128)(2,1)S(1)}, bf16[1024,64]{0,1:T(8,128)(2,1)}, u32[]{:S(2)}) copy-start(bf16[1024,64]{0,1:T(8,128)(2,1)} %param.9) | copy-start | bytes 393220
  65.2 0.6 copy-start.4
  65.9 23.1 %all-to-all-start.2 = ((bf16[8,32,1280]{2,1,0:T(8,128)(2,1)}), bf16[8,32,1280]{2,1,0:T(8,128)(2,1)S(1)}, u32[]{:S(2)}, u32[]{:S(2)}) async-start(bf16[8,32,1280]{2,1,0:T(8,128)(2,1)} %bitcast.5), calls=%async_computation.2 | async-start | bytes 1310720 | tf_op jit(solution)/shard_map/all_to_all | solution.py:296
  73.1 9.2 %collective-permute-start.5 = (bf16[80,256]{1,0:T(8,128)(2,1)}, bf16[80,256]{1,0:T(8,128)(2,1)S(1)}, u32[]{:S(2)}, u32[]{:S(2)}) collective-permute-start(bf16[80,256]{1,0:T(8,128)(2,1)} %copy-done.4), channel_id=1, source_target_pairs={{0,48},{16,0},{32,16},{48,32},{1,49},{17,1},{33,17},{49,33},{2,50}... | collective-permute-start | bytes 122888 | tf_op jit(solution)/shard_map/ppermute | solution.py:230
  75.8 6.5 %collective-permute-start.6 = (bf16[80,256]{1,0:T(8,128)(2,1)S(1)}, bf16[80,256]{1,0:T(8,128)(2,1)S(1)}, u32[]{:S(2)}, u32[]{:S(2)}) collective-permute-start(bf16[80,256]{1,0:T(8,128)(2,1)S(1)} %get-tuple-element.42), channel_id=1, source_target_pairs={{0,16},{16,32},{32,48},{48,0},{1,17},{17,33},{33,49},{49,1},{2,18}... | collective-permute-start | bytes 122888 | tf_op jit(solution)/shard_map/ppermute | solution.py:230
  80.1 7.4 %collective-permute-start.7 = (bf16[80,256]{1,0:T(8,128)(2,1)S(1)}, bf16[80,256]{1,0:T(8,128)(2,1)S(1)}, u32[]{:S(2)}, u32[]{:S(2)}) collective-permute-start(bf16[80,256]{1,0:T(8,128)(2,1)S(1)} %get-tuple-element.43), channel_id=1, source_target_pairs={{0,32},{16,48},{32,0},{48,16},{1,33},{17,49},{33,1},{49,17},{2,34}... | collective-permute-start | bytes 122888 | tf_op jit(solution)/shard_map/ppermute | solution.py:230
  89.7 19.3 %all-to-all-start.3 = ((bf16[8,16,256]{2,1,0:T(8,128)(2,1)}), bf16[8,16,256]{2,1,0:T(8,128)(2,1)S(1)}, u32[]{:S(2)}, u32[]{:S(2)}) async-start(bf16[8,16,256]{2,1,0:T(8,128)(2,1)} %shard_map.99), calls=%async_computation.3 | async-start | bytes 131072 | tf_op jit(solution)/shard_map/all_to_all | solution.py:307
  96.7 5.5 %collective-permute-start.3 = (bf16[16,256]{1,0:T(8,128)(2,1)S(1)}, bf16[16,256]{1,0:T(8,128)(2,1)S(1)}, u32[]{:S(2)}, u32[]{:S(2)}) collective-permute-start(bf16[16,256]{1,0:T(8,128)(2,1)S(1)} %get-tuple-element.37), channel_id=1, source_target_pairs={{0,16},{16,0},{32,48},{48,32},{1,17},{17,1},{33,49},{49,33},{2,18}... | collective-permute-start | bytes 24584 | tf_op jit(solution)/shard_map/ppermute | solution.py:234
  102.2 6.7 %collective-permute-start.4 = (bf16[16,256]{1,0:T(8,128)(2,1)S(1)}, bf16[16,256]{1,0:T(8,128)(2,1)S(1)}, u32[]{:S(2)}, u32[]{:S(2)}) collective-permute-start(bf16[16,256]{1,0:T(8,128)(2,1)S(1)} %get-tuple-element.39), channel_id=1, source_target_pairs={{0,48},{16,32},{32,16},{48,0},{1,49},{17,33},{33,17},{49,1},{2,50}... | collective-permute-start | bytes 24584 | tf_op jit(solution)/shard_map/ppermute | solution.py:234
Sparse Core Ops, SparseCore 0:
  10.1 39.3 all-gather.2

commit v8 on v6

--- a/solution.py
+++ b/solution.py
@@ -63,11 +63,10 @@
 
 
 def merge_body(
-    w_hbm, at_hbm, b_hbm, g_hbm, acts_hbm, pay_ref, many_hbm, w_ref, at_ref, b_ref, g_ref, acts_ref, sems, more
+    w_hbm, at_hbm, b_hbm, g_hbm, pay_ref, w_ref, at_ref, b_ref, g_ref, sems
 ):
     copies = fetch(
         (
-            (acts_hbm, acts_ref),
             (w_hbm, w_ref),
             (at_hbm, at_ref),
             (b_hbm, b_ref),
@@ -75,9 +74,7 @@
         ),
         sems,
     )
-    copies[0].wait()
-    repeats = fetch([(acts_ref, many_hbm.at[z]) for z in range(NZ)], more)
-    for copy in copies[1:]:
+    for copy in copies:
         copy.wait()
     din, width = w_ref.shape
     tokens = g_ref.shape[0]
@@ -91,8 +88,6 @@
     for y in range(NY):
         pay_ref[y, pl.ds(0, tokens), :] = g_ref[...]
         pay_ref[y, pl.ds(tokens, 16), :] = tail
-    for copy in repeats:
-        copy.wait()
 
 
 def scale_body(x_ref, got_ref, mag_ref, b_ref, *outs):
@@ -111,6 +106,11 @@
                 got_ref[block * half + h, pl.ds(0, tokens), :].astype(F32) * scale
             ).astype(BF16)
         out[pl.ds(half * tokens, b_ref.shape[0]), :] = b_ref[...]
+
+
+def many_body(acts_ref, many_hbm, sems):
+    for copy in fetch([(acts_ref, many_hbm.at[z]) for z in range(NZ)], sems):
+        copy.wait()
 
 
 def bring_body(wide_hbm, out_ref, sems):
@@ -249,18 +249,25 @@
     a_turned = a_left.T
     wide = lax.all_gather(w_base, "x")
     parts = (w_base, a_turned, b_right, grad_y)
-    pay, many = call(
+    (pay,) = call(
         merge_body,
-        [shape((NY, grad_y.shape[0] + 16, width)), shape((NZ, rows, din))],
+        [shape((NY, grad_y.shape[0] + 16, width))],
         2 * din * width * rank,
-        *parts, acts,
-        far=(0, 1, 2, 3, 4),
-        out_specs=[VMEM, HBM],
-        scratch=[pltpu.VMEM(p.shape, p.dtype) for p in (*parts, acts)]
-        + [pltpu.SemaphoreType.DMA((5,)), pltpu.SemaphoreType.DMA((NZ,))],
+        *parts,
+        far=(0, 1, 2, 3),
+        scratch=[pltpu.VMEM(p.shape, p.dtype) for p in parts]
+        + [pltpu.SemaphoreType.DMA((4,))],
         limit=60,
     )
     got = lax.all_to_all(pay, "din", 0, 0, tiled=True)
+    (many,) = call(
+        many_body,
+        [shape((NZ, rows, din))],
+        0,
+        after(acts, pay),
+        out_specs=[HBM],
+        scratch=[pltpu.SemaphoreType.DMA((NZ,))],
+    )
     scaled = call(
         scale_body,
         [shape((tokens + rank, width))] * NX,

time: 117 us -> 118 us (level)
  the two profiles are of different devices: /device:TPU:14 before, /device:TPU:8 now
where the time goes in v8:
time: 118 us
  starting transfers between devices  61.8 us (52%)
  waiting for transfers between devices  29.3 us (25%)
  between operations  14.2 us (12%)
  Pallas kernels  10.1 us (9%)
  local copies, waits for them, and re-layouts  2.21 us (2%)
    ppermute x6, starting transfers between devices, shift(): return lax.ppermute(block, 'x', [(i, (i + hop) % NX) for i in range(NX)])  20.3 us
    all_to_all x1, waiting for transfers between devices, local(): got = lax.all_to_all(pay, 'din', 0, 0, tiled=True)  14.9 us
    all_to_all x1, starting transfers between devices, local(): lax.all_to_all(after(many, got), 'z', 0, 0, tiled=True).reshape(tokens, din)  10.3 us
    pallas_call x9, Pallas kernels, call(): pl.pallas_call(body, out_shape=outs, in_specs=specs, out_specs=out_specs...  10.1 us
    all_to_all x1, starting transfers between devices, local(): got = lax.all_to_all(pay, 'din', 0, 0, tiled=True)  9.27 us
    ppermute x2, starting transfers between devices, swap(): return lax.ppermute(block, 'x', [(i, i ^ mask) for i in range(NX)])  7.35 us
    all_to_all x1, starting transfers between devices, local(): right = lax.all_to_all(after(pay, send), 'din', 0, 0, tiled=True)  7.26 us
    all_to_all x1, starting transfers between devices, local(): back = lax.all_to_all(part.reshape(NZ, rows, wider), 'z', 0, 0, tiled=True)  7.2 us
  transfers between devices with their start and end apart: 13, of which 7 were waited for; matrix products, arithmetic and copies ran while one was open for 0% of the time, Pallas kernels for 4%

profile of v8, /device:TPU:8, one launch (start us, length us, event | category | flops | bytes accessed | tf_op | source)
XLA Modules:
  0.0 117.6 jit_solution(13259222224520315606)
XLA Ops:
  7.9 2.3 %shard_map.93 = bf16[8,144,256]{2,1,0:T(8,128)(2,1)} custom-call(bf16[1024,256]{1,0:T(8,128)(2,1)} %w_hbm.1, bf16[64,1024]{1,0:T(8,128)(2,1)} %bitcast.9, bf16[64,256]{1,0:T(8,128)(2,1)} %b_ref.1, bf16[128,256]{1,0:T(8,128)(2,1)} %g_hbm.1), custom_call_target="tpu_custom_call" | custom-call | flops 33554432 | bytes 1343488 | tf_op jit(solution)/shard_map/pallas_call | solution.py:37
  10.2 9.3 %all-to-all-start = ((bf16[8,144,256]{2,1,0:T(8,128)(2,1)}), bf16[8,144,256]{2,1,0:T(8,128)(2,1)S(1)}, u32[]{:S(2)}, u32[]{:S(2)}) async-start(bf16[8,144,256]{2,1,0:T(8,128)(2,1)} %shard_map.93), calls=%async_computation | async-start | bytes 1179648 | tf_op jit(solution)/shard_map/all_to_all | solution.py:262
  19.5 0.9 shard_map.96
  20.4 14.9 %all-to-all-done.got_ref = bf16[8,144,256]{2,1,0:T(8,128)(2,1)S(1)} async-done(((bf16[8,144,256]{2,1,0:T(8,128)(2,1)}), bf16[8,144,256]{2,1,0:T(8,128)(2,1)S(1)}, u32[]{:S(2)}, u32[]{:S(2)}) %all-to-all-start) | async-done | bytes 589856 | tf_op jit(solution)/shard_map/all_to_all | solution.py:262
  35.2 10.3 %all-to-all-start.1 = ((bf16[8,32,1024]{2,1,0:T(8,128)(2,1)}), bf16[8,32,1024]{2,1,0:T(8,128)(2,1)S(1)}, u32[]{:S(2)}, u32[]{:S(2)}) async-start(bf16[8,32,1024]{2,1,0:T(8,128)(2,1)} %shard_map.96), calls=%async_computation.1 | async-start | bytes 1048576 | tf_op jit(solution)/shard_map/all_to_all | solution.py:278
  45.6 0.8 shard_map.94
  46.4 3.4 %collective-permute-start = (bf16[320,256]{1,0:T(8,128)(2,1)}, bf16[320,256]{1,0:T(8,128)(2,1)S(1)}, u32[]{:S(2)}, u32[]{:S(2)}) collective-permute-start(bf16[320,256]{1,0:T(8,128)(2,1)} %get-tuple-element.25), channel_id=1, source_target_pairs={{0,16},{16,32},{32,48},{48,0},{1,17},{17,33},{33,49},{49,1},{2,18}... | collective-permute-start | bytes 491528 | tf_op jit(solution)/shard_map/ppermute | solution.py:230
  49.8 3.7 %collective-permute-start.1 = (bf16[320,256]{1,0:T(8,128)(2,1)}, bf16[320,256]{1,0:T(8,128)(2,1)S(1)}, u32[]{:S(2)}, u32[]{:S(2)}) collective-permute-start(bf16[320,256]{1,0:T(8,128)(2,1)} %get-tuple-element.26), channel_id=1, source_target_pairs={{0,48},{16,0},{32,16},{48,32},{1,49},{17,1},{33,17},{49,33},{2,50}... | collective-permute-start | bytes 491528 | tf_op jit(solution)/shard_map/ppermute | solution.py:230
  53.5 3.7 %collective-permute-start.2 = (bf16[320,256]{1,0:T(8,128)(2,1)}, bf16[320,256]{1,0:T(8,128)(2,1)S(1)}, u32[]{:S(2)}, u32[]{:S(2)}) collective-permute-start(bf16[320,256]{1,0:T(8,128)(2,1)} %get-tuple-element.27), channel_id=1, source_target_pairs={{0,32},{16,48},{32,0},{48,16},{1,33},{17,49},{33,1},{49,17},{2,34}... | collective-permute-start | bytes 491528 | tf_op jit(solution)/shard_map/ppermute | solution.py:230
  57.2 1.6 %copy-done = bf16[4096,256]{1,0:T(8,128)(2,1)S(1)} copy-done((bf16[4096,256]{1,0:T(8,128)(2,1)S(1)}, bf16[4096,256]{1,0:T(8,128)(2,1)}, u32[]{:S(2)}) %copy-start) | copy-done | bytes 2097176
  59.0 3.4 %collective-permute-done.2.s3 = bf16[320,256]{1,0:T(8,128)(2,1)S(1)} collective-permute-done((bf16[320,256]{1,0:T(8,128)(2,1)}, bf16[320,256]{1,0:T(8,128)(2,1)S(1)}, u32[]{:S(2)}, u32[]{:S(2)}) %collective-permute-start.2) | collective-permute-done | bytes 163872 | tf_op jit(solution)/shard_map/ppermute | solution.py:230
  62.4 3.8 %shard_map.97 = (bf16[256,1280]{1,0:T(8,128)(2,1)}, bf16[80,256]{1,0:T(8,128)(2,1)S(1)}, bf16[80,256]{1,0:T(8,128)(2,1)S(1)}, bf16[80,256]{1,0:T(8,128)(2,1)S(1)}, bf16[80,256]{1,0:T(8,128)(2,1)S(1)}) custom-call(s32[1]{0:T(128)} %bitcast.x_ref, bf16[320,256]{1,0:T(8,128)(2,1)S(1)} %get-tuple-element.24.s0, bf16[320,256]{1,0:T(8,128)(2,1)S(1)} %collective-permute-done.s1, ...), custom_call_target="tpu_custom_call" | custom-call | flops 1073741824 | bytes 4227076 | tf_op jit(solution)/shard_map/pallas_call | solution.py:37
  66.9 7.2 %all-to-all-start.2 = ((bf16[8,32,1280]{2,1,0:T(8,128)(2,1)}), bf16[8,32,1280]{2,1,0:T(8,128)(2,1)S(1)}, u32[]{:S(2)}, u32[]{:S(2)}) async-start(bf16[8,32,1280]{2,1,0:T(8,128)(2,1)} %bitcast.5), calls=%async_computation.2 | async-start | bytes 1310720 | tf_op jit(solution)/shard_map/all_to_all | solution.py:303
  74.1 3.4 %collective-permute-start.5 = (bf16[80,256]{1,0:T(8,128)(2,1)}, bf16[80,256]{1,0:T(8,128)(2,1)S(1)}, u32[]{:S(2)}, u32[]{:S(2)}) collective-permute-start(bf16[80,256]{1,0:T(8,128)(2,1)} %copy-done.5), channel_id=1, source_target_pairs={{0,48},{16,0},{32,16},{48,32},{1,49},{17,1},{33,17},{49,33},{2,50}... | collective-permute-start | bytes 122888 | tf_op jit(solution)/shard_map/ppermute | solution.py:230
  77.5 2.4 %collective-permute-start.6 = (bf16[80,256]{1,0:T(8,128)(2,1)S(1)}, bf16[80,256]{1,0:T(8,128)(2,1)S(1)}, u32[]{:S(2)}, u32[]{:S(2)}) collective-permute-start(bf16[80,256]{1,0:T(8,128)(2,1)S(1)} %get-tuple-element.38), channel_id=1, source_target_pairs={{0,16},{16,32},{32,48},{48,0},{1,17},{17,33},{33,49},{49,1},{2,18}... | collective-permute-start | bytes 122888 | tf_op jit(solution)/shard_map/ppermute | solution.py:230
  79.9 3.7 %collective-permute-start.7 = (bf16[80,256]{1,0:T(8,128)(2,1)S(1)}, bf16[80,256]{1,0:T(8,128)(2,1)S(1)}, u32[]{:S(2)}, u32[]{:S(2)}) collective-permute-start(bf16[80,256]{1,0:T(8,128)(2,1)S(1)} %get-tuple-element.39), channel_id=1, source_target_pairs={{0,32},{16,48},{32,0},{48,16},{1,33},{17,49},{33,1},{49,17},{2,34}... | collective-permute-start | bytes 122888 | tf_op jit(solution)/shard_map/ppermute | solution.py:230
  83.7 1.0 collective-permute-done.6.r2
  84.6 2.7 %collective-permute-done.7.r3 = bf16[80,256]{1,0:T(8,128)(2,1)S(1)} collective-permute-done((bf16[80,256]{1,0:T(8,128)(2,1)S(1)}, bf16[80,256]{1,0:T(8,128)(2,1)S(1)}, u32[]{:S(2)}, u32[]{:S(2)}) %collective-permute-start.7) | collective-permute-done | bytes 40992 | tf_op jit(solution)/shard_map/ppermute | solution.py:230
  88.0 1.8 %all-to-all-done.2.got_ref = bf16[8,32,1280]{2,1,0:T(8,128)(2,1)S(1)} async-done(((bf16[8,32,1280]{2,1,0:T(8,128)(2,1)}), bf16[8,32,1280]{2,1,0:T(8,128)(2,1)S(1)}, u32[]{:S(2)}, u32[]{:S(2)}) %all-to-all-start.2) | async-done | bytes 655392 | tf_op jit(solution)/shard_map/all_to_all | solution.py:303
  90.5 7.3 %all-to-all-start.3 = ((bf16[8,16,256]{2,1,0:T(8,128)(2,1)}), bf16[8,16,256]{2,1,0:T(8,128)(2,1)S(1)}, u32[]{:S(2)}, u32[]{:S(2)}) async-start(bf16[8,16,256]{2,1,0:T(8,128)(2,1)} %shard_map.100), calls=%async_computation.3 | async-start | bytes 131072 | tf_op jit(solution)/shard_map/all_to_all | solution.py:314
  97.8 3.1 %collective-permute-start.3 = (bf16[16,256]{1,0:T(8,128)(2,1)S(1)}, bf16[16,256]{1,0:T(8,128)(2,1)S(1)}, u32[]{:S(2)}, u32[]{:S(2)}) collective-permute-start(bf16[16,256]{1,0:T(8,128)(2,1)S(1)} %get-tuple-element.33), channel_id=1, source_target_pairs={{0,16},{16,0},{32,48},{48,32},{1,17},{17,1},{33,49},{49,33},{2,18}... | collective-permute-start | bytes 24584 | tf_op jit(solution)/shard_map/ppermute | solution.py:234
  100.9 2.4 %collective-permute-done.3.got_ref = bf16[16,256]{1,0:T(8,128)(2,1)S(1)} collective-permute-done((bf16[16,256]{1,0:T(8,128)(2,1)S(1)}, bf16[16,256]{1,0:T(8,128)(2,1)S(1)}, u32[]{:S(2)}, u32[]{:S(2)}) %collective-permute-start.3) | collective-permute-done | bytes 8224 | tf_op jit(solution)/shard_map/ppermute | solution.py:234
  103.3 4.3 %collective-permute-start.4 = (bf16[16,256]{1,0:T(8,128)(2,1)S(1)}, bf16[16,256]{1,0:T(8,128)(2,1)S(1)}, u32[]{:S(2)}, u32[]{:S(2)}) collective-permute-start(bf16[16,256]{1,0:T(8,128)(2,1)S(1)} %get-tuple-element.35), channel_id=1, source_target_pairs={{0,48},{16,32},{32,16},{48,0},{1,49},{17,33},{33,17},{49,1},{2,50}... | collective-permute-start | bytes 24584 | tf_op jit(solution)/shard_map/ppermute | solution.py:234
  107.6 2.5 %collective-permute-done.4.more_ref = bf16[16,256]{1,0:T(8,128)(2,1)S(1)} collective-permute-done((bf16[16,256]{1,0:T(8,128)(2,1)S(1)}, bf16[16,256]{1,0:T(8,128)(2,1)S(1)}, u32[]{:S(2)}, u32[]{:S(2)}) %collective-permute-start.4) | collective-permute-done | bytes 8224 | tf_op jit(solution)/shard_map/ppermute | solution.py:234
  (24 shorter events, 3.6 us)
Async XLA Ops:
  7.2 12.3 %copy-start.3 = (bf16[32,1024]{1,0:T(8,128)(2,1)S(1)}, bf16[32,1024]{1,0:T(8,128)(2,1)}, u32[]{:S(2)}) copy-start(bf16[32,1024]{1,0:T(8,128)(2,1)} %acts_ref) | copy-start | bytes 196612
  7.2 50.1 %all-gather.3.cloned.1.call-start = ((), (), s32[]{:S(2)}) async-start(), calls=%async_computation.4 | async-start | bytes 2621440 | tf_op jit(solution)/shard_map/all_gather | solution.py:250
  7.9 37.6 %copy-start.2 = (bf16[64,256]{1,0:T(8,128)(2,1)S(1)}, bf16[64,256]{1,0:T(8,128)(2,1)}, u32[]{:S(2)}) copy-start(bf16[64,256]{1,0:T(8,128)(2,1)} %b_ref.1) | copy-start | bytes 98308
  7.9 37.6 %copy-start.4 = (f32[256]{0:T(256)S(1)}, f32[256]{0:T(256)}, u32[]{:S(2)}) copy-start(f32[256]{0:T(256)} %param.11) | copy-start | bytes 3076
  10.2 25.0 %all-to-all-start = ((bf16[8,144,256]{2,1,0:T(8,128)(2,1)}), bf16[8,144,256]{2,1,0:T(8,128)(2,1)S(1)}, u32[]{:S(2)}, u32[]{:S(2)}) async-start(bf16[8,144,256]{2,1,0:T(8,128)(2,1)} %shard_map.93), calls=%async_computation | async-start | bytes 1179648 | tf_op jit(solution)/shard_map/all_to_all | solution.py:262
  35.2 27.2 %all-to-all-start.1 = ((bf16[8,32,1024]{2,1,0:T(8,128)(2,1)}), bf16[8,32,1024]{2,1,0:T(8,128)(2,1)S(1)}, u32[]{:S(2)}, u32[]{:S(2)}) async-start(bf16[8,32,1024]{2,1,0:T(8,128)(2,1)} %shard_map.96), calls=%async_computation.1 | async-start | bytes 1048576 | tf_op jit(solution)/shard_map/all_to_all | solution.py:278
  46.4 12.6 %collective-permute-start = (bf16[320,256]{1,0:T(8,128)(2,1)}, bf16[320,256]{1,0:T(8,128)(2,1)S(1)}, u32[]{:S(2)}, u32[]{:S(2)}) collective-permute-start(bf16[320,256]{1,0:T(8,128)(2,1)} %get-tuple-element.25), channel_id=1, source_target_pairs={{0,16},{16,32},{32,48},{48,0},{1,17},{17,33},{33,49},{49,1},{2,18}... | collective-permute-start | bytes 491528 | tf_op jit(solution)/shard_map/ppermute | solution.py:230
  49.8 9.2 %collective-permute-start.1 = (bf16[320,256]{1,0:T(8,128)(2,1)}, bf16[320,256]{1,0:T(8,128)(2,1)S(1)}, u32[]{:S(2)}, u32[]{:S(2)}) collective-permute-start(bf16[320,256]{1,0:T(8,128)(2,1)} %get-tuple-element.26), channel_id=1, source_target_pairs={{0,48},{16,0},{32,16},{48,32},{1,49},{17,1},{33,17},{49,33},{2,50}... | collective-permute-start | bytes 491528 | tf_op jit(solution)/shard_map/ppermute | solution.py:230
  53.5 8.9 %collective-permute-start.2 = (bf16[320,256]{1,0:T(8,128)(2,1)}, bf16[320,256]{1,0:T(8,128)(2,1)S(1)}, u32[]{:S(2)}, u32[]{:S(2)}) collective-permute-start(bf16[320,256]{1,0:T(8,128)(2,1)} %get-tuple-element.27), channel_id=1, source_target_pairs={{0,32},{16,48},{32,0},{48,16},{1,33},{17,49},{33,1},{49,17},{2,34}... | collective-permute-start | bytes 491528 | tf_op jit(solution)/shard_map/ppermute | solution.py:230
  57.2 1.6 %copy-start = (bf16[4096,256]{1,0:T(8,128)(2,1)S(1)}, bf16[4096,256]{1,0:T(8,128)(2,1)}, u32[]{:S(2)}) copy-start(bf16[4096,256]{1,0:T(8,128)(2,1)} %all-gather.3.cloned.1.call-done) | copy-start | bytes 6291460
  58.8 3.6 %copy-start.1 = (bf16[1024,64]{0,1:T(8,128)(2,1)S(1)}, bf16[1024,64]{0,1:T(8,128)(2,1)}, u32[]{:S(2)}) copy-start(bf16[1024,64]{0,1:T(8,128)(2,1)} %param.9) | copy-start | bytes 393220
  66.3 0.6 copy-start.5
  66.9 22.9 %all-to-all-start.2 = ((bf16[8,32,1280]{2,1,0:T(8,128)(2,1)}), bf16[8,32,1280]{2,1,0:T(8,128)(2,1)S(1)}, u32[]{:S(2)}, u32[]{:S(2)}) async-start(bf16[8,32,1280]{2,1,0:T(8,128)(2,1)} %bitcast.5), calls=%async_computation.2 | async-start | bytes 1310720 | tf_op jit(solution)/shard_map/all_to_all | solution.py:303
  74.1 9.6 %collective-permute-start.5 = (bf16[80,256]{1,0:T(8,128)(2,1)}, bf16[80,256]{1,0:T(8,128)(2,1)S(1)}, u32[]{:S(2)}, u32[]{:S(2)}) collective-permute-start(bf16[80,256]{1,0:T(8,128)(2,1)} %copy-done.5), channel_id=1, source_target_pairs={{0,48},{16,0},{32,16},{48,32},{1,49},{17,1},{33,17},{49,33},{2,50}... | collective-permute-start | bytes 122888 | tf_op jit(solution)/shard_map/ppermute | solution.py:230
  77.5 7.1 %collective-permute-start.6 = (bf16[80,256]{1,0:T(8,128)(2,1)S(1)}, bf16[80,256]{1,0:T(8,128)(2,1)S(1)}, u32[]{:S(2)}, u32[]{:S(2)}) collective-permute-start(bf16[80,256]{1,0:T(8,128)(2,1)S(1)} %get-tuple-element.38), channel_id=1, source_target_pairs={{0,16},{16,32},{32,48},{48,0},{1,17},{17,33},{33,49},{49,1},{2,18}... | collective-permute-start | bytes 122888 | tf_op jit(solution)/shard_map/ppermute | solution.py:230
  79.9 7.4 %collective-permute-start.7 = (bf16[80,256]{1,0:T(8,128)(2,1)S(1)}, bf16[80,256]{1,0:T(8,128)(2,1)S(1)}, u32[]{:S(2)}, u32[]{:S(2)}) collective-permute-start(bf16[80,256]{1,0:T(8,128)(2,1)S(1)} %get-tuple-element.39), channel_id=1, source_target_pairs={{0,32},{16,48},{32,0},{48,16},{1,33},{17,49},{33,1},{49,17},{2,34}... | collective-permute-start | bytes 122888 | tf_op jit(solution)/shard_map/ppermute | solution.py:230
  90.5 19.5 %all-to-all-start.3 = ((bf16[8,16,256]{2,1,0:T(8,128)(2,1)}), bf16[8,16,256]{2,1,0:T(8,128)(2,1)S(1)}, u32[]{:S(2)}, u32[]{:S(2)}) async-start(bf16[8,16,256]{2,1,0:T(8,128)(2,1)} %shard_map.100), calls=%async_computation.3 | async-start | bytes 131072 | tf_op jit(solution)/shard_map/all_to_all | solution.py:314
  97.8 5.5 %collective-permute-start.3 = (bf16[16,256]{1,0:T(8,128)(2,1)S(1)}, bf16[16,256]{1,0:T(8,128)(2,1)S(1)}, u32[]{:S(2)}, u32[]{:S(2)}) collective-permute-start(bf16[16,256]{1,0:T(8,128)(2,1)S(1)} %get-tuple-element.33), channel_id=1, source_target_pairs={{0,16},{16,0},{32,48},{48,32},{1,17},{17,1},{33,49},{49,33},{2,18}... | collective-permute-start | bytes 24584 | tf_op jit(solution)/shard_map/ppermute | solution.py:234
  103.3 6.7 %collective-permute-start.4 = (bf16[16,256]{1,0:T(8,128)(2,1)S(1)}, bf16[16,256]{1,0:T(8,128)(2,1)S(1)}, u32[]{:S(2)}, u32[]{:S(2)}) collective-permute-start(bf16[16,256]{1,0:T(8,128)(2,1)S(1)} %get-tuple-element.35), channel_id=1, source_target_pairs={{0,48},{16,32},{32,16},{48,0},{1,49},{17,33},{33,17},{49,1},{2,50}... | collective-permute-start | bytes 24584 | tf_op jit(solution)/shard_map/ppermute | solution.py:234
Sparse Core Ops, SparseCore 0:
  10.1 41.5 all-gather.2

commit v9 on v6

--- a/solution.py
+++ b/solution.py
@@ -15,7 +15,7 @@
 SMEM = pl.BlockSpec(memory_space=pltpu.SMEM)
 HBM = pl.BlockSpec(memory_space=pltpu.HBM)
 MIB = 1024 * 1024
-STEP = 256
+STEP = 512
 HOPS = (0, 1, 3, 2)
 
 

time: 117 us -> 117 us (level)
  no operation moved by 1% of the time
where the time goes in v9:
time: 117 us
  starting transfers between devices  46.6 us (40%)
  blocking collectives  25 us (21%)
  waiting for transfers between devices  19 us (16%)
  between operations  14.2 us (12%)
  Pallas kernels  9.48 us (8%)
  local copies, waits for them, and re-layouts  2.21 us (2%)
    all_to_all x1, blocking collectives, local(): got = lax.all_to_all(pay, 'din', 0, 0, tiled=True)  25 us
    ppermute x6, starting transfers between devices, shift(): return lax.ppermute(block, 'x', [(i, (i + hop) % NX) for i in range(NX)])  18.3 us
    all_to_all x1, starting transfers between devices, local(): lax.all_to_all(after(many, got), 'z', 0, 0, tiled=True).reshape(tokens, din)  10.3 us
    pallas_call x8, Pallas kernels, call(): pl.pallas_call(body, out_shape=outs, in_specs=specs, out_specs=out_specs...  9.48 us
    ppermute x6, waiting for transfers between devices, shift(): return lax.ppermute(block, 'x', [(i, (i + hop) % NX) for i in range(NX)])  9.05 us
    ppermute x2, waiting for transfers between devices, swap(): return lax.ppermute(block, 'x', [(i, i ^ mask) for i in range(NX)])  8.44 us
    all_to_all x1, starting transfers between devices, local(): back = lax.all_to_all(part.reshape(NZ, rows, wider), 'z', 0, 0, tiled=True)  7.2 us
    all_to_all x1, starting transfers between devices, local(): right = lax.all_to_all(after(pay, send), 'din', 0, 0, tiled=True)  6.97 us
  transfers between devices with their start and end apart: 12, of which 6 were waited for; matrix products, arithmetic and copies ran while one was open for 0% of the time, Pallas kernels for 4%

profile of v9, /device:TPU:14, one launch (start us, length us, event | category | flops | bytes accessed | tf_op | source)
XLA Modules:
  0.0 116.5 jit_solution(7767927681774704302)
XLA Ops:
  7.9 2.6 %shard_map.93 = (bf16[8,144,256]{2,1,0:T(8,128)(2,1)}, bf16[8,32,1024]{2,1,0:T(8,128)(2,1)}) custom-call(bf16[1024,256]{1,0:T(8,128)(2,1)} %w_hbm.1, bf16[64,1024]{1,0:T(8,128)(2,1)} %bitcast.9, bf16[64,256]{1,0:T(8,128)(2,1)} %b_ref.1, bf16[128,256]{1,0:T(8,128)(2,1)} %g_hbm.1, bf16[32,1024]{1,0:T(8,128)(2,1)} %acts_hbm.1), custom_call_target="tpu_custom_call" | custom-call | flops 33554432 | bytes 1933312 | tf_op jit(solution)/shard_map/pallas_call | solution.py:37
  10.5 25.0 %all_to_all.20.got_ref = bf16[8,144,256]{2,1,0:T(8,128)(2,1)S(1)} all-to-all(bf16[8,144,256]{2,1,0:T(8,128)(2,1)} %get-tuple-element.25), channel_id=1, replica_groups=mesh['din'=8,'x'=4,'z'=8,'layer'=2] {'din'}, dimensions={0} | all-to-all | bytes 1179648 | tf_op jit(solution)/shard_map/all_to_all | solution.py:263
  35.5 10.3 %all-to-all-start.1 = ((bf16[8,32,1024]{2,1,0:T(8,128)(2,1)}), bf16[8,32,1024]{2,1,0:T(8,128)(2,1)S(1)}, u32[]{:S(2)}, u32[]{:S(2)}) async-start(bf16[8,32,1024]{2,1,0:T(8,128)(2,1)} %get-tuple-element.31), calls=%async_computation.1 | async-start | bytes 1048576 | tf_op jit(solution)/shard_map/all_to_all | solution.py:271
  45.8 0.9 shard_map.94
  46.7 2.4 %collective-permute-start = (bf16[320,256]{1,0:T(8,128)(2,1)}, bf16[320,256]{1,0:T(8,128)(2,1)S(1)}, u32[]{:S(2)}, u32[]{:S(2)}) collective-permute-start(bf16[320,256]{1,0:T(8,128)(2,1)} %get-tuple-element.27), channel_id=1, source_target_pairs={{0,16},{16,32},{32,48},{48,0},{1,17},{17,33},{33,49},{49,1},{2,18}... | collective-permute-start | bytes 491528 | tf_op jit(solution)/shard_map/ppermute | solution.py:230
  49.1 3.5 %collective-permute-start.1 = (bf16[320,256]{1,0:T(8,128)(2,1)}, bf16[320,256]{1,0:T(8,128)(2,1)S(1)}, u32[]{:S(2)}, u32[]{:S(2)}) collective-permute-start(bf16[320,256]{1,0:T(8,128)(2,1)} %get-tuple-element.28), channel_id=1, source_target_pairs={{0,48},{16,0},{32,16},{48,32},{1,49},{17,1},{33,17},{49,33},{2,50}... | collective-permute-start | bytes 491528 | tf_op jit(solution)/shard_map/ppermute | solution.py:230
  52.5 3.3 %collective-permute-start.2 = (bf16[320,256]{1,0:T(8,128)(2,1)}, bf16[320,256]{1,0:T(8,128)(2,1)S(1)}, u32[]{:S(2)}, u32[]{:S(2)}) collective-permute-start(bf16[320,256]{1,0:T(8,128)(2,1)} %get-tuple-element.29), channel_id=1, source_target_pairs={{0,32},{16,48},{32,0},{48,16},{1,33},{17,49},{33,1},{49,17},{2,34}... | collective-permute-start | bytes 491528 | tf_op jit(solution)/shard_map/ppermute | solution.py:230
  55.9 1.6 %copy-done = bf16[4096,256]{1,0:T(8,128)(2,1)S(1)} copy-done((bf16[4096,256]{1,0:T(8,128)(2,1)S(1)}, bf16[4096,256]{1,0:T(8,128)(2,1)}, u32[]{:S(2)}) %copy-start) | copy-done | bytes 2097176
  57.7 0.9 collective-permute-done.1.s2
  58.5 2.9 %collective-permute-done.2.s3 = bf16[320,256]{1,0:T(8,128)(2,1)S(1)} collective-permute-done((bf16[320,256]{1,0:T(8,128)(2,1)}, bf16[320,256]{1,0:T(8,128)(2,1)S(1)}, u32[]{:S(2)}, u32[]{:S(2)}) %collective-permute-start.2) | collective-permute-done | bytes 163872 | tf_op jit(solution)/shard_map/ppermute | solution.py:230
  61.5 3.8 %shard_map.96 = (bf16[256,1280]{1,0:T(8,128)(2,1)}, bf16[80,256]{1,0:T(8,128)(2,1)S(1)}, bf16[80,256]{1,0:T(8,128)(2,1)S(1)}, bf16[80,256]{1,0:T(8,128)(2,1)S(1)}, bf16[80,256]{1,0:T(8,128)(2,1)S(1)}) custom-call(s32[1]{0:T(128)} %bitcast.x_ref, bf16[320,256]{1,0:T(8,128)(2,1)S(1)} %get-tuple-element.26.s0, bf16[320,256]{1,0:T(8,128)(2,1)S(1)} %collective-permute-done.s1, ...), custom_call_target="tpu_custom_call" | custom-call | flops 1073741824 | bytes 4227076 | tf_op jit(solution)/shard_map/pallas_call | solution.py:37
  65.9 7.2 %all-to-all-start.2 = ((bf16[8,32,1280]{2,1,0:T(8,128)(2,1)}), bf16[8,32,1280]{2,1,0:T(8,128)(2,1)S(1)}, u32[]{:S(2)}, u32[]{:S(2)}) async-start(bf16[8,32,1280]{2,1,0:T(8,128)(2,1)} %bitcast.5), calls=%async_computation.2 | async-start | bytes 1310720 | tf_op jit(solution)/shard_map/all_to_all | solution.py:296
  73.1 2.7 %collective-permute-start.5 = (bf16[80,256]{1,0:T(8,128)(2,1)}, bf16[80,256]{1,0:T(8,128)(2,1)S(1)}, u32[]{:S(2)}, u32[]{:S(2)}) collective-permute-start(bf16[80,256]{1,0:T(8,128)(2,1)} %copy-done.4), channel_id=1, source_target_pairs={{0,48},{16,0},{32,16},{48,32},{1,49},{17,1},{33,17},{49,33},{2,50}... | collective-permute-start | bytes 122888 | tf_op jit(solution)/shard_map/ppermute | solution.py:230
  75.8 4.3 %collective-permute-start.6 = (bf16[80,256]{1,0:T(8,128)(2,1)S(1)}, bf16[80,256]{1,0:T(8,128)(2,1)S(1)}, u32[]{:S(2)}, u32[]{:S(2)}) collective-permute-start(bf16[80,256]{1,0:T(8,128)(2,1)S(1)} %get-tuple-element.40), channel_id=1, source_target_pairs={{0,16},{16,32},{32,48},{48,0},{1,17},{17,33},{33,49},{49,1},{2,18}... | collective-permute-start | bytes 122888 | tf_op jit(solution)/shard_map/ppermute | solution.py:230
  80.2 2.1 %collective-permute-start.7 = (bf16[80,256]{1,0:T(8,128)(2,1)S(1)}, bf16[80,256]{1,0:T(8,128)(2,1)S(1)}, u32[]{:S(2)}, u32[]{:S(2)}) collective-permute-start(bf16[80,256]{1,0:T(8,128)(2,1)S(1)} %get-tuple-element.41), channel_id=1, source_target_pairs={{0,32},{16,48},{32,0},{48,16},{1,33},{17,49},{33,1},{49,17},{2,34}... | collective-permute-start | bytes 122888 | tf_op jit(solution)/shard_map/ppermute | solution.py:230
  82.3 5.3 %collective-permute-done.7.r3 = bf16[80,256]{1,0:T(8,128)(2,1)S(1)} collective-permute-done((bf16[80,256]{1,0:T(8,128)(2,1)S(1)}, bf16[80,256]{1,0:T(8,128)(2,1)S(1)}, u32[]{:S(2)}, u32[]{:S(2)}) %collective-permute-start.7) | collective-permute-done | bytes 40992 | tf_op jit(solution)/shard_map/ppermute | solution.py:230
  88.2 0.8 all-to-all-done.2.got_ref
  89.0 0.7 shard_map.97
  89.7 7.0 %all-to-all-start.3 = ((bf16[8,16,256]{2,1,0:T(8,128)(2,1)}), bf16[8,16,256]{2,1,0:T(8,128)(2,1)S(1)}, u32[]{:S(2)}, u32[]{:S(2)}) async-start(bf16[8,16,256]{2,1,0:T(8,128)(2,1)} %shard_map.99), calls=%async_computation.3 | async-start | bytes 131072 | tf_op jit(solution)/shard_map/all_to_all | solution.py:307
  96.7 1.9 %collective-permute-start.3 = (bf16[16,256]{1,0:T(8,128)(2,1)S(1)}, bf16[16,256]{1,0:T(8,128)(2,1)S(1)}, u32[]{:S(2)}, u32[]{:S(2)}) collective-permute-start(bf16[16,256]{1,0:T(8,128)(2,1)S(1)} %get-tuple-element.35), channel_id=1, source_target_pairs={{0,16},{16,0},{32,48},{48,32},{1,17},{17,1},{33,49},{49,33},{2,18}... | collective-permute-start | bytes 24584 | tf_op jit(solution)/shard_map/ppermute | solution.py:234
  98.6 3.6 %collective-permute-done.3.got_ref = bf16[16,256]{1,0:T(8,128)(2,1)S(1)} collective-permute-done((bf16[16,256]{1,0:T(8,128)(2,1)S(1)}, bf16[16,256]{1,0:T(8,128)(2,1)S(1)}, u32[]{:S(2)}, u32[]{:S(2)}) %collective-permute-start.3) | collective-permute-done | bytes 8224 | tf_op jit(solution)/shard_map/ppermute | solution.py:234
  102.2 1.9 %collective-permute-start.4 = (bf16[16,256]{1,0:T(8,128)(2,1)S(1)}, bf16[16,256]{1,0:T(8,128)(2,1)S(1)}, u32[]{:S(2)}, u32[]{:S(2)}) collective-permute-start(bf16[16,256]{1,0:T(8,128)(2,1)S(1)} %get-tuple-element.37), channel_id=1, source_target_pairs={{0,48},{16,32},{32,16},{48,0},{1,49},{17,33},{33,17},{49,1},{2,50}... | collective-permute-start | bytes 24584 | tf_op jit(solution)/shard_map/ppermute | solution.py:234
  104.2 4.8 %collective-permute-done.4.more_ref = bf16[16,256]{1,0:T(8,128)(2,1)S(1)} collective-permute-done((bf16[16,256]{1,0:T(8,128)(2,1)S(1)}, bf16[16,256]{1,0:T(8,128)(2,1)S(1)}, u32[]{:S(2)}, u32[]{:S(2)}) %collective-permute-start.4) | collective-permute-done | bytes 8224 | tf_op jit(solution)/shard_map/ppermute | solution.py:234
  109.0 0.7 shard_map.100
  (20 shorter events, 2.2 us)
Async XLA Ops:
  7.2 38.7 %copy-start.2 = (bf16[64,256]{1,0:T(8,128)(2,1)S(1)}, bf16[64,256]{1,0:T(8,128)(2,1)}, u32[]{:S(2)}) copy-start(bf16[64,256]{1,0:T(8,128)(2,1)} %b_ref.1) | copy-start | bytes 98308
  7.2 38.7 %copy-start.3 = (f32[256]{0:T(256)S(1)}, f32[256]{0:T(256)}, u32[]{:S(2)}) copy-start(f32[256]{0:T(256)} %param.11) | copy-start | bytes 3076
  7.2 48.7 %all-gather.3.cloned.1.call-start = ((), (), s32[]{:S(2)}) async-start(), calls=%async_computation.4 | async-start | bytes 2621440 | tf_op jit(solution)/shard_map/all_gather | solution.py:250
  35.5 26.0 %all-to-all-start.1 = ((bf16[8,32,1024]{2,1,0:T(8,128)(2,1)}), bf16[8,32,1024]{2,1,0:T(8,128)(2,1)S(1)}, u32[]{:S(2)}, u32[]{:S(2)}) async-start(bf16[8,32,1024]{2,1,0:T(8,128)(2,1)} %get-tuple-element.31), calls=%async_computation.1 | async-start | bytes 1048576 | tf_op jit(solution)/shard_map/all_to_all | solution.py:271
  46.7 11.0 %collective-permute-start = (bf16[320,256]{1,0:T(8,128)(2,1)}, bf16[320,256]{1,0:T(8,128)(2,1)S(1)}, u32[]{:S(2)}, u32[]{:S(2)}) collective-permute-start(bf16[320,256]{1,0:T(8,128)(2,1)} %get-tuple-element.27), channel_id=1, source_target_pairs={{0,16},{16,32},{32,48},{48,0},{1,17},{17,33},{33,49},{49,1},{2,18}... | collective-permute-start | bytes 491528 | tf_op jit(solution)/shard_map/ppermute | solution.py:230
  49.1 9.5 %collective-permute-start.1 = (bf16[320,256]{1,0:T(8,128)(2,1)}, bf16[320,256]{1,0:T(8,128)(2,1)S(1)}, u32[]{:S(2)}, u32[]{:S(2)}) collective-permute-start(bf16[320,256]{1,0:T(8,128)(2,1)} %get-tuple-element.28), channel_id=1, source_target_pairs={{0,48},{16,0},{32,16},{48,32},{1,49},{17,1},{33,17},{49,33},{2,50}... | collective-permute-start | bytes 491528 | tf_op jit(solution)/shard_map/ppermute | solution.py:230
  52.5 8.9 %collective-permute-start.2 = (bf16[320,256]{1,0:T(8,128)(2,1)}, bf16[320,256]{1,0:T(8,128)(2,1)S(1)}, u32[]{:S(2)}, u32[]{:S(2)}) collective-permute-start(bf16[320,256]{1,0:T(8,128)(2,1)} %get-tuple-element.29), channel_id=1, source_target_pairs={{0,32},{16,48},{32,0},{48,16},{1,33},{17,49},{33,1},{49,17},{2,34}... | collective-permute-start | bytes 491528 | tf_op jit(solution)/shard_map/ppermute | solution.py:230
  55.9 1.6 %copy-start = (bf16[4096,256]{1,0:T(8,128)(2,1)S(1)}, bf16[4096,256]{1,0:T(8,128)(2,1)}, u32[]{:S(2)}) copy-start(bf16[4096,256]{1,0:T(8,128)(2,1)} %all-gather.3.cloned.1.call-done) | copy-start | bytes 6291460
  57.5 4.0 %copy-start.1 = (bf16[1024,64]{0,1:T(8,128)(2,1)S(1)}, bf16[1024,64]{0,1:T(8,128)(2,1)}, u32[]{:S(2)}) copy-start(bf16[1024,64]{0,1:T(8,128)(2,1)} %param.9) | copy-start | bytes 393220
  65.3 0.6 copy-start.4
  65.9 23.1 %all-to-all-start.2 = ((bf16[8,32,1280]{2,1,0:T(8,128)(2,1)}), bf16[8,32,1280]{2,1,0:T(8,128)(2,1)S(1)}, u32[]{:S(2)}, u32[]{:S(2)}) async-start(bf16[8,32,1280]{2,1,0:T(8,128)(2,1)} %bitcast.5), calls=%async_computation.2 | async-start | bytes 1310720 | tf_op jit(solution)/shard_map/all_to_all | solution.py:296
  73.1 9.2 %collective-permute-start.5 = (bf16[80,256]{1,0:T(8,128)(2,1)}, bf16[80,256]{1,0:T(8,128)(2,1)S(1)}, u32[]{:S(2)}, u32[]{:S(2)}) collective-permute-start(bf16[80,256]{1,0:T(8,128)(2,1)} %copy-done.4), channel_id=1, source_target_pairs={{0,48},{16,0},{32,16},{48,32},{1,49},{17,1},{33,17},{49,33},{2,50}... | collective-permute-start | bytes 122888 | tf_op jit(solution)/shard_map/ppermute | solution.py:230
  75.8 6.5 %collective-permute-start.6 = (bf16[80,256]{1,0:T(8,128)(2,1)S(1)}, bf16[80,256]{1,0:T(8,128)(2,1)S(1)}, u32[]{:S(2)}, u32[]{:S(2)}) collective-permute-start(bf16[80,256]{1,0:T(8,128)(2,1)S(1)} %get-tuple-element.40), channel_id=1, source_target_pairs={{0,16},{16,32},{32,48},{48,0},{1,17},{17,33},{33,49},{49,1},{2,18}... | collective-permute-start | bytes 122888 | tf_op jit(solution)/shard_map/ppermute | solution.py:230
  80.2 7.4 %collective-permute-start.7 = (bf16[80,256]{1,0:T(8,128)(2,1)S(1)}, bf16[80,256]{1,0:T(8,128)(2,1)S(1)}, u32[]{:S(2)}, u32[]{:S(2)}) collective-permute-start(bf16[80,256]{1,0:T(8,128)(2,1)S(1)} %get-tuple-element.41), channel_id=1, source_target_pairs={{0,32},{16,48},{32,0},{48,16},{1,33},{17,49},{33,1},{49,17},{2,34}... | collective-permute-start | bytes 122888 | tf_op jit(solution)/shard_map/ppermute | solution.py:230
  89.7 19.3 %all-to-all-start.3 = ((bf16[8,16,256]{2,1,0:T(8,128)(2,1)}), bf16[8,16,256]{2,1,0:T(8,128)(2,1)S(1)}, u32[]{:S(2)}, u32[]{:S(2)}) async-start(bf16[8,16,256]{2,1,0:T(8,128)(2,1)} %shard_map.99), calls=%async_computation.3 | async-start | bytes 131072 | tf_op jit(solution)/shard_map/all_to_all | solution.py:307
  96.7 5.5 %collective-permute-start.3 = (bf16[16,256]{1,0:T(8,128)(2,1)S(1)}, bf16[16,256]{1,0:T(8,128)(2,1)S(1)}, u32[]{:S(2)}, u32[]{:S(2)}) collective-permute-start(bf16[16,256]{1,0:T(8,128)(2,1)S(1)} %get-tuple-element.35), channel_id=1, source_target_pairs={{0,16},{16,0},{32,48},{48,32},{1,17},{17,1},{33,49},{49,33},{2,18}... | collective-permute-start | bytes 24584 | tf_op jit(solution)/shard_map/ppermute | solution.py:234
  102.2 6.7 %collective-permute-start.4 = (bf16[16,256]{1,0:T(8,128)(2,1)S(1)}, bf16[16,256]{1,0:T(8,128)(2,1)S(1)}, u32[]{:S(2)}, u32[]{:S(2)}) collective-permute-start(bf16[16,256]{1,0:T(8,128)(2,1)S(1)} %get-tuple-element.37), channel_id=1, source_target_pairs={{0,48},{16,32},{32,16},{48,0},{1,49},{17,33},{33,17},{49,1},{2,50}... | collective-permute-start | bytes 24584 | tf_op jit(solution)/shard_map/ppermute | solution.py:234
Sparse Core Ops, SparseCore 0:
  10.1 39.1 all-gather.2
